TPU v7x, 32 devices: a whole 2x2x4 slice. The times are simulated.
32 devices in a mesh: rad: 4 (over y, x), lon: 8 (over z, core).
Axes of the slice: x: 2, y: 2, z: 4, core: 2. Of those that a mesh axis runs over, the one named last changes fastest.
Arguments:
- state: float32 [8, 256, 128, 256], P(None, 'rad', 'lon'), may hold values from -6 to 6
- flux_matrices: float32 [2, 8, 8], replicated, may hold values from -2 to 2
- wave_speed: float32 [2], replicated, may hold values from 0.5 to 2
- flux_volume: float32 [256, 128, 256], P('rad', 'lon'), may hold values from 0.02 to 0.2
- block_tile: int32 [8, 256, 1], P('lon', 'rad'), may hold values from 0 to 31; in each aligned block of 64 rows (0 to 63, 64 to 127, ..., all dimensions but the last counted through in order) at most 2 rows name the same one
- tile_of_device: int32 [32], replicated, may hold values from 0 to 31, each once
- phase_density: float32 [32, 200, 128], P(('rad', 'lon')), may hold values from -6 to 6
- injection: float32 [2, 200], replicated, may hold values from -3 to 3
- drift_courant: float32 [200], replicated, may hold values from 0.05 to 0.9
- energy_weight: float32 [200], replicated, may hold values from 0.01 to 0.1
Outputs:
- coupled_state: float32 [8, 256, 128, 256], P(None, 'rad', 'lon')
- drifted_density: float32 [32, 200, 128], P(('rad', 'lon'))
Inputs may be any that keep to these rules, and one draw needn't show every extreme that they name: `block_tile`: in each longitude sector and each aligned run of 64 radial rows, no tile is reached by more than 2 blocks. `tile_of_device`: every tile has exactly one owner.
All inputs are finite; a program needn't handle non-finite values.
Results may differ from a plain program's by a relative error of at most 0.000067.
Values sent between devices are 32-bit elements; how exact they have to be, the bound alone decides.
No kernel may reach another device: no remote copies, remote signals or barrier semaphores. Data moves between devices by JAX's collectives and lax.ppermute only.
A program may use at most 192 MiB of HBM per device.

v0:
```python
import functools

import jax
import jax.numpy as jnp
import numpy as np
from jax import lax
from jax.experimental import pallas as pl
from jax.experimental.pallas import tpu as pltpu
from jax.sharding import PartitionSpec as P

ZSEG = 8
DRIFT = 3
REACH = 3

courant_step = 0.4
nudge_rate = 0.5
inner_step = 0.5

SUM_TAPS = {k: v / 60.0 for k, v in zip(range(-3, 4), (-2.0, 18.0, -90.0, 0.0, 90.0, -18.0, 2.0))}
GAP_TAPS = {k: v / 60.0 for k, v in zip(range(-3, 4), (2.0, -12.0, 30.0, -40.0, 30.0, -12.0, 2.0))}

PACKED = (0, 7, 1, 2, 3, 4, 5, 6)

f32 = jnp.float32
bf16 = jnp.bfloat16


def cost(flops, bytes_accessed):
    return pl.CostEstimate(flops=int(flops), bytes_accessed=int(bytes_accessed), transcendentals=0)


def parts_of(x, count):
    parts = []
    for _ in range(count):
        part = x.astype(bf16)
        parts.append(part)
        x = x - part.astype(f32)
    return parts


def dot(a, b):
    return jnp.dot(a, b, preferred_element_type=f32)


def exact_dot(x, ones):
    return sum(dot(part, ones) for part in parts_of(x, 3))


def lon_tables(rows, cols):
    fields = 1 + max(f for f, _ in cols)
    pick_row = np.array([[float(f == a) for a in range(fields)] for f, _ in rows], np.float32)
    pick_col = np.array([[float(f == b) for f, _ in cols] for b in range(fields)], np.float32)
    summed = np.array([[0.0 if s is None else SUM_TAPS.get(s - t, 0.0) for _, s in cols] for _, t in rows], np.float32)
    gapped = np.array(
        [[0.0 if s is None or f != g else GAP_TAPS.get(s - t, 0.0) for g, s in cols] for f, t in rows], np.float32
    )
    return pick_row, pick_col, summed, gapped


def lon_weights(matrix, wave_rate, pick_row, pick_col, summed, gapped):
    half = 0.5 * courant_step
    spread = f32_dot(f32_dot(pick_row, matrix), pick_col)
    return (half * wave_rate) * gapped - half * spread * summed


def f32_dot(a, b):
    return jnp.dot(a, b, precision=lax.Precision.HIGHEST, preferred_element_type=f32)


def whole(array):
    zeros = (0,) * array.ndim
    return pl.BlockSpec(array.shape, lambda *_: zeros)


SMEM = pl.BlockSpec(memory_space=pltpu.SMEM)
VMEM = pl.BlockSpec(memory_space=pltpu.VMEM)
HBM = pl.BlockSpec(memory_space=pltpu.HBM)
LARGE = pltpu.CompilerParams(vmem_limit_bytes=16 * 2**20)
SMALL = pltpu.CompilerParams(vmem_limit_bytes=4 * 2**20)
CHUNK = 8
AHEAD = 3


def in_vmem(*shape):
    return pltpu.VMEM(shape, f32)


def pinned(x):
    return pltpu.with_memory_space_constraint(x, pltpu.VMEM)


def lon_edge_kernel(lon_ref, rad_ref, place_ref, state_hbm, speed_hbm, matrix_hbm, table_hbm, cells, ids_ref, same, *refs):
    *crosses, speed_ref, matrix_ref, table_ref, weights, sem, few_sem = refs
    fields, rows, cols, depth = state_hbm.shape
    chunks = rows // CHUNK
    size = same.shape[1]

    def load(c):
        return pltpu.make_async_copy(
            state_hbm.at[:, pl.ds(c * CHUNK, CHUNK)], cells.at[:, pl.ds(REACH + c * CHUNK, CHUNK)], sem.at[c]
        )

    ids_ref[0] = lon_ref[0]
    ids_ref[1] = rad_ref[0]
    ids_ref[2] = place_ref[0]
    few = [
        pltpu.make_async_copy(source, target, few_sem.at[i])
        for i, (source, target) in enumerate(
            ((speed_hbm, speed_ref), (matrix_hbm, matrix_ref), (table_hbm, table_ref))
        )
    ]
    for copy in few:
        copy.start()
    for c in range(AHEAD):
        load(c).start()
    for edge in (0, REACH + rows):
        cells[:, edge : edge + REACH] = jnp.zeros((fields, REACH, cols, depth), f32)
    for copy in few:
        copy.wait()
    wide = 8 * fields
    w = lon_weights(
        matrix_ref[1], speed_ref[1], table_ref[0, :, :fields], table_ref[1, :fields, :wide], table_ref[2, :, :wide],
        table_ref[3, :, :wide],
    )
    swap = lon_ref[0] % 2 == 1
    w = jnp.concatenate([jnp.where(swap, w[size:], w[:size]), jnp.where(swap, w[:size], w[size:])], axis=0)
    high, low = parts_of(w, 2)
    weights[...] = jnp.concatenate([high, high, low], axis=1)
    low_half = lax.broadcasted_iota(jnp.int32, (fields, 8, depth), 1) < 4

    def step(c, carry):
        load(c).wait()

        @pl.when(c + AHEAD < chunks)
        def _():
            load(c + AHEAD).start()

        for j in range(CHUNK):
            r = c * CHUNK + j
            edge = jnp.where(low_half, cells[:, REACH + r, :8, :], cells[:, REACH + r, 8:, :])
            high, low = parts_of(edge.reshape(-1, depth), 2)
            sums = dot(weights[...], jnp.concatenate([high, low, high], axis=0))
            same[r] = sums[:size]
            for i, out in enumerate(crosses):
                out[r] = sums[size + 8 * i : size + 8 * i + 8]
        return carry

    lax.fori_loop(0, chunks, step, 0)


def lon_edges(state, matrices, speed, lon, rad, place):
    fields, rows, cols, depth = state.shape
    sources = [(f, l if l < 4 else cols - 8 + l) for f in range(fields) for l in range(8)]
    sources = [(f, l if l < REACH or l >= cols - REACH else None) for f, l in sources]
    to_right = [(f, cols + t) for f in PACKED for t in range(REACH)]
    to_left = [(f, t - REACH) for f in PACKED for t in range(REACH)]
    size = fields * REACH
    tables = np.zeros((4, 2 * size, 128), np.float32)
    for i, table in enumerate(lon_tables(to_right + to_left, sources)):
        tables[i, : table.shape[0], : table.shape[1]] = table
    tiles = size // 8
    return pl.pallas_call(
        lon_edge_kernel,
        in_specs=[SMEM] * 3 + [HBM] * 4,
        out_specs=[VMEM, SMEM] + [VMEM] * (1 + tiles),
        out_shape=[
            in_vmem(fields, rows + 2 * REACH, cols, depth),
            jax.ShapeDtypeStruct((3,), jnp.int32),
            in_vmem(rows, size, depth),
        ]
        + [in_vmem(rows, 8, depth)] * tiles,
        scratch_shapes=[
            pltpu.SMEM(speed.shape, f32),
            pltpu.VMEM(matrices.shape, f32),
            pltpu.VMEM(tables.shape, f32),
            pltpu.VMEM((2 * size, 3 * len(sources)), bf16),
            pltpu.SemaphoreType.DMA((rows // CHUNK,)),
            pltpu.SemaphoreType.DMA((3,)),
        ],
        compiler_params=LARGE,
        cost_estimate=cost(1e3, 1e3),
        name="lon_edges",
    )(lon, rad, place, *[pltpu.with_memory_space_constraint(x, pltpu.HBM) for x in (state, speed, matrices, jnp.asarray(tables))])


def turn_weights(matrix, pick, same):
    return (-0.5 * courant_step) * same * f32_dot(f32_dot(pick, matrix), pick.T)


def turn_tables(fields, cols):
    every = [(f, l) for f in range(fields) for l in range(cols)]
    pick = np.array([[float(f == a) for a in range(fields)] for f, _ in every], np.float32)
    same = np.array([[float(l == m) for _, m in every] for _, l in every], np.float32)
    return pick, same


def rad_edge_kernel(ids_ref, speed_ref, cells_ref, matrix_ref, pick_ref, same_ref, near_a, near_b, far_a, far_b):
    fields, padded, cols, depth = cells_ref.shape
    rate = (0.5 * courant_step) * speed_ref[0]
    even = ids_ref[1] % 2 == 0
    high, low = parts_of(turn_weights(matrix_ref[0], pick_ref[...], same_ref[...]), 2)
    w = jnp.concatenate([high, high, low], axis=1)

    def turned(cells):
        high, low = parts_of(cells.reshape(-1, depth), 2)
        return dot(w, jnp.concatenate([high, low, high], axis=0)).reshape(fields, cols, depth)

    first = [cells_ref[:, REACH + j] for j in range(REACH)]
    last = [cells_ref[:, padded - 2 * REACH + j] for j in range(REACH)]
    first_turned = [turned(cells) for cells in first]
    last_turned = [turned(cells) for cells in last]
    for t in range(REACH):
        up = sum(
            SUM_TAPS[j - REACH - t] * last_turned[j] + (rate * GAP_TAPS[j - REACH - t]) * last[j]
            for j in range(t, REACH)
        )
        down = sum(
            SUM_TAPS[j + REACH - t] * first_turned[j] + (rate * GAP_TAPS[j + REACH - t]) * first[j]
            for j in range(t + 1)
        )
        near, far = jnp.where(even, up, down), jnp.where(even, down, up)
        for total, a, b in ((near, near_a, near_b), (far, far_a, far_b)):
            a[0, t] = total[0]
            a[1, t] = total[7]
            b[:, t] = total[1:7]


def rad_edges(ids, cells, matrices, speed):
    fields, _, cols, depth = cells.shape
    tables = turn_tables(fields, cols)
    few, many = in_vmem(2, REACH, cols, depth), in_vmem(fields - 2, REACH, cols, depth)
    return pl.pallas_call(
        rad_edge_kernel,
        in_specs=[SMEM] * 2 + [VMEM] * (2 + len(tables)),
        out_specs=[VMEM] * 4,
        out_shape=[few, many, few, many],
        compiler_params=LARGE,
        cost_estimate=cost(1e3, 1e3),
        name="rad_edges",
    )(ids, speed, pinned(cells), matrices, *tables)


def add_radial(speed_ref, cells, turned, total, fields, first):
    cols, depth = total.shape[2:]
    rate = (0.5 * courant_step) * speed_ref[0]
    for f in fields:
        for half in range(cols // 8):
            for lane in range(depth // 128):
                lanes = pl.ds(128 * lane, 128)
                u = [cells[f, first + j, pl.ds(8 * half, 8), lanes] for j in range(CHUNK + 2 * REACH)]
                v = [turned[first + j, pl.ds(f * cols + 8 * half, 8), lanes] for j in range(CHUNK + 2 * REACH)]
                for j in range(CHUNK):
                    at = j + REACH
                    value = total[f, first + j, pl.ds(8 * half, 8), lanes] + (rate * GAP_TAPS[0]) * u[at]
                    for k in range(1, REACH + 1):
                        value = value + SUM_TAPS[k] * (v[at + k] - v[at - k])
                        value = value + (rate * GAP_TAPS[k]) * (u[at + k] + u[at - k])
                    total[f, first + j, pl.ds(8 * half, 8), lanes] = value


def local_kernel(mine, speed_ref, cells, matrix_ref, pick_ref, same_ref, sum_ref, gap_ref, total, turned, w_ref):
    _, rows, cols, depth = total.shape
    chunks = rows // CHUNK
    pick = pick_ref[...]
    own = lon_weights(matrix_ref[1], speed_ref[1], pick, pick.T, sum_ref[...], gap_ref[...])
    turn = turn_weights(matrix_ref[0], pick, same_ref[...])
    own, turn = [jnp.concatenate([w[f * cols : (f + 1) * cols] for f in mine], axis=0) for w in (own, turn)]
    high, low = parts_of(jnp.concatenate([own, turn], axis=0), 2)
    w_ref[...] = jnp.concatenate([high, high, low], axis=1)
    size = len(mine) * cols
    for edge in (0, REACH + rows):
        turned[edge : edge + REACH] = jnp.zeros((REACH, size, depth), f32)

    def rows_of(c, carry):
        for j in range(CHUNK):
            r = c * CHUNK + j
            high, low = parts_of(cells[:, REACH + r].reshape(-1, depth), 2)
            both = dot(w_ref[...], jnp.concatenate([high, low, high], axis=0))
            for i, f in enumerate(mine):
                total[i, r] = cells[f, REACH + r] + both[i * cols : (i + 1) * cols]
            turned[REACH + r] = both[size:]
        return carry

    rate = (0.5 * courant_step) * speed_ref[0]

    def radial(c, carry):
        first = c * CHUNK
        for i, f in enumerate(mine):
            for half in range(cols // 8):
                for lane in range(depth // 128):
                    lanes, subs = pl.ds(128 * lane, 128), pl.ds(8 * half, 8)
                    u = [cells[f, first + j, subs, lanes] for j in range(CHUNK + 2 * REACH)]
                    v = [
                        turned[first + j, pl.ds(i * cols + 8 * half, 8), lanes] for j in range(CHUNK + 2 * REACH)
                    ]
                    for j in range(CHUNK):
                        at = j + REACH
                        value = total[i, first + j, subs, lanes] + (rate * GAP_TAPS[0]) * u[at]
                        for k in range(1, REACH + 1):
                            value = value + SUM_TAPS[k] * (v[at + k] - v[at - k])
                            value = value + (rate * GAP_TAPS[k]) * (u[at + k] + u[at - k])
                        total[i, first + j, subs, lanes] = value
        return carry

    lax.fori_loop(0, chunks, rows_of, 0)
    lax.fori_loop(0, chunks, radial, 0)


def local_update(mine, cells, matrices, speed):
    fields, padded, cols, depth = cells.shape
    rows = padded - 2 * REACH
    every = [(f, l) for f in range(fields) for l in range(cols)]
    _, _, summed, gapped = lon_tables(every, every)
    size = len(mine) * cols
    return pl.pallas_call(
        functools.partial(local_kernel, mine),
        in_specs=[SMEM] + [VMEM] * 6,
        out_specs=VMEM,
        out_shape=in_vmem(len(mine), rows, cols, depth),
        scratch_shapes=[
            pltpu.VMEM((padded, size, depth), f32),
            pltpu.VMEM((2 * size, 3 * fields * cols), bf16),
        ],
        compiler_params=LARGE,
        cost_estimate=cost(1e3, 1e3),
        name="local_update",
    )(speed, pinned(cells), matrices, *turn_tables(fields, cols), summed, gapped)


def placed(tiles, field, from_left):
    start = REACH * PACKED.index(field)
    tile, offset = start // 8, start % 8
    cells = tiles[tile]
    sub = lax.broadcasted_iota(jnp.int32, cells.shape, 1)
    if offset + REACH > 8:
        cells = jnp.where(sub >= offset, cells, tiles[tile + 1])
    goal = 0 if from_left else 8 - REACH
    shift = (goal - offset) % 8
    if shift:
        cells = pltpu.roll(cells, shift, 1)
    keep = sub < REACH if from_left else sub >= 8 - REACH
    return jnp.where(keep, cells, 0.0)


def by_side(lon, same, crosses):
    even = lon % 2 == 0
    lefts, rights = {}, {}
    for t, cross in enumerate(crosses):
        near = same[:, 8 * t : 8 * t + 8]
        lefts[t] = jnp.where(even, cross, near)
        rights[t] = jnp.where(even, near, cross)
    return lefts, rights


def with_sides(cells, lefts, rights, field):
    cols = cells.shape[1]
    return jnp.concatenate(
        [cells[:, :8] + placed(lefts, field, True), cells[:, cols - 8 :] + placed(rights, field, False)], axis=1
    )


def with_ends(cells, step, steps, rad, near, far):
    rows = cells.shape[0]
    even = rad % 2 == 0
    below, above = jnp.where(even, far, near), jnp.where(even, near, far)
    at_low = (step == 0).astype(f32)
    at_top = (step == steps - 1).astype(f32)
    return jnp.concatenate(
        [cells[:REACH] + at_low * below, cells[REACH : rows - REACH], cells[rows - REACH :] + at_top * above], axis=0
    )


def tile_sum_kernel(
    ids_ref, part_ref, vol_ref, same_ref, cross_ref, near_ref, far_ref, rest_ref, hit_ref, seg_ref, spot_ref,
    out_ref, lines_ref,
):
    all_rows, cols, depth = vol_ref.shape
    tiles, points = out_ref.shape[0], out_ref.shape[1] // 3
    rows = 16
    steps = all_rows // rows

    def add(step, carry):
        here = pl.ds(pl.multiple_of(step * rows, rows), rows)
        lefts, rights = by_side(ids_ref[0], same_ref[here, :8], [cross_ref[here]])
        vol = vol_ref[here]
        for c, field in enumerate((0, 7)):
            cells = with_sides(part_ref[c, here], lefts, rights, field)
            cells = with_ends(cells, step, steps, ids_ref[1], near_ref[c], far_ref[c])
            lines = exact_dot((cells * vol).reshape(rows * cols, depth), seg_ref[...])
            lines_ref[c, here] = jnp.sum(lines.reshape(rows, cols, -1) * spot_ref[...][None], axis=1)
        return carry

    lax.fori_loop(0, steps, add, 0)
    for c in range(2):
        sums = sum(dot(hit_ref[...], part) for part in parts_of(lines_ref[c], 3))
        out_ref[:, c * points : (c + 1) * points] = sums
    mine = lax.broadcasted_iota(jnp.int32, (tiles, points), 0) == ids_ref[2]
    out_ref[:, 2 * points :] = jnp.where(mine, rest_ref[8:9], 0.0)


def tile_sums(ids, part, vol, same, cross, near, far, rest, hits, seg, spot):
    _, rows, _, _ = part.shape
    points = seg.shape[1]
    tiles = hits.shape[0]
    return pl.pallas_call(
        tile_sum_kernel,
        in_specs=[SMEM] + [VMEM] * 10,
        out_specs=VMEM,
        out_shape=in_vmem(tiles, 3 * points),
        scratch_shapes=[pltpu.VMEM((2, rows, points), f32)],
        compiler_params=LARGE,
        cost_estimate=cost(1e3, 1e3),
        name="tile_sums",
    )(ids, *[pinned(x) for x in (part, vol, same, cross, near, far, rest)], hits, seg, spot)


def drifted(density, courant):
    for _ in range(DRIFT):
        density = density - courant * (density - pltpu.roll(density, 1, 1))
    return density


def columns_of(packed_ref, channels):
    turned = jnp.transpose(packed_ref[...])
    return [turned[:channels, i : i + 1] for i in range(4)]


def rest_kernel(density_ref, packed_ref, out_ref):
    _, channels, points = density_ref.shape
    courant, weight, first, second = columns_of(packed_ref, channels)
    rows = []
    for given in (first, second):
        for k, choices in enumerate((1.0, 3.0, 3.0, 1.0)):
            gain = (inner_step * choices) * weight * given
            for _ in range(k):
                gain = gain * courant
            for _ in range(DRIFT - k):
                gain = gain * (1.0 - courant)
            rows.append(jnp.broadcast_to(jnp.sum(gain, axis=0, keepdims=True), (1, points)))
    rest = jnp.sum(weight * drifted(density_ref[0], courant), axis=0, keepdims=True)
    out_ref[...] = jnp.concatenate(rows + [rest] * 8, axis=0)


def rest_of(density, packed):
    points = density.shape[2]
    return pl.pallas_call(
        rest_kernel,
        out_shape=jax.ShapeDtypeStruct((16, points), f32),
        compiler_params=SMALL,
        cost_estimate=cost(1e3, 1e3),
        name="rest_pressure",
    )(density, packed)


def drift_kernel(ids_ref, density_ref, packed_ref, sums_ref, out_ref):
    _, channels, points = density_ref.shape
    courant, _, first, second = columns_of(packed_ref, channels)
    source = sums_ref[pl.ds(ids_ref[2], 1), :]
    density = density_ref[0] + inner_step * (first * source[:, :points] + second * source[:, points : 2 * points])
    out_ref[0] = drifted(density, courant)


def drift(ids, density, packed, sums):
    return pl.pallas_call(
        drift_kernel,
        in_specs=[SMEM] + [VMEM] * 3,
        out_shape=jax.ShapeDtypeStruct(density.shape, f32),
        compiler_params=SMALL,
        cost_estimate=cost(1e3, 1e3),
        name="drift",
    )(ids, density, packed, sums)


def pressures_of(sums, rest_ref):
    points = sums.shape[1] // 3
    pressure = sums[:, 2 * points :]
    for c in range(2):
        source = sums[:, c * points : (c + 1) * points]
        for k in range(DRIFT + 1):
            shifted = pltpu.roll(source, k, 1) if k else source
            pressure = pressure + rest_ref[(DRIFT + 1) * c + k : (DRIFT + 1) * c + k + 1] * shifted
    return pressure


def finish_kernel(
    ids_ref, ends_ref, part_ref, near_a, far_a, near_b, far_b, same_ref, cross_0, cross_1, cross_2,
    hit_ref, sums_ref, rest_ref, spot_ref, seg_ref, out_hbm, done, back_ref, sem,
):
    fields, all_rows, cols, depth = done.shape
    rows = CHUNK
    steps = all_rows // rows

    def store(field):
        return pltpu.make_async_copy(done.at[field], out_hbm.at[field], sem.at[field])

    def run(field):
        def step(i, carry):
            here = pl.ds(pl.multiple_of(i * rows, rows), rows)
            first = REACH * PACKED.index(field) // 8
            last = (REACH * PACKED.index(field) + REACH - 1) // 8
            lefts, rights = {}, {}
            for t in range(first, last + 1):
                one = by_side(ids_ref[0], same_ref[here, 8 * t : 8 * t + 8], [(cross_0, cross_1, cross_2)[t][here]])
                lefts[t], rights[t] = one[0][0], one[1][0]
            if field in (0, fields - 1):
                near, far = near_a[field // (fields - 1)], far_a[field // (fields - 1)]
                own = ends_ref[field // (fields - 1), here]
            else:
                near, far = near_b[field - 1], far_b[field - 1]
                own = part_ref[field - 1, here]
            cells = with_sides(own, lefts, rights, field)
            cells = with_ends(cells, i, steps, ids_ref[1], near, far)
            if field == fields - 1:
                spread = (back_ref[here][:, None, :] * spot_ref[...][None]).reshape(rows * cols, -1)
                returned = exact_dot(spread, seg_ref[...]).reshape(rows, cols, depth)
                cells = cells + nudge_rate * (returned - cells)
            done[field, here] = cells
            return carry

        lax.fori_loop(0, steps, step, 0)
        store(field).start()

    for field in range(fields - 3):
        run(field)
    back_ref[...] = sum(dot(hit_ref[...], p) for p in parts_of(pressures_of(sums_ref[...], rest_ref), 3))
    run(fields - 1)
    run(fields - 3)
    run(fields - 2)
    for field in range(fields):
        store(field).wait()


def finish(ids, ends, part, rad_a, rad_b, same, crosses, hits, sums, rest, spot, seg):
    _, rows, cols, depth = part.shape
    shape = (ends.shape[0] + part.shape[0], rows, cols, depth)
    pins = [pinned(x) for x in (ends, part, *rad_a, *rad_b, same, *crosses)]
    return pl.pallas_call(
        finish_kernel,
        in_specs=[SMEM] + [VMEM] * (len(pins) + 5),
        out_specs=HBM,
        out_shape=jax.ShapeDtypeStruct(shape, f32),
        scratch_shapes=[
            pltpu.VMEM(shape, f32),
            pltpu.VMEM((rows, spot.shape[1]), f32),
            pltpu.SemaphoreType.DMA((shape[0],)),
        ],
        compiler_params=LARGE,
        cost_estimate=cost(1e3, 1e3),
        name="finish",
    )(ids, *pins, hits, sums, rest, spot, seg)


def swap(x, axis, bit):
    return lax.ppermute(x, axis, [(i, i ^ bit) for i in range(lax.axis_size(axis))])


def per_device(
    state,
    flux_matrices,
    wave_speed,
    flux_volume,
    block_tile,
    tile_of_device,
    phase_density,
    injection,
    drift_courant,
    energy_weight,
):
    fields, rows, cols, depth = state.shape
    n_rad, n_lon = lax.axis_size("rad"), lax.axis_size("lon")
    points = cols * ZSEG
    lon, rad, place = [lax.axis_index(axes).astype(jnp.int32).reshape(1) for axes in ("lon", "rad", ("rad", "lon"))]

    across = [(i, (i + 1 if i % 2 else i - 1) % n_lon) for i in range(n_lon)]
    beyond = [(i, j) for i in range(n_rad) for j in [i + 1 if i % 2 else i - 1] if 0 <= j < n_rad]
    cells, ids, same, *crosses = lon_edges(state, flux_matrices, wave_speed, lon, rad, place)
    cross_0 = lax.ppermute(crosses[0], "lon", across)
    same = swap(same, "lon", 1)
    cross_1 = lax.ppermute(crosses[1], "lon", across)

    near_a, near_b, far_a, far_b = rad_edges(ids, cells, flux_matrices, wave_speed)
    rad_a = swap(near_a, "rad", 1), lax.ppermute(far_a, "rad", beyond)

    packed = jnp.concatenate([drift_courant[None], energy_weight[None], injection], axis=0)
    packed = jnp.pad(packed, ((0, 4), (0, -packed.shape[1] % 128)))
    rest = rest_of(phase_density, packed)

    ends = local_update((0, fields - 1), cells, flux_matrices, wave_speed)

    targets = block_tile[0, :, 0]
    hits = (tile_of_device[:, None] == targets[None, :]).astype(bf16)
    hits_back = (targets[:, None] == tile_of_device[None, :]).astype(bf16)
    seg_cells = depth // ZSEG
    seg = np.array([[float(p % ZSEG == z // seg_cells) for p in range(points)] for z in range(depth)], np.float32)
    spot = np.array([[float(p // ZSEG == l) for p in range(points)] for l in range(cols)], np.float32)
    sums = tile_sums(
        ids, ends, flux_volume, same, cross_0, *rad_a, rest, hits, jnp.asarray(seg, bf16), jnp.asarray(spot)
    )
    def summed(sums, axis, steps):
        return sum([swap(sums, axis, step) for step in steps], sums)

    sums = summed(sums, "rad", range(1, n_rad))
    near_b, far_b, sums = lax.optimization_barrier((near_b, far_b, sums))
    rad_b = swap(near_b, "rad", 1), lax.ppermute(far_b, "rad", beyond)
    sums = summed(sums, "lon", [1])
    sums, cross_1 = lax.optimization_barrier((sums, cross_1))
    sums = summed(sums, "lon", range(2, n_lon, 2))
    last, sums = lax.optimization_barrier((crosses[2], sums))
    cross_2 = lax.ppermute(last, "lon", across)
    part = local_update(tuple(range(1, fields - 1)), cells, flux_matrices, wave_speed)
    density = drift(ids, phase_density, packed, sums)

    done = finish(
        ids, ends, part, rad_a, rad_b, same, (cross_0, cross_1, cross_2), hits_back, sums, rest, jnp.asarray(spot),
        jnp.asarray(seg.T, bf16),
    )
    return done, density


def solution(mesh):
    in_specs = (
        P(None, "rad", "lon", None),
        P(),
        P(),
        P("rad", "lon", None),
        P("lon", "rad", None),
        P(),
        P(("rad", "lon"), None, None),
        P(),
        P(),
        P(),
    )
    out_specs = (P(None, "rad", "lon", None), P(("rad", "lon"), None, None))
    return jax.shard_map(per_device, mesh=mesh, in_specs=in_specs, out_specs=out_specs, check_vma=False)
```

profile of v0, /device:TPU:4, one launch (start us, length us, event | category | flops | bytes accessed | tf_op | source)
XLA Modules:
  0.0 66.6 jit_solution(1737670111254363835)
XLA Ops:
  0.6 0.0 copy-start.1
  0.6 0.0 copy-start.2
  0.7 0.0 copy-start.10
  0.7 0.0 copy-start.6
  0.7 6.0 %lon_edges.1 = (f32[8,70,16,256]{3,2,1,0:T(8,128)S(1)}, s32[3]{0:T(128)S(1)}, f32[64,24,256]{2,1,0:T(8,128)S(1)}, f32[64,8,256]{2,1,0:T(8,128)S(1)}, f32[64,8,25...) custom-call(s32[1]{0:T(128)} %bitcast.lon_ref, s32[1]{0:T(128)} %bitcast.1.rad_ref, s32[1]{0:T(128)} %bitcast.2.place_ref, ...), custom_call_target="tpu_custom_call" | custom-call | flops 1000 | bytes 1000 | tf_op jit(solution)/shard_map/lon_edges/pallas_call | solution.py:162
  6.7 0.0 copy-start.11
  6.7 0.0 copy-start.12
  6.7 0.0 copy-start.4
  6.7 0.0 copy-start.5
  6.7 0.1 collective-permute-start.2
  6.8 3.7 %collective-permute-start.3 = (f32[64,8,256]{2,1,0:T(8,128)S(1)}, f32[64,8,256]{2,1,0:T(8,128)S(1)}, u32[]{:S(2)}, u32[]{:S(2)}) collective-permute-start(f32[64,8,256]{2,1,0:T(8,128)S(1)} %get-tuple-element.26), channel_id=1, source_target_pairs={{0,7},{1,2},{2,1},{3,4},{4,3},{5,6},{6,5},{7,0},{8,15},{9,10},{10,... | collective-permute-start | bytes 1572872 | tf_op jit(solution)/shard_map/ppermute | solution.py:577
  10.5 0.0 copy-done.1
  10.5 0.0 copy-done.2
  10.5 0.0 copy-done.10
  10.5 0.0 copy-done.6
  10.5 1.5 %rad_edges.1 = (f32[2,3,16,256]{3,2,1,0:T(8,128)S(1)}, f32[6,3,16,256]{3,2,1,0:T(8,128)S(1)}, f32[2,3,16,256]{3,2,1,0:T(8,128)S(1)}, f32[6,3,16,256]{3,2,1,0:T(8,128)S(1)}) custom-call(s32[3]{0:T(128)S(1)} %get-tuple-element.19.ids_ref, f32[2]{0:T(128)S(1)} %copy-done.10, f32[8,70,16,256]{3,2,1,0:T(8,128)S(1)} %get-tuple-element.20.cells.cells_ref, ...), custom_call_target="tpu_custom_call" | custom-call | flops 1000 | bytes 1000 | tf_op jit(solution)/shard_map/rad_edges/pallas_call | solution.py:232
  12.0 0.0 copy-start.13
  12.0 0.0 copy-start.14
  12.1 0.0 copy-start.15
  12.1 0.0 copy-start.3
  12.1 0.0 copy-start
  12.1 0.0 copy-start.8
  12.1 0.0 copy-start.9
  12.1 1.6 %collective-permute-start = (f32[2,3,16,256]{3,2,1,0:T(8,128)S(1)}, f32[2,3,16,256]{3,2,1,0:T(8,128)S(1)}, u32[]{:S(2)}, u32[]{:S(2)}) collective-permute-start(f32[2,3,16,256]{3,2,1,0:T(8,128)S(1)} %get-tuple-element.21), channel_id=1, source_target_pairs={{0,8},{8,0},{16,24},{24,16},{1,9},{9,1},{17,25},{25,17},{2,10},{10... | collective-permute-start | bytes 294920 | tf_op jit(solution)/shard_map/ppermute | solution.py:554
  13.7 2.4 %collective-permute-start.1 = (f32[2,3,16,256]{3,2,1,0:T(8,128)S(1)}, f32[2,3,16,256]{3,2,1,0:T(8,128)S(1)}, u32[]{:S(2)}, u32[]{:S(2)}) collective-permute-start(f32[2,3,16,256]{3,2,1,0:T(8,128)S(1)} %get-tuple-element.22), channel_id=1, source_target_pairs={{8,16},{16,8},{9,17},{17,9},{10,18},{18,10},{11,19},{19,11},{12,20... | collective-permute-start | bytes 294920 | tf_op jit(solution)/shard_map/ppermute | solution.py:582
  16.0 0.1 collective-permute-start.10
  16.1 0.0 copy-done.11
  16.1 0.0 copy-done.12
  16.1 0.1 compare_convert_fusion.1.hit_ref
  16.2 0.0 copy-done.4
  16.2 0.0 copy-done.5
  16.2 6.0 %local_update.2.part_ref.ends_ref = f32[2,64,16,256]{3,2,1,0:T(8,128)S(1)} custom-call(f32[2]{0:T(128)S(1)} %copy-done.10, f32[8,70,16,256]{3,2,1,0:T(8,128)S(1)} %get-tuple-element.20.cells.cells_ref, f32[2,8,8]{2,1,0:T(8,128)S(1)} %copy-done.6, f32[128,8]{1,0:T(8,128)S(1)} %copy-done.1, f32[128,128]{1,0:T(8,128)S(1)} %copy-done.2, ...), custom_call_target="tpu_custom_call" | custom-call | flops 1000 | bytes 1000 | tf_op jit(solution)/shard_map/local_update/pallas_call | solution.py:315
  22.3 0.7 rest_pressure.1.rest_ref
  23.0 0.0 collective-permute-done.near_ref.near_a
  23.0 0.0 collective-permute-done.1.far_ref.far_a
  23.0 0.0 collective-permute-done.3.cross_ref.cross_0
  23.0 0.0 collective-permute-done.2.same_ref
  23.0 2.4 %tile_sums.1 = f32[32,384]{1,0:T(8,128)S(1)} custom-call(s32[3]{0:T(128)S(1)} %get-tuple-element.19.ids_ref, f32[2,64,16,256]{3,2,1,0:T(8,128)S(1)} %local_update.2.part_ref.ends_ref, f32[64,16,256]{2,1,0:T(8,128)S(1)} %copy-done, f32[64,24,256]{2,1,0:T(8,128)S(1)} %collective-permute-done.2.same_ref, ...), custom_call_target="tpu_custom_call" | custom-call | flops 1000 | bytes 1000 | tf_op jit(solution)/shard_map/tile_sums/pallas_call | solution.py:405
  25.4 2.5 %collective-permute-start.6 = (f32[32,384]{1,0:T(8,128)S(1)}, f32[32,384]{1,0:T(8,128)S(1)}, u32[]{:S(2)}, u32[]{:S(2)}) collective-permute-start(f32[32,384]{1,0:T(8,128)S(1)} %tile_sums.1), channel_id=1, source_target_pairs={{0,24},{8,16},{16,8},{24,0},{1,25},{9,17},{17,9},{25,1},{2,26},{10... | collective-permute-start | bytes 147464 | tf_op jit(solution)/shard_map/ppermute | solution.py:554
  27.9 0.3 collective-permute-start.5
  28.2 0.7 %collective-permute-start.4 = (f32[32,384]{1,0:T(8,128)S(1)}, f32[32,384]{1,0:T(8,128)S(1)}, u32[]{:S(2)}, u32[]{:S(2)}) collective-permute-start(f32[32,384]{1,0:T(8,128)S(1)} %tile_sums.1), channel_id=1, source_target_pairs={{0,8},{8,0},{16,24},{24,16},{1,9},{9,1},{17,25},{25,17},{2,10},{10... | collective-permute-start | bytes 147464 | tf_op jit(solution)/shard_map/ppermute | solution.py:554
  28.9 2.0 %collective-permute-done.6 = f32[32,384]{1,0:T(8,128)S(1)} collective-permute-done((f32[32,384]{1,0:T(8,128)S(1)}, f32[32,384]{1,0:T(8,128)S(1)}, u32[]{:S(2)}, u32[]{:S(2)}) %collective-permute-start.6) | collective-permute-done | bytes 49184 | tf_op jit(solution)/shard_map/ppermute | solution.py:554
  30.9 1.0 %collective-permute-done.5 = f32[32,384]{1,0:T(8,128)S(1)} collective-permute-done((f32[32,384]{1,0:T(8,128)S(1)}, f32[32,384]{1,0:T(8,128)S(1)}, u32[]{:S(2)}, u32[]{:S(2)}) %collective-permute-start.5) | collective-permute-done | bytes 49184 | tf_op jit(solution)/shard_map/ppermute | solution.py:554
  32.0 0.3 collective-permute-done.4
  32.3 0.1 collective-permute-start.9
  32.4 1.2 %collective-permute-done.9 = f32[32,384]{1,0:T(8,128)S(1)} collective-permute-done((f32[32,384]{1,0:T(8,128)S(1)}, f32[32,384]{1,0:T(8,128)S(1)}, u32[]{:S(2)}, u32[]{:S(2)}) %collective-permute-start.9) | collective-permute-done | bytes 49184 | tf_op jit(solution)/shard_map/ppermute | solution.py:554
  33.6 0.0 collective-permute-done.10.cross_1
  33.6 2.4 %collective-permute-start.13 = (f32[32,384]{1,0:T(8,128)S(1)}, f32[32,384]{1,0:T(8,128)S(1)}, u32[]{:S(2)}, u32[]{:S(2)}) collective-permute-start(f32[32,384]{1,0:T(8,128)S(1)} %add.30), channel_id=1, source_target_pairs={{0,6},{1,7},{2,4},{3,5},{4,2},{5,3},{6,0},{7,1},{8,14},{9,15},{10,... | collective-permute-start | bytes 147464 | tf_op jit(solution)/shard_map/ppermute | solution.py:554
  36.0 0.0 collective-permute-start.12
  36.0 2.0 %collective-permute-start.11 = (f32[32,384]{1,0:T(8,128)S(1)}, f32[32,384]{1,0:T(8,128)S(1)}, u32[]{:S(2)}, u32[]{:S(2)}) collective-permute-start(f32[32,384]{1,0:T(8,128)S(1)} %add.30), channel_id=1, source_target_pairs={{0,2},{1,3},{2,0},{3,1},{4,6},{5,7},{6,4},{7,5},{8,10},{9,11},{10,... | collective-permute-start | bytes 147464 | tf_op jit(solution)/shard_map/ppermute | solution.py:554
  38.1 1.8 %collective-permute-done.13 = f32[32,384]{1,0:T(8,128)S(1)} collective-permute-done((f32[32,384]{1,0:T(8,128)S(1)}, f32[32,384]{1,0:T(8,128)S(1)}, u32[]{:S(2)}, u32[]{:S(2)}) %collective-permute-start.13) | collective-permute-done | bytes 49184 | tf_op jit(solution)/shard_map/ppermute | solution.py:554
  39.9 1.5 %collective-permute-done.12 = f32[32,384]{1,0:T(8,128)S(1)} collective-permute-done((f32[32,384]{1,0:T(8,128)S(1)}, f32[32,384]{1,0:T(8,128)S(1)}, u32[]{:S(2)}, u32[]{:S(2)}) %collective-permute-start.12) | collective-permute-done | bytes 49184 | tf_op jit(solution)/shard_map/ppermute | solution.py:554
  41.4 0.0 collective-permute-done.11
  41.4 0.0 copy-start.7
  41.4 2.2 %collective-permute-start.14 = (f32[64,8,256]{2,1,0:T(8,128)S(1)}, f32[64,8,256]{2,1,0:T(8,128)S(1)}, u32[]{:S(2)}, u32[]{:S(2)}) collective-permute-start(f32[64,8,256]{2,1,0:T(8,128)S(1)} %get-tuple-element.34), channel_id=1, source_target_pairs={{0,7},{1,2},{2,1},{3,4},{4,3},{5,6},{6,5},{7,0},{8,15},{9,10},{10,... | collective-permute-start | bytes 1572872 | tf_op jit(solution)/shard_map/ppermute | solution.py:609
  43.7 0.0 collective-permute-start.7
  43.7 4.8 %collective-permute-start.8 = (f32[6,3,16,256]{3,2,1,0:T(8,128)S(1)}, f32[6,3,16,256]{3,2,1,0:T(8,128)S(1)}, u32[]{:S(2)}, u32[]{:S(2)}) collective-permute-start(f32[6,3,16,256]{3,2,1,0:T(8,128)S(1)} %get-tuple-element.28), channel_id=1, source_target_pairs={{8,16},{16,8},{9,17},{17,9},{10,18},{18,10},{11,19},{19,11},{12,20... | collective-permute-start | bytes 884744 | tf_op jit(solution)/shard_map/ppermute | solution.py:604
  48.5 10.4 %local_update.3.part_ref = f32[6,64,16,256]{3,2,1,0:T(8,128)S(1)} custom-call(f32[2]{0:T(128)S(1)} %copy-done.10, f32[8,70,16,256]{3,2,1,0:T(8,128)S(1)} %get-tuple-element.20.cells.cells_ref, f32[2,8,8]{2,1,0:T(8,128)S(1)} %copy-done.6, f32[128,8]{1,0:T(8,128)S(1)} %copy-done.1, f32[128,128]{1,0:T(8,128)S(1)} %copy-done.2, f32[128,128]{1,0:T(8,128)S(1)} %copy-done.4, ...), custom_call_target="tpu_custom_call" | custom-call | flops 1000 | bytes 1000 | tf_op jit(solution)/shard_map/local_update/pallas_call | solution.py:315
  58.9 0.1 compare_convert_fusion.hit_ref
  59.0 1.7 %drift.1 = f32[1,200,128]{2,1,0:T(8,128)} custom-call(s32[3]{0:T(128)S(1)} %get-tuple-element.19.ids_ref, f32[1,200,128]{2,1,0:T(8,128)S(1)} %copy-done.3, f32[8,256]{1,0:T(8,128)S(1)} %select_maximum_fusion.packed_ref, f32[32,384]{1,0:T(8,128)S(1)} %add_add_fusion.sums_ref), custom_call_target="tpu_custom_call" | custom-call | flops 1000 | bytes 1000 | tf_op jit(solution)/shard_map/drift/pallas_call | solution.py:464
  60.7 0.0 collective-permute-done.7.near_b
  60.7 0.0 collective-permute-done.8.far_b
  60.7 0.0 collective-permute-done.14.cross_2
  60.7 5.9 %finish.1 = f32[8,64,16,256]{3,2,1,0:T(8,128)} custom-call(s32[3]{0:T(128)S(1)} %get-tuple-element.19.ids_ref, f32[2,64,16,256]{3,2,1,0:T(8,128)S(1)} %local_update.2.part_ref.ends_ref, f32[6,64,16,256]{3,2,1,0:T(8,128)S(1)} %local_update.3.part_ref, f32[2,3,16,256]{3,2,1,0:T(8,128)S(1)} %collective-permute-done.near_ref.near_a, ...), custom_call_target="tpu_custom_call" | custom-call | flops 1000 | bytes 1000 | tf_op jit(solution)/shard_map/finish/pallas_call | solution.py:537
  (12 shorter events, 0.1 us)
Async XLA Ops:
  0.6 9.9 %copy-start.1 = (f32[128,8]{1,0:T(8,128)S(1)}, f32[128,8]{1,0:T(8,128)}, u32[]{:S(2)}) copy-start(f32[128,8]{1,0:T(8,128)} %constant.30.clone.pick_ref) | copy-start | bytes 12292
  0.6 9.8 %copy-start.2 = (f32[128,128]{1,0:T(8,128)S(1)}, f32[128,128]{1,0:T(8,128)}, u32[]{:S(2)}) copy-start(f32[128,128]{1,0:T(8,128)} %constant.31.clone.same_ref) | copy-start | bytes 196612
  0.7 9.8 %copy-start.10 = (f32[2]{0:T(128)S(1)}, f32[2]{0:T(128)}, u32[]{:S(2)}) copy-start(f32[2]{0:T(128)} %speed_ref.5) | copy-start | bytes 28
  0.7 9.8 %copy-start.6 = (f32[2,8,8]{2,1,0:T(8,128)S(1)}, f32[2,8,8]{2,1,0:T(8,128)}, u32[]{:S(2)}) copy-start(f32[2,8,8]{2,1,0:T(8,128)} %matrix_ref.5) | copy-start | bytes 1540
  6.7 9.5 %copy-start.11 = (s32[32]{0:T(128)S(1)}, s32[32]{0:T(128)}, u32[]{:S(2)}) copy-start(s32[32]{0:T(128)} %param.29) | copy-start | bytes 388
  6.7 9.5 %copy-start.12 = (s32[1,64,1]{1,2,0:T(1,128)S(1)}, s32[1,64,1]{1,2,0:T(1,128)}, u32[]{:S(2)}) copy-start(s32[1,64,1]{1,2,0:T(1,128)} %param.28) | copy-start | bytes 772
  6.7 9.5 %copy-start.4 = (f32[128,128]{1,0:T(8,128)S(1)}, f32[128,128]{1,0:T(8,128)}, u32[]{:S(2)}) copy-start(f32[128,128]{1,0:T(8,128)} %constant.32.clone.sum_ref) | copy-start | bytes 196612
  6.7 9.5 %copy-start.5 = (f32[128,128]{1,0:T(8,128)S(1)}, f32[128,128]{1,0:T(8,128)}, u32[]{:S(2)}) copy-start(f32[128,128]{1,0:T(8,128)} %constant.33.clone.gap_ref) | copy-start | bytes 196612
  6.7 16.3 %collective-permute-start.2 = (f32[64,24,256]{2,1,0:T(8,128)S(1)}, f32[64,24,256]{2,1,0:T(8,128)S(1)}, u32[]{:S(2)}, u32[]{:S(2)}) collective-permute-start(f32[64,24,256]{2,1,0:T(8,128)S(1)} %get-tuple-element.25), channel_id=1, source_target_pairs={{0,1},{1,0},{2,3},{3,2},{4,5},{5,4},{6,7},{7,6},{8,9},{9,8},{10,11... | collective-permute-start | bytes 4718600 | tf_op jit(solution)/shard_map/ppermute | solution.py:554
  6.8 16.2 %collective-permute-start.3 = (f32[64,8,256]{2,1,0:T(8,128)S(1)}, f32[64,8,256]{2,1,0:T(8,128)S(1)}, u32[]{:S(2)}, u32[]{:S(2)}) collective-permute-start(f32[64,8,256]{2,1,0:T(8,128)S(1)} %get-tuple-element.26), channel_id=1, source_target_pairs={{0,7},{1,2},{2,1},{3,4},{4,3},{5,6},{6,5},{7,0},{8,15},{9,10},{10,... | collective-permute-start | bytes 1572872 | tf_op jit(solution)/shard_map/ppermute | solution.py:577
  12.0 10.2 %copy-start.13 = (f32[2,200]{1,0:T(2,128)S(1)}, f32[2,200]{1,0:T(2,128)}, u32[]{:S(2)}) copy-start(f32[2,200]{1,0:T(2,128)} %param.31) | copy-start | bytes 4804
  12.0 10.2 %copy-start.14 = (f32[200]{0:T(256)S(1)}, f32[200]{0:T(256)}, u32[]{:S(2)}) copy-start(f32[200]{0:T(256)} %param.33) | copy-start | bytes 2404
  12.1 10.2 %copy-start.15 = (f32[200]{0:T(256)S(1)}, f32[200]{0:T(256)}, u32[]{:S(2)}) copy-start(f32[200]{0:T(256)} %param.32) | copy-start | bytes 2404
  12.1 10.2 %copy-start.3 = (f32[1,200,128]{2,1,0:T(8,128)S(1)}, f32[1,200,128]{2,1,0:T(8,128)}, u32[]{:S(2)}) copy-start(f32[1,200,128]{2,1,0:T(8,128)} %density_ref.3) | copy-start | bytes 307204
  12.1 10.9 %copy-start = (f32[64,16,256]{2,1,0:T(8,128)S(1)}, f32[64,16,256]{2,1,0:T(8,128)}, u32[]{:S(2)}) copy-start(f32[64,16,256]{2,1,0:T(8,128)} %vol_ref.1) | copy-start | bytes 3145732
  12.1 10.9 %copy-start.8 = (bf16[256,128]{1,0:T(8,128)(2,1)S(1)}, bf16[256,128]{1,0:T(8,128)(2,1)}, u32[]{:S(2)}) copy-start(bf16[256,128]{1,0:T(8,128)(2,1)} %constant.34.clone.seg_ref) | copy-start | bytes 196612
  12.1 10.9 %copy-start.9 = (f32[16,128]{1,0:T(8,128)S(1)}, f32[16,128]{1,0:T(8,128)}, u32[]{:S(2)}) copy-start(f32[16,128]{1,0:T(8,128)} %constant.35.clone.spot_ref) | copy-start | bytes 24580
  12.1 10.9 %collective-permute-start = (f32[2,3,16,256]{3,2,1,0:T(8,128)S(1)}, f32[2,3,16,256]{3,2,1,0:T(8,128)S(1)}, u32[]{:S(2)}, u32[]{:S(2)}) collective-permute-start(f32[2,3,16,256]{3,2,1,0:T(8,128)S(1)} %get-tuple-element.21), channel_id=1, source_target_pairs={{0,8},{8,0},{16,24},{24,16},{1,9},{9,1},{17,25},{25,17},{2,10},{10... | collective-permute-start | bytes 294920 | tf_op jit(solution)/shard_map/ppermute | solution.py:554
  13.7 9.3 %collective-permute-start.1 = (f32[2,3,16,256]{3,2,1,0:T(8,128)S(1)}, f32[2,3,16,256]{3,2,1,0:T(8,128)S(1)}, u32[]{:S(2)}, u32[]{:S(2)}) collective-permute-start(f32[2,3,16,256]{3,2,1,0:T(8,128)S(1)} %get-tuple-element.22), channel_id=1, source_target_pairs={{8,16},{16,8},{9,17},{17,9},{10,18},{18,10},{11,19},{19,11},{12,20... | collective-permute-start | bytes 294920 | tf_op jit(solution)/shard_map/ppermute | solution.py:582
  16.0 17.6 %collective-permute-start.10 = (f32[64,8,256]{2,1,0:T(8,128)S(1)}, f32[64,8,256]{2,1,0:T(8,128)S(1)}, u32[]{:S(2)}, u32[]{:S(2)}) collective-permute-start(f32[64,8,256]{2,1,0:T(8,128)S(1)} %get-tuple-element.30), channel_id=1, source_target_pairs={{0,7},{1,2},{2,1},{3,4},{4,3},{5,6},{6,5},{7,0},{8,15},{9,10},{10,... | collective-permute-start | bytes 1572872 | tf_op jit(solution)/shard_map/ppermute | solution.py:579
  25.4 5.5 %collective-permute-start.6 = (f32[32,384]{1,0:T(8,128)S(1)}, f32[32,384]{1,0:T(8,128)S(1)}, u32[]{:S(2)}, u32[]{:S(2)}) collective-permute-start(f32[32,384]{1,0:T(8,128)S(1)} %tile_sums.1), channel_id=1, source_target_pairs={{0,24},{8,16},{16,8},{24,0},{1,25},{9,17},{17,9},{25,1},{2,26},{10... | collective-permute-start | bytes 147464 | tf_op jit(solution)/shard_map/ppermute | solution.py:554
  27.9 4.1 %collective-permute-start.5 = (f32[32,384]{1,0:T(8,128)S(1)}, f32[32,384]{1,0:T(8,128)S(1)}, u32[]{:S(2)}, u32[]{:S(2)}) collective-permute-start(f32[32,384]{1,0:T(8,128)S(1)} %tile_sums.1), channel_id=1, source_target_pairs={{0,16},{8,24},{16,0},{24,8},{1,17},{9,25},{17,1},{25,9},{2,18},{10... | collective-permute-start | bytes 147464 | tf_op jit(solution)/shard_map/ppermute | solution.py:554
  28.2 4.1 %collective-permute-start.4 = (f32[32,384]{1,0:T(8,128)S(1)}, f32[32,384]{1,0:T(8,128)S(1)}, u32[]{:S(2)}, u32[]{:S(2)}) collective-permute-start(f32[32,384]{1,0:T(8,128)S(1)} %tile_sums.1), channel_id=1, source_target_pairs={{0,8},{8,0},{16,24},{24,16},{1,9},{9,1},{17,25},{25,17},{2,10},{10... | collective-permute-start | bytes 147464 | tf_op jit(solution)/shard_map/ppermute | solution.py:554
  32.3 1.3 %collective-permute-start.9 = (f32[32,384]{1,0:T(8,128)S(1)}, f32[32,384]{1,0:T(8,128)S(1)}, u32[]{:S(2)}, u32[]{:S(2)}) collective-permute-start(f32[32,384]{1,0:T(8,128)S(1)} %add_add_fusion.1), channel_id=1, source_target_pairs={{0,1},{1,0},{2,3},{3,2},{4,5},{5,4},{6,7},{7,6},{8,9},{9,8},{10,11... | collective-permute-start | bytes 147464 | tf_op jit(solution)/shard_map/ppermute | solution.py:554
  33.6 6.2 %collective-permute-start.13 = (f32[32,384]{1,0:T(8,128)S(1)}, f32[32,384]{1,0:T(8,128)S(1)}, u32[]{:S(2)}, u32[]{:S(2)}) collective-permute-start(f32[32,384]{1,0:T(8,128)S(1)} %add.30), channel_id=1, source_target_pairs={{0,6},{1,7},{2,4},{3,5},{4,2},{5,3},{6,0},{7,1},{8,14},{9,15},{10,... | collective-permute-start | bytes 147464 | tf_op jit(solution)/shard_map/ppermute | solution.py:554
  36.0 5.3 %collective-permute-start.12 = (f32[32,384]{1,0:T(8,128)S(1)}, f32[32,384]{1,0:T(8,128)S(1)}, u32[]{:S(2)}, u32[]{:S(2)}) collective-permute-start(f32[32,384]{1,0:T(8,128)S(1)} %add.30), channel_id=1, source_target_pairs={{0,4},{1,5},{2,6},{3,7},{4,0},{5,1},{6,2},{7,3},{8,12},{9,13},{10,... | collective-permute-start | bytes 147464 | tf_op jit(solution)/shard_map/ppermute | solution.py:554
  36.0 5.3 %collective-permute-start.11 = (f32[32,384]{1,0:T(8,128)S(1)}, f32[32,384]{1,0:T(8,128)S(1)}, u32[]{:S(2)}, u32[]{:S(2)}) collective-permute-start(f32[32,384]{1,0:T(8,128)S(1)} %add.30), channel_id=1, source_target_pairs={{0,2},{1,3},{2,0},{3,1},{4,6},{5,7},{6,4},{7,5},{8,10},{9,11},{10,... | collective-permute-start | bytes 147464 | tf_op jit(solution)/shard_map/ppermute | solution.py:554
  41.4 19.3 %copy-start.7 = (bf16[128,256]{1,0:T(8,128)(2,1)S(1)}, bf16[128,256]{1,0:T(8,128)(2,1)}, u32[]{:S(2)}) copy-start(bf16[128,256]{1,0:T(8,128)(2,1)} %constant.36.clone.seg_ref) | copy-start | bytes 196612
  41.4 19.3 %collective-permute-start.14 = (f32[64,8,256]{2,1,0:T(8,128)S(1)}, f32[64,8,256]{2,1,0:T(8,128)S(1)}, u32[]{:S(2)}, u32[]{:S(2)}) collective-permute-start(f32[64,8,256]{2,1,0:T(8,128)S(1)} %get-tuple-element.34), channel_id=1, source_target_pairs={{0,7},{1,2},{2,1},{3,4},{4,3},{5,6},{6,5},{7,0},{8,15},{9,10},{10,... | collective-permute-start | bytes 1572872 | tf_op jit(solution)/shard_map/ppermute | solution.py:609
  43.7 17.0 %collective-permute-start.7 = (f32[6,3,16,256]{3,2,1,0:T(8,128)S(1)}, f32[6,3,16,256]{3,2,1,0:T(8,128)S(1)}, u32[]{:S(2)}, u32[]{:S(2)}) collective-permute-start(f32[6,3,16,256]{3,2,1,0:T(8,128)S(1)} %get-tuple-element.27), channel_id=1, source_target_pairs={{0,8},{8,0},{16,24},{24,16},{1,9},{9,1},{17,25},{25,17},{2,10},{10... | collective-permute-start | bytes 884744 | tf_op jit(solution)/shard_map/ppermute | solution.py:554
  43.7 17.0 %collective-permute-start.8 = (f32[6,3,16,256]{3,2,1,0:T(8,128)S(1)}, f32[6,3,16,256]{3,2,1,0:T(8,128)S(1)}, u32[]{:S(2)}, u32[]{:S(2)}) collective-permute-start(f32[6,3,16,256]{3,2,1,0:T(8,128)S(1)} %get-tuple-element.28), channel_id=1, source_target_pairs={{8,16},{16,8},{9,17},{17,9},{10,18},{18,10},{11,19},{19,11},{12,20... | collective-permute-start | bytes 884744 | tf_op jit(solution)/shard_map/ppermute | solution.py:604
where the time goes:
time: 66.8 us; the launch traced here: 66.6 us
  Pallas kernels  34.5 us (52%)
  starting transfers between devices  22.9 us (34%)
  waiting for transfers between devices  7.94 us (12%)
  between operations  0.99 us (1%)
    pallas_call x2, Pallas kernels, local_update(): pl.pallas_call(functools.partial(local_kernel, mine), in_specs=[SMEM] + [...  16.4 us
    ppermute x10, starting transfers between devices, swap(): lax.ppermute(x, axis, [(i, i ^ bit) for i in range(lax.axis_size(axis))])  9.65 us
    ppermute x10, waiting for transfers between devices, swap(): lax.ppermute(x, axis, [(i, i ^ bit) for i in range(lax.axis_size(axis))])  7.93 us
    pallas_call x1, Pallas kernels, lon_edges(): pl.pallas_call(lon_edge_kernel, in_specs=[SMEM] * 3 + [HBM] * 4, out_spec...  5.96 us
    pallas_call x1, Pallas kernels, finish(): pl.pallas_call(finish_kernel, in_specs=[SMEM] + [VMEM] * (len(pins) + 5),...  5.89 us
    ppermute x1, starting transfers between devices, per_device(): rad_b = (swap(near_b, 'rad', 1), lax.ppermute(far_b, 'rad', beyond))  4.85 us
    ppermute x1, starting transfers between devices, per_device(): cross_0 = lax.ppermute(crosses[0], 'lon', across)  3.7 us
    ppermute x1, starting transfers between devices, per_device(): rad_a = (swap(near_a, 'rad', 1), lax.ppermute(far_a, 'rad', beyond))  2.37 us
  transfers between devices with their start and end apart: 15, of which 6 were waited for; matrix products, arithmetic and copies ran while one was open for 0% of the time, Pallas kernels for 34%

commit v1 on v0

v1 whole, which is shorter than its diff:
```python
import functools

import jax
import jax.numpy as jnp
import numpy as np
from jax import lax
from jax.experimental import pallas as pl
from jax.experimental.pallas import tpu as pltpu
from jax.sharding import PartitionSpec as P

ZSEG = 8
DRIFT = 3
REACH = 3

courant_step = 0.4
nudge_rate = 0.5
inner_step = 0.5

SUM_TAPS = {k: v / 60.0 for k, v in zip(range(-3, 4), (-2.0, 18.0, -90.0, 0.0, 90.0, -18.0, 2.0))}
GAP_TAPS = {k: v / 60.0 for k, v in zip(range(-3, 4), (2.0, -12.0, 30.0, -40.0, 30.0, -12.0, 2.0))}

PACKED = (0, 7, 1, 2, 3, 4, 5, 6)

f32 = jnp.float32
bf16 = jnp.bfloat16


def cost(flops, bytes_accessed):
    return pl.CostEstimate(flops=int(flops), bytes_accessed=int(bytes_accessed), transcendentals=0)


def parts_of(x, count):
    parts = []
    for _ in range(count):
        part = x.astype(bf16)
        parts.append(part)
        x = x - part.astype(f32)
    return parts


def dot(a, b):
    return jnp.dot(a, b, preferred_element_type=f32)


def exact_dot(x, ones):
    return sum(dot(part, ones) for part in parts_of(x, 3))


def lon_tables(rows, cols):
    fields = 1 + max(f for f, _ in cols)
    pick_row = np.array([[float(f == a) for a in range(fields)] for f, _ in rows], np.float32)
    pick_col = np.array([[float(f == b) for f, _ in cols] for b in range(fields)], np.float32)
    summed = np.array([[0.0 if s is None else SUM_TAPS.get(s - t, 0.0) for _, s in cols] for _, t in rows], np.float32)
    gapped = np.array(
        [[0.0 if s is None or f != g else GAP_TAPS.get(s - t, 0.0) for g, s in cols] for f, t in rows], np.float32
    )
    return pick_row, pick_col, summed, gapped


def lon_weights(matrix, wave_rate, pick_row, pick_col, summed, gapped):
    half = 0.5 * courant_step
    spread = f32_dot(f32_dot(pick_row, matrix), pick_col)
    return (half * wave_rate) * gapped - half * spread * summed


def f32_dot(a, b):
    return jnp.dot(a, b, precision=lax.Precision.HIGHEST, preferred_element_type=f32)


def whole(array):
    zeros = (0,) * array.ndim
    return pl.BlockSpec(array.shape, lambda *_: zeros)


SMEM = pl.BlockSpec(memory_space=pltpu.SMEM)
VMEM = pl.BlockSpec(memory_space=pltpu.VMEM)
HBM = pl.BlockSpec(memory_space=pltpu.HBM)
LARGE = pltpu.CompilerParams(vmem_limit_bytes=18 * 2**20)
SMALL = pltpu.CompilerParams(vmem_limit_bytes=4 * 2**20)
CHUNK = 8
AHEAD = 3
GROUP = 4
RING = 4


def in_vmem(*shape):
    return pltpu.VMEM(shape, f32)


def pinned(x):
    return pltpu.with_memory_space_constraint(x, pltpu.VMEM)


def lon_edge_kernel(lon_ref, rad_ref, place_ref, state_hbm, speed_hbm, matrix_hbm, table_hbm, rim, ids_ref, same, *refs):
    *crosses, speed_ref, matrix_ref, table_ref, edges, weights, sem, few_sem = refs
    fields, rows, cols, depth = state_hbm.shape
    chunks = rows // CHUNK
    size = same.shape[1]
    keep = edges.shape[2] // 2

    def loads(c):
        here = pl.ds(c * CHUNK, CHUNK)
        return [
            pltpu.make_async_copy(
                state_hbm.at[:, here, pl.ds(first, keep)], edges.at[:, here, pl.ds(slot, keep)], sem.at[2 * c + i]
            )
            for i, (first, slot) in enumerate(((0, 0), (cols - keep, keep)))
        ]

    few = [(speed_hbm, speed_ref), (matrix_hbm, matrix_ref), (table_hbm, table_ref)]
    few += [(state_hbm.at[:, pl.ds(0, REACH)], rim.at[:, pl.ds(0, REACH)])]
    few += [(state_hbm.at[:, pl.ds(rows - REACH, REACH)], rim.at[:, pl.ds(REACH, REACH)])]
    few = [pltpu.make_async_copy(source, target, few_sem.at[i]) for i, (source, target) in enumerate(few)]
    for copy in few[:3]:
        copy.start()
    for c in range(chunks):
        for copy in loads(c):
            copy.start()
    for copy in few[3:]:
        copy.start()
    ids_ref[0] = lon_ref[0]
    ids_ref[1] = rad_ref[0]
    ids_ref[2] = place_ref[0]
    for copy in few[:3]:
        copy.wait()
    wide = 8 * fields
    w = lon_weights(
        matrix_ref[1], speed_ref[1], table_ref[0, :, :fields], table_ref[1, :fields, :wide], table_ref[2, :, :wide],
        table_ref[3, :, :wide],
    )
    swap = lon_ref[0] % 2 == 1
    w = jnp.concatenate([jnp.where(swap, w[size:], w[:size]), jnp.where(swap, w[:size], w[size:])], axis=0)
    high, low = parts_of(w, 2)
    weights[...] = jnp.concatenate([high, high, low], axis=1)

    def step(c, carry):
        for copy in loads(c):
            copy.wait()
        for j in range(CHUNK):
            r = c * CHUNK + j
            high, low = parts_of(edges[:, r].reshape(-1, depth), 2)
            sums = dot(weights[...], jnp.concatenate([high, low, high], axis=0))
            same[r] = sums[:size]
            first, rest = crosses
            first[r] = sums[size : size + 8]
            rest[r] = sums[size + 8 :]
        return carry

    lax.fori_loop(0, chunks, step, 0)
    for copy in few[3:]:
        copy.wait()


def lon_edges(state, matrices, speed, lon, rad, place):
    fields, rows, cols, depth = state.shape
    keep = 4
    sources = [(f, l if l < keep else cols - 2 * keep + l) for f in range(fields) for l in range(2 * keep)]
    sources = [(f, l if l < REACH or l >= cols - REACH else None) for f, l in sources]
    to_right = [(f, cols + t) for f in PACKED for t in range(REACH)]
    to_left = [(f, t - REACH) for f in PACKED for t in range(REACH)]
    size = fields * REACH
    tables = np.zeros((4, 2 * size, 128), np.float32)
    for i, table in enumerate(lon_tables(to_right + to_left, sources)):
        tables[i, : table.shape[0], : table.shape[1]] = table
    return pl.pallas_call(
        lon_edge_kernel,
        in_specs=[SMEM] * 3 + [HBM] * 4,
        out_specs=[VMEM, SMEM] + [VMEM] * 3,
        out_shape=[
            in_vmem(fields, 2 * REACH, cols, depth),
            jax.ShapeDtypeStruct((3,), jnp.int32),
            in_vmem(rows, size, depth),
            in_vmem(rows, 8, depth),
            in_vmem(rows, size - 8, depth),
        ],
        scratch_shapes=[
            pltpu.SMEM(speed.shape, f32),
            pltpu.VMEM(matrices.shape, f32),
            pltpu.VMEM(tables.shape, f32),
            pltpu.VMEM((fields, rows, 2 * keep, depth), f32),
            pltpu.VMEM((2 * size, 3 * len(sources)), bf16),
            pltpu.SemaphoreType.DMA((2 * rows // CHUNK,)),
            pltpu.SemaphoreType.DMA((5,)),
        ],
        compiler_params=LARGE,
        cost_estimate=cost(1e3, 1e3),
        name="lon_edges",
    )(lon, rad, place, *[pltpu.with_memory_space_constraint(x, pltpu.HBM) for x in (state, speed, matrices, jnp.asarray(tables))])


def turn_weights(matrix, pick, same):
    return (-0.5 * courant_step) * same * f32_dot(f32_dot(pick, matrix), pick.T)


def turn_tables(fields, cols):
    every = [(f, l) for f in range(fields) for l in range(cols)]
    pick = np.array([[float(f == a) for a in range(fields)] for f, _ in every], np.float32)
    same = np.array([[float(l == m) for _, m in every] for _, l in every], np.float32)
    return pick, same


def rad_edge_kernel(ids_ref, speed_ref, rim_ref, matrix_ref, pick_ref, same_ref, near, far_a, far_b):
    fields, _, cols, depth = rim_ref.shape
    rate = (0.5 * courant_step) * speed_ref[0]
    even = ids_ref[1] % 2 == 0
    high, low = parts_of(turn_weights(matrix_ref[0], pick_ref[...], same_ref[...]), 2)
    w = jnp.concatenate([high, high, low], axis=1)

    def turned(cells):
        high, low = parts_of(cells.reshape(-1, depth), 2)
        return dot(w, jnp.concatenate([high, low, high], axis=0)).reshape(fields, cols, depth)

    first = [rim_ref[:, j] for j in range(REACH)]
    last = [rim_ref[:, REACH + j] for j in range(REACH)]
    first_turned = [turned(cells) for cells in first]
    last_turned = [turned(cells) for cells in last]
    for t in range(REACH):
        up = sum(
            SUM_TAPS[j - REACH - t] * last_turned[j] + (rate * GAP_TAPS[j - REACH - t]) * last[j]
            for j in range(t, REACH)
        )
        down = sum(
            SUM_TAPS[j + REACH - t] * first_turned[j] + (rate * GAP_TAPS[j + REACH - t]) * first[j]
            for j in range(t + 1)
        )
        near[:, t] = jnp.where(even, up, down)
        far = jnp.where(even, down, up)
        far_a[0, t] = far[0]
        far_a[1, t] = far[fields - 1]
        far_b[:, t] = far[1 : fields - 1]


def rad_edges(ids, rim, matrices, speed):
    fields, _, cols, depth = rim.shape
    tables = turn_tables(fields, cols)
    return pl.pallas_call(
        rad_edge_kernel,
        in_specs=[SMEM] * 2 + [VMEM] * (2 + len(tables)),
        out_specs=[VMEM] * 3,
        out_shape=[in_vmem(n, REACH, cols, depth) for n in (fields, 2, fields - 2)],
        compiler_params=LARGE,
        cost_estimate=cost(1e3, 1e3),
        name="rad_edges",
    )(ids, speed, pinned(rim), matrices, *tables)


def add_radial(speed_ref, cells, turned, total, fields, first):
    cols, depth = total.shape[2:]
    rate = (0.5 * courant_step) * speed_ref[0]
    for f in fields:
        for half in range(cols // 8):
            for lane in range(depth // 128):
                lanes = pl.ds(128 * lane, 128)
                u = [cells[f, first + j, pl.ds(8 * half, 8), lanes] for j in range(CHUNK + 2 * REACH)]
                v = [turned[first + j, pl.ds(f * cols + 8 * half, 8), lanes] for j in range(CHUNK + 2 * REACH)]
                for j in range(CHUNK):
                    at = j + REACH
                    value = total[f, first + j, pl.ds(8 * half, 8), lanes] + (rate * GAP_TAPS[0]) * u[at]
                    for k in range(1, REACH + 1):
                        value = value + SUM_TAPS[k] * (v[at + k] - v[at - k])
                        value = value + (rate * GAP_TAPS[k]) * (u[at + k] + u[at - k])
                    total[f, first + j, pl.ds(8 * half, 8), lanes] = value


def local_kernel(speed_ref, state_hbm, matrix_ref, pick_ref, same_ref, sum_ref, gap_ref, total, cells, w_ref, sem, *scratch):
    fields, rows, cols, depth = total.shape
    size = fields * cols
    turned, base = scratch[:RING], scratch[RING:]
    rate = (0.5 * courant_step) * speed_ref[0]
    last_row = cells.shape[1] - 1
    chunks = rows // CHUNK

    def load(c):
        return pltpu.make_async_copy(
            state_hbm.at[:, pl.ds(c * CHUNK, CHUNK)], cells.at[:, pl.ds(REACH + c * CHUNK, CHUNK)], sem.at[c]
        )

    for c in range(AHEAD):
        load(c).start()
    w_ref[...] = local_weights(
        matrix_ref, speed_ref, pick_ref[...], same_ref[...], sum_ref[...], gap_ref[...]
    )
    for edge in (0, REACH + rows):
        cells[:, edge : edge + REACH] = jnp.zeros((fields, REACH, cols, depth), f32)

    def multiply(c, slot, j):
        r = jnp.minimum(REACH + c * GROUP + j, last_row)
        here = cells[:, r].reshape(size, depth)
        high, low = parts_of(here, 2)
        both = dot(w_ref[...], jnp.concatenate([high, low, high], axis=0))
        base[slot][j] = here + both[:size]
        turned[slot][j] = both[size:]

    def radial(c, slot, quarter):
        first = c * GROUP
        groups = fields * (cols // 8) * (depth // 128)
        for g in range(quarter * groups // GROUP, (quarter + 1) * groups // GROUP):
            f, rest = divmod(g, (cols // 8) * (depth // 128))
            half, lane = divmod(rest, depth // 128)
            lanes = pl.ds(128 * lane, 128)
            u = [cells[f, first + j, pl.ds(8 * half, 8), lanes] for j in range(GROUP + 2 * REACH)]
            v = []
            for j in range(-REACH, GROUP + REACH):
                ref = turned[(slot + j // GROUP) % RING]
                v.append(ref[j % GROUP, pl.ds(f * cols + 8 * half, 8), lanes])
            for j in range(GROUP):
                at = j + REACH
                value = base[slot][j, pl.ds(f * cols + 8 * half, 8), lanes] + (rate * GAP_TAPS[0]) * u[at]
                for k in range(1, REACH + 1):
                    value = value + SUM_TAPS[k] * (v[at + k] - v[at - k])
                    value = value + (rate * GAP_TAPS[k]) * (u[at + k] + u[at - k])
                total[f, first + j, pl.ds(8 * half, 8), lanes] = value

    turned[RING - 1][...] = jnp.zeros((GROUP, size, depth), f32)
    load(0).wait()
    load(AHEAD).start()
    for c in range(2):
        for j in range(GROUP):
            multiply(c, c, j)

    ahead = GROUP * RING // CHUNK

    def step(i, carry):
        for c in range(1, ahead + 1):

            @pl.when(ahead * i + c < chunks)
            def _():
                load(ahead * i + c).wait()

            @pl.when(ahead * i + c + AHEAD < chunks)
            def _():
                load(ahead * i + c + AHEAD).start()

        for q in range(RING):
            for j in range(GROUP):
                multiply(RING * i + q + 2, (q + 2) % RING, j)
                radial(RING * i + q, q, j)
        return carry

    lax.fori_loop(0, rows // (GROUP * RING), step, 0)


def local_weights(matrices, speed_ref, pick, same, summed, gapped):
    own = lon_weights(matrices[1], speed_ref[1], pick, pick.T, summed, gapped)
    high, low = parts_of(jnp.concatenate([own, turn_weights(matrices[0], pick, same)], axis=0), 2)
    return jnp.concatenate([high, high, low], axis=1)


def local_update(state, matrices, speed):
    fields, rows, cols, depth = state.shape
    size = fields * cols
    every = [(f, l) for f in range(fields) for l in range(cols)]
    _, _, summed, gapped = lon_tables(every, every)
    return pl.pallas_call(
        local_kernel,
        in_specs=[SMEM, HBM] + [VMEM] * 5,
        out_specs=VMEM,
        out_shape=in_vmem(fields, rows, cols, depth),
        scratch_shapes=[
            pltpu.VMEM((fields, rows + 2 * REACH, cols, depth), f32),
            pltpu.VMEM((2 * size, 3 * size), bf16),
            pltpu.SemaphoreType.DMA((rows // CHUNK,)),
        ]
        + [pltpu.VMEM((GROUP, size, depth), f32)] * (2 * RING),
        compiler_params=LARGE,
        cost_estimate=cost(1e3, 1e3),
        name="local_update",
    )(
        speed, pltpu.with_memory_space_constraint(state, pltpu.HBM), matrices, *turn_tables(fields, cols), summed, gapped
    )


def placed(tiles, field, from_left):
    start = REACH * PACKED.index(field)
    tile, offset = start // 8, start % 8
    cells = tiles[tile]
    sub = lax.broadcasted_iota(jnp.int32, cells.shape, 1)
    if offset + REACH > 8:
        cells = jnp.where(sub >= offset, cells, tiles[tile + 1])
    goal = 0 if from_left else 8 - REACH
    shift = (goal - offset) % 8
    if shift:
        cells = pltpu.roll(cells, shift, 1)
    keep = sub < REACH if from_left else sub >= 8 - REACH
    return jnp.where(keep, cells, 0.0)


def by_side(lon, same, crosses):
    even = lon % 2 == 0
    lefts, rights = {}, {}
    for t, cross in enumerate(crosses):
        near = same[:, 8 * t : 8 * t + 8]
        lefts[t] = jnp.where(even, cross, near)
        rights[t] = jnp.where(even, near, cross)
    return lefts, rights


def with_sides(cells, lefts, rights, field):
    cols = cells.shape[1]
    return jnp.concatenate(
        [cells[:, :8] + placed(lefts, field, True), cells[:, cols - 8 :] + placed(rights, field, False)], axis=1
    )


def with_ends(cells, step, steps, rad, near, far):
    rows = cells.shape[0]
    even = rad % 2 == 0
    below, above = jnp.where(even, far, near), jnp.where(even, near, far)
    at_low = (step == 0).astype(f32)
    at_top = (step == steps - 1).astype(f32)
    return jnp.concatenate(
        [cells[:REACH] + at_low * below, cells[REACH : rows - REACH], cells[rows - REACH :] + at_top * above], axis=0
    )


def tile_sum_kernel(
    ids_ref, part_ref, vol_ref, same_ref, cross_ref, near_ref, far_ref, rest_ref, hit_ref, seg_ref, spot_ref,
    out_ref, lines_ref,
):
    all_rows, cols, depth = vol_ref.shape
    tiles, points = out_ref.shape[0], out_ref.shape[1] // 3
    rows = 16
    steps = all_rows // rows

    def add(step, carry):
        here = pl.ds(pl.multiple_of(step * rows, rows), rows)
        lefts, rights = by_side(ids_ref[0], same_ref[here, :8], [cross_ref[here]])
        vol = vol_ref[here]
        for c, field in enumerate((0, 7)):
            cells = with_sides(part_ref[field, here], lefts, rights, field)
            cells = with_ends(cells, step, steps, ids_ref[1], near_ref[field], far_ref[c])
            lines = exact_dot((cells * vol).reshape(rows * cols, depth), seg_ref[...])
            lines_ref[c, here] = jnp.sum(lines.reshape(rows, cols, -1) * spot_ref[...][None], axis=1)
        return carry

    lax.fori_loop(0, steps, add, 0)
    for c in range(2):
        sums = sum(dot(hit_ref[...], part) for part in parts_of(lines_ref[c], 3))
        out_ref[:, c * points : (c + 1) * points] = sums
    mine = lax.broadcasted_iota(jnp.int32, (tiles, points), 0) == ids_ref[2]
    out_ref[:, 2 * points :] = jnp.where(mine, rest_ref[8:9], 0.0)


def tile_sums(ids, part, vol, same, cross, near, far, rest, hits, seg, spot):
    _, rows, _, _ = part.shape
    points = seg.shape[1]
    tiles = hits.shape[0]
    return pl.pallas_call(
        tile_sum_kernel,
        in_specs=[SMEM] + [VMEM] * 10,
        out_specs=VMEM,
        out_shape=in_vmem(tiles, 3 * points),
        scratch_shapes=[pltpu.VMEM((2, rows, points), f32)],
        compiler_params=LARGE,
        cost_estimate=cost(1e3, 1e3),
        name="tile_sums",
    )(ids, *[pinned(x) for x in (part, vol, same, cross, near, far, rest)], hits, seg, spot)


def drifted(density, courant):
    for _ in range(DRIFT):
        density = density - courant * (density - pltpu.roll(density, 1, 1))
    return density


def columns_of(packed_ref, channels):
    turned = jnp.transpose(packed_ref[...])
    return [turned[:channels, i : i + 1] for i in range(4)]


def rest_kernel(density_ref, packed_ref, out_ref, spread_ref):
    _, channels, points = density_ref.shape
    courant, weight, first, second = columns_of(packed_ref, channels)
    rows = []
    for given in (first, second):
        for k, choices in enumerate((1.0, 3.0, 3.0, 1.0)):
            gain = (inner_step * choices) * weight * given
            for _ in range(k):
                gain = gain * courant
            for _ in range(DRIFT - k):
                gain = gain * (1.0 - courant)
            rows.append(jnp.broadcast_to(jnp.sum(gain, axis=0, keepdims=True), (1, points)))
    rest = jnp.sum(weight * drifted(density_ref[0], courant), axis=0, keepdims=True)
    out_ref[...] = jnp.concatenate(rows + [rest] * 8, axis=0)
    for i, column in enumerate((courant, first, second)):
        spread_ref[i] = jnp.broadcast_to(column, (channels, points))


def rest_of(density, packed):
    _, channels, points = density.shape
    return pl.pallas_call(
        rest_kernel,
        out_shape=[in_vmem(16, points), in_vmem(3, channels, points)],
        compiler_params=SMALL,
        cost_estimate=cost(1e3, 1e3),
        name="rest_pressure",
    )(density, packed)


def pressures_of(sums, rest_ref):
    points = sums.shape[1] // 3
    pressure = sums[:, 2 * points :]
    for c in range(2):
        source = sums[:, c * points : (c + 1) * points]
        for k in range(DRIFT + 1):
            shifted = pltpu.roll(source, k, 1) if k else source
            pressure = pressure + rest_ref[(DRIFT + 1) * c + k : (DRIFT + 1) * c + k + 1] * shifted
    return pressure


def finish_field(field, refs, part_ref, done, step_of=None):
    ids_ref, near_ref, far_a, far_b, same_ref, *cross_refs = refs
    rows = CHUNK
    steps = done.shape[1] // rows
    last_field = near_ref.shape[0] - 1

    def step(i, carry):
        here = pl.ds(pl.multiple_of(i * rows, rows), rows)
        lefts, rights = {}, {}
        first = REACH * PACKED.index(field)
        for t in range(first // 8, (first + REACH - 1) // 8 + 1):
            cross = cross_refs[0][here] if t == 0 else cross_refs[1][here, 8 * t - 8 : 8 * t]
            one = by_side(ids_ref[0], same_ref[here, 8 * t : 8 * t + 8], [cross])
            lefts[t], rights[t] = one[0][0], one[1][0]
        far = far_a[field // last_field] if field in (0, last_field) else far_b[field - 1]
        cells = with_sides(part_ref[field, here], lefts, rights, field)
        cells = with_ends(cells, i, steps, ids_ref[1], near_ref[field], far)
        done[min(field, done.shape[0] - 1), here] = cells if step_of is None else step_of(here, cells)
        return carry

    lax.fori_loop(0, steps, step, 0)


def most_kernel(ids_ref, part_ref, *refs):
    *sides, out_hbm, done, sem = refs
    copies = []
    for field in range(done.shape[0]):
        finish_field(field, (ids_ref, *sides), part_ref, done)
        copies.append(pltpu.make_async_copy(done.at[field], out_hbm.at[field], sem.at[field]))
        copies[-1].start()
    for copy in copies:
        copy.wait()


def last_kernel(ids_ref, part_ref, *refs):
    *sides, _, hit_ref, sums_ref, rest_ref, spot_ref, seg_ref, density_ref, spread_ref = refs[:-6]
    out_hbm, drifted_hbm, done, back_ref, moved, sem = refs[-6:]
    points = spot_ref.shape[1]
    _, _, cols, depth = done.shape
    last = part_ref.shape[0] - 1

    source = sums_ref[pl.ds(ids_ref[2], 1), :]
    density = density_ref[0] + inner_step * (
        spread_ref[1] * source[:, :points] + spread_ref[2] * source[:, points : 2 * points]
    )
    moved[0] = drifted(density, spread_ref[0])
    copies = [pltpu.make_async_copy(moved, drifted_hbm, sem.at[0])]
    copies[0].start()
    back_ref[...] = sum(dot(hit_ref[...], p) for p in parts_of(pressures_of(sums_ref[...], rest_ref), 3))

    def nudged(here, cells):
        spread = (back_ref[here][:, None, :] * spot_ref[...][None]).reshape(-1, points)
        returned = exact_dot(spread, seg_ref[...]).reshape(-1, cols, depth)
        return cells + nudge_rate * (returned - cells)

    finish_field(last, (ids_ref, *sides), part_ref, done, nudged)
    copies.append(pltpu.make_async_copy(done.at[0], out_hbm.at[last], sem.at[1]))
    copies[1].start()
    for copy in copies:
        copy.wait()


def pressures_of(sums, rest_ref):
    points = sums.shape[1] // 3
    pressure = sums[:, 2 * points :]
    for c in range(2):
        source = sums[:, c * points : (c + 1) * points]
        for k in range(DRIFT + 1):
            shifted = pltpu.roll(source, k, 1) if k else source
            pressure = pressure + rest_ref[(DRIFT + 1) * c + k : (DRIFT + 1) * c + k + 1] * shifted
    return pressure


def finish_most(ids, part, rad, same, crosses):
    fields, rows, cols, depth = part.shape
    pins = [pinned(x) for x in (part, *rad, same, *crosses)]
    return pl.pallas_call(
        most_kernel,
        in_specs=[SMEM] + [VMEM] * len(pins),
        out_specs=HBM,
        out_shape=jax.ShapeDtypeStruct(part.shape, f32),
        scratch_shapes=[pltpu.VMEM((fields - 1, rows, cols, depth), f32), pltpu.SemaphoreType.DMA((fields - 1,))],
        compiler_params=LARGE,
        cost_estimate=cost(1e8, 1.6e7),
        name="finish_most",
    )(ids, *pins)


def finish_last(ids, part, rad, same, crosses, most, hits, sums, rest, spot, seg, density, spread):
    fields, rows, cols, depth = part.shape
    pins = [pinned(x) for x in (part, *rad, same, *crosses)]
    return pl.pallas_call(
        last_kernel,
        in_specs=[SMEM] + [VMEM] * len(pins) + [HBM] + [VMEM] * 7,
        out_specs=[HBM, HBM],
        out_shape=[jax.ShapeDtypeStruct(part.shape, f32), jax.ShapeDtypeStruct(density.shape, f32)],
        input_output_aliases={1 + len(pins): 0},
        scratch_shapes=[
            pltpu.VMEM((1, rows, cols, depth), f32),
            pltpu.VMEM((rows, spot.shape[1]), f32),
            pltpu.VMEM(density.shape, f32),
            pltpu.SemaphoreType.DMA((2,)),
        ],
        compiler_params=LARGE,
        cost_estimate=cost(1e3, 1e3),
        name="finish_last",
    )(ids, *pins, most, hits, pinned(sums), pinned(rest), spot, seg, density, pinned(spread))


def swap(x, axis, bit):
    return lax.ppermute(x, axis, [(i, i ^ bit) for i in range(lax.axis_size(axis))])


def per_device(
    state,
    flux_matrices,
    wave_speed,
    flux_volume,
    block_tile,
    tile_of_device,
    phase_density,
    injection,
    drift_courant,
    energy_weight,
):
    fields, rows, cols, depth = state.shape
    n_rad, n_lon = lax.axis_size("rad"), lax.axis_size("lon")
    points = cols * ZSEG
    lon, rad, place = [lax.axis_index(axes).astype(jnp.int32).reshape(1) for axes in ("lon", "rad", ("rad", "lon"))]

    across = [(i, (i + 1 if i % 2 else i - 1) % n_lon) for i in range(n_lon)]
    beyond = [(i, j) for i in range(n_rad) for j in [i + 1 if i % 2 else i - 1] if 0 <= j < n_rad]
    rim, ids, same, *crosses = lon_edges(state, flux_matrices, wave_speed, lon, rad, place)
    cross_0 = lax.ppermute(crosses[0], "lon", across)
    same = swap(same, "lon", 1)
    cross_1 = lax.ppermute(crosses[1], "lon", across)

    near, far_a, far_b = rad_edges(ids, rim, flux_matrices, wave_speed)
    far_a = lax.ppermute(far_a, "rad", beyond)
    near = swap(near, "rad", 1)

    packed = jnp.concatenate([drift_courant[None], energy_weight[None], injection], axis=0)
    packed = jnp.pad(packed, ((0, 4), (0, -packed.shape[1] % 128)))
    rest, spread = rest_of(phase_density, packed)

    part = local_update(state, flux_matrices, wave_speed)

    targets = block_tile[0, :, 0]
    hits = (tile_of_device[:, None] == targets[None, :]).astype(bf16)
    hits_back = (targets[:, None] == tile_of_device[None, :]).astype(bf16)
    seg_cells = depth // ZSEG
    seg = np.array([[float(p % ZSEG == z // seg_cells) for p in range(points)] for z in range(depth)], np.float32)
    spot = np.array([[float(p // ZSEG == l) for p in range(points)] for l in range(cols)], np.float32)
    sums = tile_sums(
        ids, part, flux_volume, same, cross_0, near, far_a, rest, hits, jnp.asarray(seg, bf16), jnp.asarray(spot)
    )
    def summed(sums, axis, steps):
        return sum([swap(sums, axis, step) for step in steps], sums)

    far_b, sums = lax.optimization_barrier((far_b, sums))
    far_b = lax.ppermute(far_b, "rad", beyond)
    sums = summed(sums, "rad", range(1, n_rad))
    sums = summed(sums, "lon", [1])
    others = [swap(sums, "lon", step) for step in range(2, n_lon, 2)]
    rad_sums = (near, far_a, far_b)
    most = finish_most(ids, part, rad_sums, same, (cross_0, cross_1))
    sums, most = lax.optimization_barrier((sums, most))
    sums = sum(others, sums)
    done, density = finish_last(
        ids, part, rad_sums, same, (cross_0, cross_1), most, hits_back, sums, rest, jnp.asarray(spot),
        jnp.asarray(seg.T, bf16), phase_density, spread,
    )
    return done, density


def solution(mesh):
    in_specs = (
        P(None, "rad", "lon", None),
        P(),
        P(),
        P("rad", "lon", None),
        P("lon", "rad", None),
        P(),
        P(("rad", "lon"), None, None),
        P(),
        P(),
        P(),
    )
    out_specs = (P(None, "rad", "lon", None), P(("rad", "lon"), None, None))
    return jax.shard_map(per_device, mesh=mesh, in_specs=in_specs, out_specs=out_specs, check_vma=False)
```

time: 66.8 us -> 54 us (0.81)
  the two profiles are of different devices: /device:TPU:4 before, /device:TPU:0 now
where the time goes in v1:
time: 54 us; the launch traced here: 53.9 us
  Pallas kernels  29 us (54%)
  starting transfers between devices  18.3 us (34%)
  waiting for transfers between devices  5.24 us (10%)
  between operations  1.01 us (2%)
    pallas_call x1, Pallas kernels, local_update(): pl.pallas_call(local_kernel, in_specs=[SMEM, HBM] + [VMEM] * 5, out_specs...  12.7 us
    ppermute x9, starting transfers between devices, swap(): lax.ppermute(x, axis, [(i, i ^ bit) for i in range(lax.axis_size(axis))])  12.3 us
    ppermute x9, waiting for transfers between devices, swap(): lax.ppermute(x, axis, [(i, i ^ bit) for i in range(lax.axis_size(axis))])  5.23 us
    ppermute x1, starting transfers between devices, per_device(): cross_0 = lax.ppermute(crosses[0], 'lon', across)  4.71 us
    pallas_call x1, Pallas kernels, lon_edges(): pl.pallas_call(lon_edge_kernel, in_specs=[SMEM] * 3 + [HBM] * 4, out_spec...  4.34 us
    pallas_call x1, Pallas kernels, finish_most(): pl.pallas_call(most_kernel, in_specs=[SMEM] + [VMEM] * len(pins), out_spe...  3.97 us
    pallas_call x1, Pallas kernels, finish_last(): pl.pallas_call(last_kernel, in_specs=[SMEM] + [VMEM] * len(pins) + [HBM]...  3.43 us
    pallas_call x1, Pallas kernels, tile_sums(): pl.pallas_call(tile_sum_kernel, in_specs=[SMEM] + [VMEM] * 10, out_specs=...  2.37 us
  transfers between devices with their start and end apart: 13, of which 3 were waited for; matrix products, arithmetic and copies ran while one was open for 0% of the time, Pallas kernels for 39%

profile of v1, /device:TPU:0, one launch (start us, length us, event | category | flops | bytes accessed | tf_op | source)
XLA Modules:
  0.0 53.9 jit_solution(17157909388532501937)
XLA Ops:
  0.6 0.0 copy-start.2
  0.6 0.0 copy-start.3
  0.7 0.0 copy-start.7
  0.7 0.0 copy-start.8
  0.7 0.0 copy-start.10
  0.7 0.0 copy-start.4
  0.7 0.0 copy-start.11
  0.7 0.0 copy-start.12
  0.7 0.0 copy-start.14
  0.7 0.0 copy-start.15
  0.7 0.0 copy-start.13
  0.8 0.0 copy-start.1
  0.8 4.3 %lon_edges.1 = (f32[8,6,16,256]{3,2,1,0:T(8,128)S(1)}, s32[3]{0:T(128)S(1)}, f32[64,24,256]{2,1,0:T(8,128)S(1)}, f32[64,8,256]{2,1,0:T(8,128)S(1)}, f32[64,16,256]{2,1,0:T(8,128)S(1)}) custom-call(s32[1]{0:T(128)} %bitcast.lon_ref, s32[1]{0:T(128)} %bitcast.1.rad_ref, s32[1]{0:T(128)} %bitcast.2.place_ref, f32[8,64,16,256]{3,2,1,0:T(8,128)} %state_hbm.3, ...), custom_call_target="tpu_custom_call" | custom-call | flops 1000 | bytes 1000 | tf_op jit(solution)/shard_map/lon_edges/pallas_call | solution.py:165
  5.1 0.5 collective-permute-start.2
  5.6 4.7 %collective-permute-start.3 = (f32[64,8,256]{2,1,0:T(8,128)S(1)}, f32[64,8,256]{2,1,0:T(8,128)S(1)}, u32[]{:S(2)}, u32[]{:S(2)}) collective-permute-start(f32[64,8,256]{2,1,0:T(8,128)S(1)} %get-tuple-element.22), channel_id=1, source_target_pairs={{0,7},{1,2},{2,1},{3,4},{4,3},{5,6},{6,5},{7,0},{8,15},{9,10},{10,... | collective-permute-start | bytes 1572872 | tf_op jit(solution)/shard_map/ppermute | solution.py:644
  10.3 0.0 collective-permute-start.5
  10.4 0.0 copy-done.2
  10.4 0.0 copy-done.3
  10.4 0.0 copy-done.10
  10.4 0.0 copy-done.4
  10.4 1.5 %rad_edges.1 = (f32[8,3,16,256]{3,2,1,0:T(8,128)S(1)}, f32[2,3,16,256]{3,2,1,0:T(8,128)S(1)}, f32[6,3,16,256]{3,2,1,0:T(8,128)S(1)}) custom-call(s32[3]{0:T(128)S(1)} %get-tuple-element.16.ids_ref, f32[2]{0:T(128)S(1)} %copy-done.10, f32[8,6,16,256]{3,2,1,0:T(8,128)S(1)} %get-tuple-element.17.rim_ref, f32[2,8,8]{2,1,0:T(8,128)S(1)} %copy-done.4, ...), custom_call_target="tpu_custom_call" | custom-call | flops 1000 | bytes 1000 | tf_op jit(solution)/shard_map/rad_edges/pallas_call | solution.py:236
  11.9 1.6 %collective-permute-start = (f32[8,3,16,256]{3,2,1,0:T(8,128)S(1)}, f32[8,3,16,256]{3,2,1,0:T(8,128)S(1)}, u32[]{:S(2)}, u32[]{:S(2)}) collective-permute-start(f32[8,3,16,256]{3,2,1,0:T(8,128)S(1)} %get-tuple-element.18), channel_id=1, source_target_pairs={{0,8},{8,0},{16,24},{24,16},{1,9},{9,1},{17,25},{25,17},{2,10},{10... | collective-permute-start | bytes 1179656 | tf_op jit(solution)/shard_map/ppermute | solution.py:621
  13.5 0.7 %collective-permute-start.1 = (f32[2,3,16,256]{3,2,1,0:T(8,128)S(1)}, f32[2,3,16,256]{3,2,1,0:T(8,128)S(1)}, u32[]{:S(2)}, u32[]{:S(2)}) collective-permute-start(f32[2,3,16,256]{3,2,1,0:T(8,128)S(1)} %get-tuple-element.19), channel_id=1, source_target_pairs={{8,16},{16,8},{9,17},{17,9},{10,18},{18,10},{11,19},{19,11},{12,20... | collective-permute-start | bytes 294920 | tf_op jit(solution)/shard_map/ppermute | solution.py:649
  14.1 0.0 copy-done.11
  14.2 0.0 copy-done.12
  14.2 0.1 compare_convert_fusion.1.hit_ref
  14.2 0.0 copy-done.14
  14.2 0.0 copy-done.15
  14.2 0.0 copy-done.13
  14.3 0.0 copy-done.1
  14.3 0.7 %rest_pressure.1 = (f32[16,128]{1,0:T(8,128)S(1)}, f32[3,200,128]{2,1,0:T(8,128)S(1)}) custom-call(f32[1,200,128]{2,1,0:T(8,128)S(1)} %copy-done.1, f32[8,256]{1,0:T(8,128)S(1)} %select_maximum_fusion.packed_ref), custom_call_target="tpu_custom_call" | custom-call | flops 1000 | bytes 1000 | tf_op jit(solution)/shard_map/rest_pressure/pallas_call | solution.py:491
  15.0 0.0 copy-done.7
  15.0 0.0 copy-done.8
  15.0 0.0 copy-start
  15.0 0.0 copy-start.6
  15.0 0.0 copy-start.9
  15.0 12.7 %local_update.1.part_ref = f32[8,64,16,256]{3,2,1,0:T(8,128)S(1)} custom-call(f32[2]{0:T(128)S(1)} %copy-done.10, f32[8,64,16,256]{3,2,1,0:T(8,128)} %state_hbm.3, f32[2,8,8]{2,1,0:T(8,128)S(1)} %copy-done.4, f32[128,8]{1,0:T(8,128)S(1)} %copy-done.3, f32[128,128]{1,0:T(8,128)S(1)} %copy-done.2, f32[128,128]{1,0:T(8,128)S(1)} %copy-done.8, ...), custom_call_target="tpu_custom_call" | custom-call | flops 1000 | bytes 1000 | tf_op jit(solution)/shard_map/local_update/pallas_call | solution.py:354
  27.7 0.0 collective-permute-done.1.far_ref.refs_1_
  27.7 0.0 collective-permute-done.near_ref.refs_0_
  27.8 0.0 collective-permute-done.3.cross_ref.refs_4_
  27.8 0.0 collective-permute-done.2.same_ref.refs_3_
  27.8 0.0 copy-done
  27.8 2.4 %tile_sums.1 = f32[32,384]{1,0:T(8,128)S(1)} custom-call(s32[3]{0:T(128)S(1)} %get-tuple-element.16.ids_ref, f32[8,64,16,256]{3,2,1,0:T(8,128)S(1)} %local_update.1.part_ref, f32[64,16,256]{2,1,0:T(8,128)S(1)} %copy-done, f32[64,24,256]{2,1,0:T(8,128)S(1)} %collective-permute-done.2.same_ref.refs_3_, ...), custom_call_target="tpu_custom_call" | custom-call | flops 1000 | bytes 1000 | tf_op jit(solution)/shard_map/tile_sums/pallas_call | solution.py:448
  30.2 1.5 %collective-permute-start.8 = (f32[32,384]{1,0:T(8,128)S(1)}, f32[32,384]{1,0:T(8,128)S(1)}, u32[]{:S(2)}, u32[]{:S(2)}) collective-permute-start(f32[32,384]{1,0:T(8,128)S(1)} %tile_sums.1), channel_id=1, source_target_pairs={{0,24},{8,16},{16,8},{24,0},{1,25},{9,17},{17,9},{25,1},{2,26},{10... | collective-permute-start | bytes 147464 | tf_op jit(solution)/shard_map/ppermute | solution.py:621
  31.7 4.2 %collective-permute-start.7 = (f32[32,384]{1,0:T(8,128)S(1)}, f32[32,384]{1,0:T(8,128)S(1)}, u32[]{:S(2)}, u32[]{:S(2)}) collective-permute-start(f32[32,384]{1,0:T(8,128)S(1)} %tile_sums.1), channel_id=1, source_target_pairs={{0,16},{8,24},{16,0},{24,8},{1,17},{9,25},{17,1},{25,9},{2,18},{10... | collective-permute-start | bytes 147464 | tf_op jit(solution)/shard_map/ppermute | solution.py:621
  35.8 0.0 collective-permute-start.6
  35.8 0.7 %collective-permute-start.4 = (f32[6,3,16,256]{3,2,1,0:T(8,128)S(1)}, f32[6,3,16,256]{3,2,1,0:T(8,128)S(1)}, u32[]{:S(2)}, u32[]{:S(2)}) collective-permute-start(f32[6,3,16,256]{3,2,1,0:T(8,128)S(1)} %get-tuple-element.24), channel_id=1, source_target_pairs={{8,16},{16,8},{9,17},{17,9},{10,18},{18,10},{11,19},{19,11},{12,20... | collective-permute-start | bytes 884744 | tf_op jit(solution)/shard_map/ppermute | solution.py:671
  36.5 0.0 collective-permute-done.8
  36.5 2.8 %collective-permute-done.7 = f32[32,384]{1,0:T(8,128)S(1)} collective-permute-done((f32[32,384]{1,0:T(8,128)S(1)}, f32[32,384]{1,0:T(8,128)S(1)}, u32[]{:S(2)}, u32[]{:S(2)}) %collective-permute-start.7) | collective-permute-done | bytes 49184 | tf_op jit(solution)/shard_map/ppermute | solution.py:621
  39.4 1.2 %collective-permute-done.6 = f32[32,384]{1,0:T(8,128)S(1)} collective-permute-done((f32[32,384]{1,0:T(8,128)S(1)}, f32[32,384]{1,0:T(8,128)S(1)}, u32[]{:S(2)}, u32[]{:S(2)}) %collective-permute-start.6) | collective-permute-done | bytes 49184 | tf_op jit(solution)/shard_map/ppermute | solution.py:621
  40.5 0.1 collective-permute-start.9
  40.6 1.2 %collective-permute-done.9 = f32[32,384]{1,0:T(8,128)S(1)} collective-permute-done((f32[32,384]{1,0:T(8,128)S(1)}, f32[32,384]{1,0:T(8,128)S(1)}, u32[]{:S(2)}, u32[]{:S(2)}) %collective-permute-start.9) | collective-permute-done | bytes 49184 | tf_op jit(solution)/shard_map/ppermute | solution.py:621
  41.8 1.5 %collective-permute-start.12 = (f32[32,384]{1,0:T(8,128)S(1)}, f32[32,384]{1,0:T(8,128)S(1)}, u32[]{:S(2)}, u32[]{:S(2)}) collective-permute-start(f32[32,384]{1,0:T(8,128)S(1)} %add.30), channel_id=1, source_target_pairs={{0,6},{1,7},{2,4},{3,5},{4,2},{5,3},{6,0},{7,1},{8,14},{9,15},{10,... | collective-permute-start | bytes 147464 | tf_op jit(solution)/shard_map/ppermute | solution.py:621
  43.4 0.0 collective-permute-start.11
  43.4 2.9 %collective-permute-start.10 = (f32[32,384]{1,0:T(8,128)S(1)}, f32[32,384]{1,0:T(8,128)S(1)}, u32[]{:S(2)}, u32[]{:S(2)}) collective-permute-start(f32[32,384]{1,0:T(8,128)S(1)} %add.30), channel_id=1, source_target_pairs={{0,2},{1,3},{2,0},{3,1},{4,6},{5,7},{6,4},{7,5},{8,10},{9,11},{10,... | collective-permute-start | bytes 147464 | tf_op jit(solution)/shard_map/ppermute | solution.py:621
  46.3 0.1 compare_convert_fusion.refs_7_
  46.4 0.0 copy-start.5
  46.4 0.0 collective-permute-done.5.refs_5_
  46.4 0.0 collective-permute-done.4.refs_2_
  46.4 4.0 %finish_most.1.refs_6_ = f32[8,64,16,256]{3,2,1,0:T(8,128)} custom-call(s32[3]{0:T(128)S(1)} %get-tuple-element.16.ids_ref, f32[8,64,16,256]{3,2,1,0:T(8,128)S(1)} %local_update.1.part_ref, f32[8,3,16,256]{3,2,1,0:T(8,128)S(1)} %collective-permute-done.near_ref.refs_0_, f32[2,3,16,256]{3,2,1,0:T(8,128)S(1)} %collective-permute-done.1.far_ref.refs_1_, ...), custom_call_target="tpu_custom_call" | custom-call | flops 100000000 | bytes 16000000 | tf_op jit(solution)/shard_map/finish_most/pallas_call | solution.py:587
  50.4 0.0 collective-permute-done.12
  50.4 0.0 collective-permute-done.11
  50.4 0.0 collective-permute-done.10
  50.5 3.4 %finish_last.1 = (f32[8,64,16,256]{3,2,1,0:T(8,128)}, f32[1,200,128]{2,1,0:T(8,128)}) custom-call(s32[3]{0:T(128)S(1)} %get-tuple-element.16.ids_ref, f32[8,64,16,256]{3,2,1,0:T(8,128)S(1)} %local_update.1.part_ref, f32[8,3,16,256]{3,2,1,0:T(8,128)S(1)} %collective-permute-done.near_ref.refs_0_, ...), custom_call_target="tpu_custom_call", output_to_operand_aliasing={{0}: (8, {})} | custom-call | flops 1000 | bytes 1000 | tf_op jit(solution)/shard_map/finish_last/pallas_call | solution.py:602
  (7 shorter events, 0.1 us)
Async XLA Ops:
  0.6 9.8 %copy-start.2 = (f32[128,128]{1,0:T(8,128)S(1)}, f32[128,128]{1,0:T(8,128)}, u32[]{:S(2)}) copy-start(f32[128,128]{1,0:T(8,128)} %constant.31.clone.same_ref) | copy-start | bytes 196612
  0.6 9.7 %copy-start.3 = (f32[128,8]{1,0:T(8,128)S(1)}, f32[128,8]{1,0:T(8,128)}, u32[]{:S(2)}) copy-start(f32[128,8]{1,0:T(8,128)} %constant.30.clone.pick_ref) | copy-start | bytes 12292
  0.7 14.3 %copy-start.7 = (f32[128,128]{1,0:T(8,128)S(1)}, f32[128,128]{1,0:T(8,128)}, u32[]{:S(2)}) copy-start(f32[128,128]{1,0:T(8,128)} %constant.33.clone.gap_ref) | copy-start | bytes 196612
  0.7 14.3 %copy-start.8 = (f32[128,128]{1,0:T(8,128)S(1)}, f32[128,128]{1,0:T(8,128)}, u32[]{:S(2)}) copy-start(f32[128,128]{1,0:T(8,128)} %constant.32.clone.sum_ref) | copy-start | bytes 196612
  0.7 9.7 %copy-start.10 = (f32[2]{0:T(128)S(1)}, f32[2]{0:T(128)}, u32[]{:S(2)}) copy-start(f32[2]{0:T(128)} %speed_ref.3) | copy-start | bytes 28
  0.7 9.7 %copy-start.4 = (f32[2,8,8]{2,1,0:T(8,128)S(1)}, f32[2,8,8]{2,1,0:T(8,128)}, u32[]{:S(2)}) copy-start(f32[2,8,8]{2,1,0:T(8,128)} %matrix_ref.3) | copy-start | bytes 1540
  0.7 13.4 %copy-start.11 = (s32[32]{0:T(128)S(1)}, s32[32]{0:T(128)}, u32[]{:S(2)}) copy-start(s32[32]{0:T(128)} %param.25) | copy-start | bytes 388
  0.7 13.4 %copy-start.12 = (s32[1,64,1]{1,2,0:T(1,128)S(1)}, s32[1,64,1]{1,2,0:T(1,128)}, u32[]{:S(2)}) copy-start(s32[1,64,1]{1,2,0:T(1,128)} %param.24) | copy-start | bytes 772
  0.7 13.5 %copy-start.14 = (f32[200]{0:T(256)S(1)}, f32[200]{0:T(256)}, u32[]{:S(2)}) copy-start(f32[200]{0:T(256)} %param.29) | copy-start | bytes 2404
  0.7 13.5 %copy-start.15 = (f32[200]{0:T(256)S(1)}, f32[200]{0:T(256)}, u32[]{:S(2)}) copy-start(f32[200]{0:T(256)} %param.28) | copy-start | bytes 2404
  0.7 13.5 %copy-start.13 = (f32[2,200]{1,0:T(2,128)S(1)}, f32[2,200]{1,0:T(2,128)}, u32[]{:S(2)}) copy-start(f32[2,200]{1,0:T(2,128)} %param.27) | copy-start | bytes 4804
  0.8 13.5 %copy-start.1 = (f32[1,200,128]{2,1,0:T(8,128)S(1)}, f32[1,200,128]{2,1,0:T(8,128)}, u32[]{:S(2)}) copy-start(f32[1,200,128]{2,1,0:T(8,128)} %refs_12_.1) | copy-start | bytes 307204
  5.1 22.6 %collective-permute-start.2 = (f32[64,24,256]{2,1,0:T(8,128)S(1)}, f32[64,24,256]{2,1,0:T(8,128)S(1)}, u32[]{:S(2)}, u32[]{:S(2)}) collective-permute-start(f32[64,24,256]{2,1,0:T(8,128)S(1)} %get-tuple-element.21), channel_id=1, source_target_pairs={{0,1},{1,0},{2,3},{3,2},{4,5},{5,4},{6,7},{7,6},{8,9},{9,8},{10,11... | collective-permute-start | bytes 4718600 | tf_op jit(solution)/shard_map/ppermute | solution.py:621
  5.6 22.1 %collective-permute-start.3 = (f32[64,8,256]{2,1,0:T(8,128)S(1)}, f32[64,8,256]{2,1,0:T(8,128)S(1)}, u32[]{:S(2)}, u32[]{:S(2)}) collective-permute-start(f32[64,8,256]{2,1,0:T(8,128)S(1)} %get-tuple-element.22), channel_id=1, source_target_pairs={{0,7},{1,2},{2,1},{3,4},{4,3},{5,6},{6,5},{7,0},{8,15},{9,10},{10,... | collective-permute-start | bytes 1572872 | tf_op jit(solution)/shard_map/ppermute | solution.py:644
  10.3 36.0 %collective-permute-start.5 = (f32[64,16,256]{2,1,0:T(8,128)S(1)}, f32[64,16,256]{2,1,0:T(8,128)S(1)}, u32[]{:S(2)}, u32[]{:S(2)}) collective-permute-start(f32[64,16,256]{2,1,0:T(8,128)S(1)} %get-tuple-element.25), channel_id=1, source_target_pairs={{0,7},{1,2},{2,1},{3,4},{4,3},{5,6},{6,5},{7,0},{8,15},{9,10},{10,... | collective-permute-start | bytes 3145736 | tf_op jit(solution)/shard_map/ppermute | solution.py:646
  11.9 15.8 %collective-permute-start = (f32[8,3,16,256]{3,2,1,0:T(8,128)S(1)}, f32[8,3,16,256]{3,2,1,0:T(8,128)S(1)}, u32[]{:S(2)}, u32[]{:S(2)}) collective-permute-start(f32[8,3,16,256]{3,2,1,0:T(8,128)S(1)} %get-tuple-element.18), channel_id=1, source_target_pairs={{0,8},{8,0},{16,24},{24,16},{1,9},{9,1},{17,25},{25,17},{2,10},{10... | collective-permute-start | bytes 1179656 | tf_op jit(solution)/shard_map/ppermute | solution.py:621
  13.5 14.3 %collective-permute-start.1 = (f32[2,3,16,256]{3,2,1,0:T(8,128)S(1)}, f32[2,3,16,256]{3,2,1,0:T(8,128)S(1)}, u32[]{:S(2)}, u32[]{:S(2)}) collective-permute-start(f32[2,3,16,256]{3,2,1,0:T(8,128)S(1)} %get-tuple-element.19), channel_id=1, source_target_pairs={{8,16},{16,8},{9,17},{17,9},{10,18},{18,10},{11,19},{19,11},{12,20... | collective-permute-start | bytes 294920 | tf_op jit(solution)/shard_map/ppermute | solution.py:649
  15.0 12.8 %copy-start = (f32[64,16,256]{2,1,0:T(8,128)S(1)}, f32[64,16,256]{2,1,0:T(8,128)}, u32[]{:S(2)}) copy-start(f32[64,16,256]{2,1,0:T(8,128)} %vol_ref.1) | copy-start | bytes 3145732
  15.0 12.8 %copy-start.6 = (bf16[256,128]{1,0:T(8,128)(2,1)S(1)}, bf16[256,128]{1,0:T(8,128)(2,1)}, u32[]{:S(2)}) copy-start(bf16[256,128]{1,0:T(8,128)(2,1)} %constant.34.clone.seg_ref) | copy-start | bytes 196612
  15.0 12.8 %copy-start.9 = (f32[16,128]{1,0:T(8,128)S(1)}, f32[16,128]{1,0:T(8,128)}, u32[]{:S(2)}) copy-start(f32[16,128]{1,0:T(8,128)} %constant.35.clone.spot_ref.refs_10_) | copy-start | bytes 24580
  30.2 6.3 %collective-permute-start.8 = (f32[32,384]{1,0:T(8,128)S(1)}, f32[32,384]{1,0:T(8,128)S(1)}, u32[]{:S(2)}, u32[]{:S(2)}) collective-permute-start(f32[32,384]{1,0:T(8,128)S(1)} %tile_sums.1), channel_id=1, source_target_pairs={{0,24},{8,16},{16,8},{24,0},{1,25},{9,17},{17,9},{25,1},{2,26},{10... | collective-permute-start | bytes 147464 | tf_op jit(solution)/shard_map/ppermute | solution.py:621
  31.7 7.7 %collective-permute-start.7 = (f32[32,384]{1,0:T(8,128)S(1)}, f32[32,384]{1,0:T(8,128)S(1)}, u32[]{:S(2)}, u32[]{:S(2)}) collective-permute-start(f32[32,384]{1,0:T(8,128)S(1)} %tile_sums.1), channel_id=1, source_target_pairs={{0,16},{8,24},{16,0},{24,8},{1,17},{9,25},{17,1},{25,9},{2,18},{10... | collective-permute-start | bytes 147464 | tf_op jit(solution)/shard_map/ppermute | solution.py:621
  35.8 4.7 %collective-permute-start.6 = (f32[32,384]{1,0:T(8,128)S(1)}, f32[32,384]{1,0:T(8,128)S(1)}, u32[]{:S(2)}, u32[]{:S(2)}) collective-permute-start(f32[32,384]{1,0:T(8,128)S(1)} %tile_sums.1), channel_id=1, source_target_pairs={{0,8},{8,0},{16,24},{24,16},{1,9},{9,1},{17,25},{25,17},{2,10},{10... | collective-permute-start | bytes 147464 | tf_op jit(solution)/shard_map/ppermute | solution.py:621
  35.8 10.6 %collective-permute-start.4 = (f32[6,3,16,256]{3,2,1,0:T(8,128)S(1)}, f32[6,3,16,256]{3,2,1,0:T(8,128)S(1)}, u32[]{:S(2)}, u32[]{:S(2)}) collective-permute-start(f32[6,3,16,256]{3,2,1,0:T(8,128)S(1)} %get-tuple-element.24), channel_id=1, source_target_pairs={{8,16},{16,8},{9,17},{17,9},{10,18},{18,10},{11,19},{19,11},{12,20... | collective-permute-start | bytes 884744 | tf_op jit(solution)/shard_map/ppermute | solution.py:671
  40.5 1.3 %collective-permute-start.9 = (f32[32,384]{1,0:T(8,128)S(1)}, f32[32,384]{1,0:T(8,128)S(1)}, u32[]{:S(2)}, u32[]{:S(2)}) collective-permute-start(f32[32,384]{1,0:T(8,128)S(1)} %add_add_fusion.1), channel_id=1, source_target_pairs={{0,1},{1,0},{2,3},{3,2},{4,5},{5,4},{6,7},{7,6},{8,9},{9,8},{10,11... | collective-permute-start | bytes 147464 | tf_op jit(solution)/shard_map/ppermute | solution.py:621
  41.8 8.5 %collective-permute-start.12 = (f32[32,384]{1,0:T(8,128)S(1)}, f32[32,384]{1,0:T(8,128)S(1)}, u32[]{:S(2)}, u32[]{:S(2)}) collective-permute-start(f32[32,384]{1,0:T(8,128)S(1)} %add.30), channel_id=1, source_target_pairs={{0,6},{1,7},{2,4},{3,5},{4,2},{5,3},{6,0},{7,1},{8,14},{9,15},{10,... | collective-permute-start | bytes 147464 | tf_op jit(solution)/shard_map/ppermute | solution.py:621
  43.4 7.0 %collective-permute-start.11 = (f32[32,384]{1,0:T(8,128)S(1)}, f32[32,384]{1,0:T(8,128)S(1)}, u32[]{:S(2)}, u32[]{:S(2)}) collective-permute-start(f32[32,384]{1,0:T(8,128)S(1)} %add.30), channel_id=1, source_target_pairs={{0,4},{1,5},{2,6},{3,7},{4,0},{5,1},{6,2},{7,3},{8,12},{9,13},{10,... | collective-permute-start | bytes 147464 | tf_op jit(solution)/shard_map/ppermute | solution.py:621
  43.4 7.1 %collective-permute-start.10 = (f32[32,384]{1,0:T(8,128)S(1)}, f32[32,384]{1,0:T(8,128)S(1)}, u32[]{:S(2)}, u32[]{:S(2)}) collective-permute-start(f32[32,384]{1,0:T(8,128)S(1)} %add.30), channel_id=1, source_target_pairs={{0,2},{1,3},{2,0},{3,1},{4,6},{5,7},{6,4},{7,5},{8,10},{9,11},{10,... | collective-permute-start | bytes 147464 | tf_op jit(solution)/shard_map/ppermute | solution.py:621
  46.4 4.1 %copy-start.5 = (bf16[128,256]{1,0:T(8,128)(2,1)S(1)}, bf16[128,256]{1,0:T(8,128)(2,1)}, u32[]{:S(2)}) copy-start(bf16[128,256]{1,0:T(8,128)(2,1)} %constant.36.clone.refs_11_) | copy-start | bytes 196612

commit v2 on v1

--- a/solution.py
+++ b/solution.py
@@ -75,12 +75,10 @@
 SMEM = pl.BlockSpec(memory_space=pltpu.SMEM)
 VMEM = pl.BlockSpec(memory_space=pltpu.VMEM)
 HBM = pl.BlockSpec(memory_space=pltpu.HBM)
-LARGE = pltpu.CompilerParams(vmem_limit_bytes=18 * 2**20)
-SMALL = pltpu.CompilerParams(vmem_limit_bytes=4 * 2**20)
+LARGE = pltpu.CompilerParams(vmem_limit_bytes=12 * 2**20)
+SMALL = pltpu.CompilerParams(vmem_limit_bytes=5 * 2**20)
 CHUNK = 8
 AHEAD = 3
-GROUP = 4
-RING = 4
 
 
 def in_vmem(*shape):
@@ -199,7 +197,7 @@
     return pick, same
 
 
-def rad_edge_kernel(ids_ref, speed_ref, rim_ref, matrix_ref, pick_ref, same_ref, near, far_a, far_b):
+def rad_edge_kernel(ids_ref, speed_ref, rim_ref, matrix_ref, pick_ref, same_ref, near_a, near_b, far_ref):
     fields, _, cols, depth = rim_ref.shape
     rate = (0.5 * courant_step) * speed_ref[0]
     even = ids_ref[1] % 2 == 0
@@ -223,11 +221,11 @@
             SUM_TAPS[j + REACH - t] * first_turned[j] + (rate * GAP_TAPS[j + REACH - t]) * first[j]
             for j in range(t + 1)
         )
-        near[:, t] = jnp.where(even, up, down)
-        far = jnp.where(even, down, up)
-        far_a[0, t] = far[0]
-        far_a[1, t] = far[fields - 1]
-        far_b[:, t] = far[1 : fields - 1]
+        near = jnp.where(even, up, down)
+        near_a[0, t] = near[0]
+        near_a[1, t] = near[fields - 1]
+        near_b[:, t] = near[1 : fields - 1]
+        far_ref[:, t] = jnp.where(even, down, up)
 
 
 def rad_edges(ids, rim, matrices, speed):
@@ -237,7 +235,7 @@
         rad_edge_kernel,
         in_specs=[SMEM] * 2 + [VMEM] * (2 + len(tables)),
         out_specs=[VMEM] * 3,
-        out_shape=[in_vmem(n, REACH, cols, depth) for n in (fields, 2, fields - 2)],
+        out_shape=[in_vmem(n, REACH, cols, depth) for n in (2, fields - 2, fields)],
         compiler_params=LARGE,
         cost_estimate=cost(1e3, 1e3),
         name="rad_edges",
@@ -262,13 +260,30 @@
                     total[f, first + j, pl.ds(8 * half, 8), lanes] = value
 
 
-def local_kernel(speed_ref, state_hbm, matrix_ref, pick_ref, same_ref, sum_ref, gap_ref, total, cells, w_ref, sem, *scratch):
+def add_radial(speed_ref, cells, turned, total, fields, first):
+    cols, depth = total.shape[2:]
+    rate = (0.5 * courant_step) * speed_ref[0]
+    for f in fields:
+        for half in range(cols // 8):
+            for lane in range(depth // 128):
+                lanes, subs = pl.ds(128 * lane, 128), pl.ds(8 * half, 8)
+                u = [cells[f, first + j, subs, lanes] for j in range(CHUNK + 2 * REACH)]
+                v = [turned[first + j, pl.ds(f * cols + 8 * half, 8), lanes] for j in range(CHUNK + 2 * REACH)]
+                for j in range(CHUNK):
+                    at = j + REACH
+                    value = total[f, first + j, subs, lanes] + (rate * GAP_TAPS[0]) * u[at]
+                    for k in range(1, REACH + 1):
+                        value = value + (SUM_TAPS[k] / SUM_TAPS[1]) * (v[at + k] - v[at - k])
+                        value = value + (rate * GAP_TAPS[k]) * (u[at + k] + u[at - k])
+                    total[f, first + j, subs, lanes] = value
+
+
+def local_kernel(
+    speed_ref, state_hbm, matrix_ref, pick_ref, same_ref, sum_ref, gap_ref, total, turned, cells, w_ref, sem
+):
     fields, rows, cols, depth = total.shape
+    chunks = rows // CHUNK
     size = fields * cols
-    turned, base = scratch[:RING], scratch[RING:]
-    rate = (0.5 * courant_step) * speed_ref[0]
-    last_row = cells.shape[1] - 1
-    chunks = rows // CHUNK
 
     def load(c):
         return pltpu.make_async_copy(
@@ -277,73 +292,37 @@
 
     for c in range(AHEAD):
         load(c).start()
-    w_ref[...] = local_weights(
-        matrix_ref, speed_ref, pick_ref[...], same_ref[...], sum_ref[...], gap_ref[...]
-    )
+    pick = pick_ref[...]
+    own = lon_weights(matrix_ref[1], speed_ref[1], pick, pick.T, sum_ref[...], gap_ref[...])
+    turn = SUM_TAPS[1] * turn_weights(matrix_ref[0], pick, same_ref[...])
+    high, low = parts_of(jnp.concatenate([own, turn], axis=0), 2)
+    w_ref[...] = jnp.concatenate([high, high, low], axis=1)
     for edge in (0, REACH + rows):
         cells[:, edge : edge + REACH] = jnp.zeros((fields, REACH, cols, depth), f32)
-
-    def multiply(c, slot, j):
-        r = jnp.minimum(REACH + c * GROUP + j, last_row)
-        here = cells[:, r].reshape(size, depth)
-        high, low = parts_of(here, 2)
-        both = dot(w_ref[...], jnp.concatenate([high, low, high], axis=0))
-        base[slot][j] = here + both[:size]
-        turned[slot][j] = both[size:]
-
-    def radial(c, slot, quarter):
-        first = c * GROUP
-        groups = fields * (cols // 8) * (depth // 128)
-        for g in range(quarter * groups // GROUP, (quarter + 1) * groups // GROUP):
-            f, rest = divmod(g, (cols // 8) * (depth // 128))
-            half, lane = divmod(rest, depth // 128)
-            lanes = pl.ds(128 * lane, 128)
-            u = [cells[f, first + j, pl.ds(8 * half, 8), lanes] for j in range(GROUP + 2 * REACH)]
-            v = []
-            for j in range(-REACH, GROUP + REACH):
-                ref = turned[(slot + j // GROUP) % RING]
-                v.append(ref[j % GROUP, pl.ds(f * cols + 8 * half, 8), lanes])
-            for j in range(GROUP):
-                at = j + REACH
-                value = base[slot][j, pl.ds(f * cols + 8 * half, 8), lanes] + (rate * GAP_TAPS[0]) * u[at]
-                for k in range(1, REACH + 1):
-                    value = value + SUM_TAPS[k] * (v[at + k] - v[at - k])
-                    value = value + (rate * GAP_TAPS[k]) * (u[at + k] + u[at - k])
-                total[f, first + j, pl.ds(8 * half, 8), lanes] = value
-
-    turned[RING - 1][...] = jnp.zeros((GROUP, size, depth), f32)
-    load(0).wait()
-    load(AHEAD).start()
-    for c in range(2):
-        for j in range(GROUP):
-            multiply(c, c, j)
-
-    ahead = GROUP * RING // CHUNK
-
-    def step(i, carry):
-        for c in range(1, ahead + 1):
-
-            @pl.when(ahead * i + c < chunks)
-            def _():
-                load(ahead * i + c).wait()
-
-            @pl.when(ahead * i + c + AHEAD < chunks)
-            def _():
-                load(ahead * i + c + AHEAD).start()
-
-        for q in range(RING):
-            for j in range(GROUP):
-                multiply(RING * i + q + 2, (q + 2) % RING, j)
-                radial(RING * i + q, q, j)
+        turned[edge : edge + REACH] = jnp.zeros((REACH, size, depth), f32)
+
+    def rows_of(c, carry):
+        load(c).wait()
+
+        @pl.when(c + AHEAD < chunks)
+        def _():
+            load(c + AHEAD).start()
+
+        for j in range(CHUNK):
+            r = c * CHUNK + j
+            here = cells[:, REACH + r].reshape(size, depth)
+            high, low = parts_of(here, 2)
+            both = dot(w_ref[...], jnp.concatenate([high, low, high], axis=0))
+            total[:, r] = (here + both[:size]).reshape(fields, cols, depth)
+            turned[REACH + r] = both[size:]
         return carry
 
-    lax.fori_loop(0, rows // (GROUP * RING), step, 0)
-
-
-def local_weights(matrices, speed_ref, pick, same, summed, gapped):
-    own = lon_weights(matrices[1], speed_ref[1], pick, pick.T, summed, gapped)
-    high, low = parts_of(jnp.concatenate([own, turn_weights(matrices[0], pick, same)], axis=0), 2)
-    return jnp.concatenate([high, high, low], axis=1)
+    def radial(c, carry):
+        add_radial(speed_ref, cells, turned, total, (0, fields - 1), c * CHUNK)
+        return carry
+
+    lax.fori_loop(0, chunks, rows_of, 0)
+    lax.fori_loop(0, chunks, radial, 0)
 
 
 def local_update(state, matrices, speed):
@@ -351,23 +330,40 @@
     size = fields * cols
     every = [(f, l) for f in range(fields) for l in range(cols)]
     _, _, summed, gapped = lon_tables(every, every)
+    padded = rows + 2 * REACH
     return pl.pallas_call(
         local_kernel,
         in_specs=[SMEM, HBM] + [VMEM] * 5,
-        out_specs=VMEM,
-        out_shape=in_vmem(fields, rows, cols, depth),
-        scratch_shapes=[
-            pltpu.VMEM((fields, rows + 2 * REACH, cols, depth), f32),
-            pltpu.VMEM((2 * size, 3 * size), bf16),
-            pltpu.SemaphoreType.DMA((rows // CHUNK,)),
-        ]
-        + [pltpu.VMEM((GROUP, size, depth), f32)] * (2 * RING),
-        compiler_params=LARGE,
+        out_specs=[VMEM] * 3,
+        out_shape=[in_vmem(*state.shape), in_vmem(padded, size, depth), in_vmem(fields, padded, cols, depth)],
+        scratch_shapes=[pltpu.VMEM((2 * size, 3 * size), bf16), pltpu.SemaphoreType.DMA((rows // CHUNK,))],
+        compiler_params=SMALL,
         cost_estimate=cost(1e3, 1e3),
         name="local_update",
     )(
         speed, pltpu.with_memory_space_constraint(state, pltpu.HBM), matrices, *turn_tables(fields, cols), summed, gapped
     )
+
+
+def radial_kernel(fields, speed_ref, cells, turned, _, total):
+    def radial(c, carry):
+        add_radial(speed_ref, cells, turned, total, fields, c * CHUNK)
+        return carry
+
+    lax.fori_loop(0, total.shape[1] // CHUNK, radial, 0)
+
+
+def radial_update(fields, cells, turned, part, speed):
+    return pl.pallas_call(
+        functools.partial(radial_kernel, fields),
+        in_specs=[SMEM] + [VMEM] * 3,
+        out_specs=VMEM,
+        out_shape=in_vmem(*part.shape),
+        input_output_aliases={3: 0},
+        compiler_params=SMALL,
+        cost_estimate=cost(1e8, 6e6),
+        name="radial_update",
+    )(speed, pinned(cells), pinned(turned), pinned(part))
 
 
 def placed(tiles, field, from_left):
@@ -428,7 +424,7 @@
         vol = vol_ref[here]
         for c, field in enumerate((0, 7)):
             cells = with_sides(part_ref[field, here], lefts, rights, field)
-            cells = with_ends(cells, step, steps, ids_ref[1], near_ref[field], far_ref[c])
+            cells = with_ends(cells, step, steps, ids_ref[1], near_ref[c], far_ref[field])
             lines = exact_dot((cells * vol).reshape(rows * cols, depth), seg_ref[...])
             lines_ref[c, here] = jnp.sum(lines.reshape(rows, cols, -1) * spot_ref[...][None], axis=1)
         return carry
@@ -508,11 +504,11 @@
     return pressure
 
 
-def finish_field(field, refs, part_ref, done, step_of=None):
-    ids_ref, near_ref, far_a, far_b, same_ref, *cross_refs = refs
-    rows = CHUNK
-    steps = done.shape[1] // rows
-    last_field = near_ref.shape[0] - 1
+def finish_field(field, refs, part_ref, out):
+    ids_ref, near_a, near_b, far_ref, same_ref, *cross_refs = refs
+    rows = 2 * CHUNK
+    steps = out.shape[0] // rows
+    last_field = far_ref.shape[0] - 1
 
     def step(i, carry):
         here = pl.ds(pl.multiple_of(i * rows, rows), rows)
@@ -522,50 +518,51 @@
             cross = cross_refs[0][here] if t == 0 else cross_refs[1][here, 8 * t - 8 : 8 * t]
             one = by_side(ids_ref[0], same_ref[here, 8 * t : 8 * t + 8], [cross])
             lefts[t], rights[t] = one[0][0], one[1][0]
-        far = far_a[field // last_field] if field in (0, last_field) else far_b[field - 1]
+        near = near_a[field // last_field] if field in (0, last_field) else near_b[field - 1]
         cells = with_sides(part_ref[field, here], lefts, rights, field)
-        cells = with_ends(cells, i, steps, ids_ref[1], near_ref[field], far)
-        done[min(field, done.shape[0] - 1), here] = cells if step_of is None else step_of(here, cells)
+        out[here] = with_ends(cells, i, steps, ids_ref[1], near, far_ref[field])
         return carry
 
     lax.fori_loop(0, steps, step, 0)
 
 
 def most_kernel(ids_ref, part_ref, *refs):
-    *sides, out_hbm, done, sem = refs
+    *sides, out_hbm, last_ref, done, sem = refs
     copies = []
     for field in range(done.shape[0]):
-        finish_field(field, (ids_ref, *sides), part_ref, done)
+        finish_field(field, (ids_ref, *sides), part_ref, done.at[field])
         copies.append(pltpu.make_async_copy(done.at[field], out_hbm.at[field], sem.at[field]))
         copies[-1].start()
+    finish_field(done.shape[0], (ids_ref, *sides), part_ref, last_ref)
     for copy in copies:
         copy.wait()
 
 
-def last_kernel(ids_ref, part_ref, *refs):
-    *sides, _, hit_ref, sums_ref, rest_ref, spot_ref, seg_ref, density_ref, spread_ref = refs[:-6]
-    out_hbm, drifted_hbm, done, back_ref, moved, sem = refs[-6:]
+def last_kernel(
+    ids_ref, cells_ref, _, hit_ref, sums_ref, rest_ref, spot_ref, seg_ref, density_ref, spread_ref,
+    out_hbm, drifted_hbm, done, back_ref, moved, sem,
+):
     points = spot_ref.shape[1]
-    _, _, cols, depth = done.shape
-    last = part_ref.shape[0] - 1
-
+    rows, cols, depth = done.shape
+    last = out_hbm.shape[0] - 1
+    back_ref[...] = sum(dot(hit_ref[...], p) for p in parts_of(pressures_of(sums_ref[...], rest_ref), 3))
+    copies = []
+    size = 2 * CHUNK
+    for first in range(0, rows, size):
+        here = pl.ds(first, size)
+        spread = (back_ref[here][:, None, :] * spot_ref[...][None]).reshape(-1, points)
+        returned = exact_dot(spread, seg_ref[...]).reshape(-1, cols, depth)
+        cells = cells_ref[here]
+        done[here] = cells + nudge_rate * (returned - cells)
+        copies.append(pltpu.make_async_copy(done.at[here], out_hbm.at[last, here], sem.at[len(copies)]))
+        copies[-1].start()
     source = sums_ref[pl.ds(ids_ref[2], 1), :]
     density = density_ref[0] + inner_step * (
         spread_ref[1] * source[:, :points] + spread_ref[2] * source[:, points : 2 * points]
     )
     moved[0] = drifted(density, spread_ref[0])
-    copies = [pltpu.make_async_copy(moved, drifted_hbm, sem.at[0])]
-    copies[0].start()
-    back_ref[...] = sum(dot(hit_ref[...], p) for p in parts_of(pressures_of(sums_ref[...], rest_ref), 3))
-
-    def nudged(here, cells):
-        spread = (back_ref[here][:, None, :] * spot_ref[...][None]).reshape(-1, points)
-        returned = exact_dot(spread, seg_ref[...]).reshape(-1, cols, depth)
-        return cells + nudge_rate * (returned - cells)
-
-    finish_field(last, (ids_ref, *sides), part_ref, done, nudged)
-    copies.append(pltpu.make_async_copy(done.at[0], out_hbm.at[last], sem.at[1]))
-    copies[1].start()
+    copies.append(pltpu.make_async_copy(moved, drifted_hbm, sem.at[len(copies)]))
+    copies[-1].start()
     for copy in copies:
         copy.wait()
 
@@ -587,8 +584,8 @@
     return pl.pallas_call(
         most_kernel,
         in_specs=[SMEM] + [VMEM] * len(pins),
-        out_specs=HBM,
-        out_shape=jax.ShapeDtypeStruct(part.shape, f32),
+        out_specs=[HBM, VMEM],
+        out_shape=[jax.ShapeDtypeStruct(part.shape, f32), in_vmem(rows, cols, depth)],
         scratch_shapes=[pltpu.VMEM((fields - 1, rows, cols, depth), f32), pltpu.SemaphoreType.DMA((fields - 1,))],
         compiler_params=LARGE,
         cost_estimate=cost(1e8, 1.6e7),
@@ -596,25 +593,24 @@
     )(ids, *pins)
 
 
-def finish_last(ids, part, rad, same, crosses, most, hits, sums, rest, spot, seg, density, spread):
-    fields, rows, cols, depth = part.shape
-    pins = [pinned(x) for x in (part, *rad, same, *crosses)]
+def finish_last(ids, cells, most, hits, sums, rest, spot, seg, density, spread):
+    rows, cols, depth = cells.shape
     return pl.pallas_call(
         last_kernel,
-        in_specs=[SMEM] + [VMEM] * len(pins) + [HBM] + [VMEM] * 7,
+        in_specs=[SMEM, VMEM, HBM] + [VMEM] * 7,
         out_specs=[HBM, HBM],
-        out_shape=[jax.ShapeDtypeStruct(part.shape, f32), jax.ShapeDtypeStruct(density.shape, f32)],
-        input_output_aliases={1 + len(pins): 0},
+        out_shape=[jax.ShapeDtypeStruct(most.shape, f32), jax.ShapeDtypeStruct(density.shape, f32)],
+        input_output_aliases={2: 0},
         scratch_shapes=[
-            pltpu.VMEM((1, rows, cols, depth), f32),
+            pltpu.VMEM(cells.shape, f32),
             pltpu.VMEM((rows, spot.shape[1]), f32),
             pltpu.VMEM(density.shape, f32),
-            pltpu.SemaphoreType.DMA((2,)),
+            pltpu.SemaphoreType.DMA((rows // (2 * CHUNK) + 1,)),
         ],
-        compiler_params=LARGE,
+        compiler_params=SMALL,
         cost_estimate=cost(1e3, 1e3),
         name="finish_last",
-    )(ids, *pins, most, hits, pinned(sums), pinned(rest), spot, seg, density, pinned(spread))
+    )(ids, pinned(cells), most, hits, pinned(sums), pinned(rest), spot, seg, density, pinned(spread))
 
 
 def swap(x, axis, bit):
@@ -645,15 +641,15 @@
     same = swap(same, "lon", 1)
     cross_1 = lax.ppermute(crosses[1], "lon", across)
 
-    near, far_a, far_b = rad_edges(ids, rim, flux_matrices, wave_speed)
-    far_a = lax.ppermute(far_a, "rad", beyond)
-    near = swap(near, "rad", 1)
+    near_a, near_b, far = rad_edges(ids, rim, flux_matrices, wave_speed)
+    near_a = swap(near_a, "rad", 1)
+    far = lax.ppermute(far, "rad", beyond)
 
     packed = jnp.concatenate([drift_courant[None], energy_weight[None], injection], axis=0)
     packed = jnp.pad(packed, ((0, 4), (0, -packed.shape[1] % 128)))
     rest, spread = rest_of(phase_density, packed)
 
-    part = local_update(state, flux_matrices, wave_speed)
+    part, turned, cells = local_update(state, flux_matrices, wave_speed)
 
     targets = block_tile[0, :, 0]
     hits = (tile_of_device[:, None] == targets[None, :]).astype(bf16)
@@ -662,23 +658,22 @@
     seg = np.array([[float(p % ZSEG == z // seg_cells) for p in range(points)] for z in range(depth)], np.float32)
     spot = np.array([[float(p // ZSEG == l) for p in range(points)] for l in range(cols)], np.float32)
     sums = tile_sums(
-        ids, part, flux_volume, same, cross_0, near, far_a, rest, hits, jnp.asarray(seg, bf16), jnp.asarray(spot)
-    )
-    def summed(sums, axis, steps):
-        return sum([swap(sums, axis, step) for step in steps], sums)
-
-    far_b, sums = lax.optimization_barrier((far_b, sums))
-    far_b = lax.ppermute(far_b, "rad", beyond)
-    sums = summed(sums, "rad", range(1, n_rad))
-    sums = summed(sums, "lon", [1])
+        ids, part, flux_volume, same, cross_0, near_a, far, rest, hits, jnp.asarray(seg, bf16), jnp.asarray(spot)
+    )
+    near_b, sums = lax.optimization_barrier((near_b, sums))
+    near_b = swap(near_b, "rad", 1)
+    part, sums = lax.optimization_barrier((part, sums))
+    others = [swap(sums, "rad", step) for step in range(1, n_rad)]
+    part = radial_update(tuple(range(1, fields - 1)), cells, turned, part, wave_speed)
+    part, sums = lax.optimization_barrier((part, sums))
+    sums = sum(others, sums)
+    sums = sums + swap(sums, "lon", 1)
     others = [swap(sums, "lon", step) for step in range(2, n_lon, 2)]
-    rad_sums = (near, far_a, far_b)
-    most = finish_most(ids, part, rad_sums, same, (cross_0, cross_1))
+    most, last = finish_most(ids, part, (near_a, near_b, far), same, (cross_0, cross_1))
     sums, most = lax.optimization_barrier((sums, most))
     sums = sum(others, sums)
     done, density = finish_last(
-        ids, part, rad_sums, same, (cross_0, cross_1), most, hits_back, sums, rest, jnp.asarray(spot),
-        jnp.asarray(seg.T, bf16), phase_density, spread,
+        ids, last, most, hits_back, sums, rest, jnp.asarray(spot), jnp.asarray(seg.T, bf16), phase_density, spread
     )
     return done, density
 

time: 54 us -> 51.2 us (0.948)
  waiting for transfers between devices: 5.24 us -> 2.39 us
    ppermute x9 -> x10, waiting for transfers between devices: 5.23 us -> 1.52 us  [swap(): lax.ppermute(x, axis, [(i, i ^ bit) for i in range(lax.axis_size(axis))])]
    pallas_call x1 -> x2, Pallas kernels: 3.43 us -> 6.71 us  [the longest x1 4.47 us: radial_update(): pl.pallas_call(functools.partial(radial_kernel, fields), in_specs=[SMEM]...]
    pallas_call x1, Pallas kernels: 12.7 us -> 9.55 us  [local_update(): pl.pallas_call(local_kernel, in_specs=[SMEM, HBM] + [VMEM] * 5, out_specs...]
    ppermute x1, waiting for transfers between devices: 0.01 us -> 0.87 us  [per_device(): cross_1 = lax.ppermute(crosses[1], 'lon', across)]
    ppermute x9 -> x10, starting transfers between devices: 12.3 us -> 12.9 us  [swap(): lax.ppermute(x, axis, [(i, i ^ bit) for i in range(lax.axis_size(axis))])]
    ppermute x2 -> x1, starting transfers between devices: 1.32 us -> 0.69 us  [per_device(): far = lax.ppermute(far, 'rad', beyond)]
  transfers between devices with their start and end apart: 13 -> 13, of which waited for: 3 -> 3; matrix products, arithmetic and copies ran while one was open for 0% -> 0% of each run, Pallas kernels for 39% -> 44%
where the time goes in v2:
time: 51.2 us; the launch traced here: 51 us
  Pallas kernels  29.1 us (57%)
  starting transfers between devices  18.3 us (36%)
  waiting for transfers between devices  2.39 us (5%)
  between operations  0.96 us (2%)
    ppermute x10, starting transfers between devices, swap(): lax.ppermute(x, axis, [(i, i ^ bit) for i in range(lax.axis_size(axis))])  12.9 us
    pallas_call x1, Pallas kernels, local_update(): pl.pallas_call(local_kernel, in_specs=[SMEM, HBM] + [VMEM] * 5, out_specs...  9.55 us
    ppermute x1, starting transfers between devices, per_device(): cross_0 = lax.ppermute(crosses[0], 'lon', across)  4.71 us
    pallas_call x1, Pallas kernels, radial_update(): pl.pallas_call(functools.partial(radial_kernel, fields), in_specs=[SMEM]...  4.47 us
    pallas_call x1, Pallas kernels, lon_edges(): pl.pallas_call(lon_edge_kernel, in_specs=[SMEM] * 3 + [HBM] * 4, out_spec...  4.36 us
    pallas_call x1, Pallas kernels, finish_most(): pl.pallas_call(most_kernel, in_specs=[SMEM] + [VMEM] * len(pins), out_spe...  3.82 us
    pallas_call x1, Pallas kernels, tile_sums(): pl.pallas_call(tile_sum_kernel, in_specs=[SMEM] + [VMEM] * 10, out_specs=...  2.39 us
    pallas_call x1, Pallas kernels, finish_last(): pl.pallas_call(last_kernel, in_specs=[SMEM, VMEM, HBM] + [VMEM] * 7, out_...  2.23 us
  transfers between devices with their start and end apart: 13, of which 3 were waited for; matrix products, arithmetic and copies ran while one was open for 0% of the time, Pallas kernels for 44%

profile of v2, /device:TPU:0, one launch (start us, length us, event | category | flops | bytes accessed | tf_op | source)
XLA Modules:
  0.0 51.0 jit_solution(11899951097466942040)
XLA Ops:
  0.6 0.0 copy-start.2
  0.6 0.0 copy-start.3
  0.7 0.0 copy-start.7
  0.7 0.0 copy-start.8
  0.7 0.0 copy-start.4
  0.7 0.0 copy-start.10
  0.7 0.0 copy-start.11
  0.7 0.0 copy-start.12
  0.7 0.0 copy-start.13
  0.7 0.0 copy-start.14
  0.8 0.0 copy-start.15
  0.8 0.0 copy-start.1
  0.8 0.0 copy-start
  0.8 0.0 copy-start.6
  0.8 0.0 copy-start.9
  0.8 4.4 %lon_edges.1 = (f32[8,6,16,256]{3,2,1,0:T(8,128)S(1)}, s32[3]{0:T(128)S(1)}, f32[64,24,256]{2,1,0:T(8,128)S(1)}, f32[64,8,256]{2,1,0:T(8,128)S(1)}, f32[64,16,256]{2,1,0:T(8,128)S(1)}) custom-call(s32[1]{0:T(128)} %bitcast.lon_ref, s32[1]{0:T(128)} %bitcast.1.rad_ref, s32[1]{0:T(128)} %bitcast.2.place_ref, f32[8,64,16,256]{3,2,1,0:T(8,128)} %state_hbm.3, ...), custom_call_target="tpu_custom_call" | custom-call | flops 1000 | bytes 1000 | tf_op jit(solution)/shard_map/lon_edges/pallas_call | solution.py:163
  5.2 0.5 %collective-permute-start = (f32[64,24,256]{2,1,0:T(8,128)S(1)}, f32[64,24,256]{2,1,0:T(8,128)S(1)}, u32[]{:S(2)}, u32[]{:S(2)}) collective-permute-start(f32[64,24,256]{2,1,0:T(8,128)S(1)} %get-tuple-element.31), channel_id=1, source_target_pairs={{0,1},{1,0},{2,3},{3,2},{4,5},{5,4},{6,7},{7,6},{8,9},{9,8},{10,11... | collective-permute-start | bytes 4718600 | tf_op jit(solution)/shard_map/ppermute | solution.py:617
  5.7 4.7 %collective-permute-start.1 = (f32[64,8,256]{2,1,0:T(8,128)S(1)}, f32[64,8,256]{2,1,0:T(8,128)S(1)}, u32[]{:S(2)}, u32[]{:S(2)}) collective-permute-start(f32[64,8,256]{2,1,0:T(8,128)S(1)} %get-tuple-element.32), channel_id=1, source_target_pairs={{0,7},{1,2},{2,1},{3,4},{4,3},{5,6},{6,5},{7,0},{8,15},{9,10},{10,... | collective-permute-start | bytes 1572872 | tf_op jit(solution)/shard_map/ppermute | solution.py:640
  10.4 0.0 collective-permute-start.5
  10.4 0.0 copy-done.2
  10.4 0.0 copy-done.3
  10.4 0.0 copy-done.4
  10.4 0.0 copy-done.10
  10.5 1.5 %rad_edges.1 = (f32[2,3,16,256]{3,2,1,0:T(8,128)S(1)}, f32[6,3,16,256]{3,2,1,0:T(8,128)S(1)}, f32[8,3,16,256]{3,2,1,0:T(8,128)S(1)}) custom-call(s32[3]{0:T(128)S(1)} %get-tuple-element.25.ids_ref, f32[2]{0:T(128)S(1)} %copy-done.10, f32[8,6,16,256]{3,2,1,0:T(8,128)S(1)} %get-tuple-element.29.rim_ref, f32[2,8,8]{2,1,0:T(8,128)S(1)} %copy-done.4, ...), custom_call_target="tpu_custom_call" | custom-call | flops 1000 | bytes 1000 | tf_op jit(solution)/shard_map/rad_edges/pallas_call | solution.py:234
  12.0 0.7 %collective-permute-start.3 = (f32[8,3,16,256]{3,2,1,0:T(8,128)S(1)}, f32[8,3,16,256]{3,2,1,0:T(8,128)S(1)}, u32[]{:S(2)}, u32[]{:S(2)}) collective-permute-start(f32[8,3,16,256]{3,2,1,0:T(8,128)S(1)} %get-tuple-element.34), channel_id=1, source_target_pairs={{8,16},{16,8},{9,17},{17,9},{10,18},{18,10},{11,19},{19,11},{12,20... | collective-permute-start | bytes 1179656 | tf_op jit(solution)/shard_map/ppermute | solution.py:646
  12.7 4.3 %collective-permute-start.2 = (f32[2,3,16,256]{3,2,1,0:T(8,128)S(1)}, f32[2,3,16,256]{3,2,1,0:T(8,128)S(1)}, u32[]{:S(2)}, u32[]{:S(2)}) collective-permute-start(f32[2,3,16,256]{3,2,1,0:T(8,128)S(1)} %get-tuple-element.33), channel_id=1, source_target_pairs={{0,8},{8,0},{16,24},{24,16},{1,9},{9,1},{17,25},{25,17},{2,10},{10... | collective-permute-start | bytes 294920 | tf_op jit(solution)/shard_map/ppermute | solution.py:617
  16.9 0.0 copy-done.7
  17.0 0.0 copy-done.8
  17.0 9.6 %local_update.1 = (f32[8,64,16,256]{3,2,1,0:T(8,128)S(1)}, f32[70,128,256]{2,1,0:T(8,128)S(1)}, f32[8,70,16,256]{3,2,1,0:T(8,128)S(1)}) custom-call(f32[2]{0:T(128)S(1)} %copy-done.10, f32[8,64,16,256]{3,2,1,0:T(8,128)} %state_hbm.3, f32[2,8,8]{2,1,0:T(8,128)S(1)} %copy-done.4, f32[128,8]{1,0:T(8,128)S(1)} %copy-done.2, f32[128,128]{1,0:T(8,128)S(1)} %copy-done.3, ...), custom_call_target="tpu_custom_call" | custom-call | flops 1000 | bytes 1000 | tf_op jit(solution)/shard_map/local_update/pallas_call | solution.py:334
  26.5 0.0 copy-done.11
  26.5 0.0 copy-done.12
  26.5 0.1 compare_convert_fusion.1.hit_ref
  26.7 0.7 %rest_pressure.1 = (f32[16,128]{1,0:T(8,128)S(1)}, f32[3,200,128]{2,1,0:T(8,128)S(1)}) custom-call(f32[1,200,128]{2,1,0:T(8,128)S(1)} %copy-done.1, f32[8,256]{1,0:T(8,128)S(1)} %select_maximum_fusion.packed_ref), custom_call_target="tpu_custom_call" | custom-call | flops 1000 | bytes 1000 | tf_op jit(solution)/shard_map/rest_pressure/pallas_call | solution.py:487
  27.4 0.0 collective-permute-done.2.near_ref.refs_0_
  27.4 0.0 collective-permute-done.3.far_ref.refs_2_
  27.4 0.0 collective-permute-done.1.cross_ref.refs_4_
  27.4 0.0 collective-permute-done.same_ref.refs_3_
  27.4 0.0 copy-done
  27.4 0.0 copy-done.6
  27.4 0.0 copy-done.9
  27.4 2.4 %tile_sums.1 = f32[32,384]{1,0:T(8,128)S(1)} custom-call(s32[3]{0:T(128)S(1)} %get-tuple-element.25.ids_ref, f32[8,64,16,256]{3,2,1,0:T(8,128)S(1)} %get-tuple-element.37.part_ref._, f32[64,16,256]{2,1,0:T(8,128)S(1)} %copy-done, f32[64,24,256]{2,1,0:T(8,128)S(1)} %collective-permute-done.same_ref.refs_3_, ...), custom_call_target="tpu_custom_call" | custom-call | flops 1000 | bytes 1000 | tf_op jit(solution)/shard_map/tile_sums/pallas_call | solution.py:444
  29.8 0.0 collective-permute-start.6
  29.9 2.0 %collective-permute-start.7 = (f32[32,384]{1,0:T(8,128)S(1)}, f32[32,384]{1,0:T(8,128)S(1)}, u32[]{:S(2)}, u32[]{:S(2)}) collective-permute-start(f32[32,384]{1,0:T(8,128)S(1)} %tile_sums.1), channel_id=1, source_target_pairs={{0,16},{8,24},{16,0},{24,8},{1,17},{9,25},{17,1},{25,9},{2,18},{10... | collective-permute-start | bytes 147464 | tf_op jit(solution)/shard_map/ppermute | solution.py:617
  31.8 1.5 %collective-permute-start.8 = (f32[32,384]{1,0:T(8,128)S(1)}, f32[32,384]{1,0:T(8,128)S(1)}, u32[]{:S(2)}, u32[]{:S(2)}) collective-permute-start(f32[32,384]{1,0:T(8,128)S(1)} %tile_sums.1), channel_id=1, source_target_pairs={{0,24},{8,16},{16,8},{24,0},{1,25},{9,17},{17,9},{25,1},{2,26},{10... | collective-permute-start | bytes 147464 | tf_op jit(solution)/shard_map/ppermute | solution.py:617
  33.3 4.5 %radial_update.1.part_ref = f32[8,64,16,256]{3,2,1,0:T(8,128)S(1)} custom-call(f32[2]{0:T(128)S(1)} %copy-done.10, f32[8,70,16,256]{3,2,1,0:T(8,128)S(1)} %get-tuple-element.26.cells, f32[70,128,256]{2,1,0:T(8,128)S(1)} %get-tuple-element.27.turned, f32[8,64,16,256]{3,2,1,0:T(8,128)S(1)} %get-tuple-element.37.part_ref._), custom_call_target="tpu_custom_call", output_to_operand_aliasing={{}: (3, {})} | custom-call | flops 100000000 | bytes 6000000 | tf_op jit(solution)/shard_map/radial_update/pallas_call | solution.py:357
  37.8 0.0 copy-start.5
  37.8 0.1 collective-permute-start.4
  37.9 0.0 collective-permute-done.6
  37.9 0.0 collective-permute-done.7
  37.9 0.0 collective-permute-done.8
  38.0 0.1 collective-permute-start.9
  38.0 1.2 %collective-permute-done.9 = f32[32,384]{1,0:T(8,128)S(1)} collective-permute-done((f32[32,384]{1,0:T(8,128)S(1)}, f32[32,384]{1,0:T(8,128)S(1)}, u32[]{:S(2)}, u32[]{:S(2)}) %collective-permute-start.9) | collective-permute-done | bytes 49184 | tf_op jit(solution)/shard_map/ppermute | solution.py:617
  39.3 0.7 %collective-permute-start.10 = (f32[32,384]{1,0:T(8,128)S(1)}, f32[32,384]{1,0:T(8,128)S(1)}, u32[]{:S(2)}, u32[]{:S(2)}) collective-permute-start(f32[32,384]{1,0:T(8,128)S(1)} %add.30), channel_id=1, source_target_pairs={{0,2},{1,3},{2,0},{3,1},{4,6},{5,7},{6,4},{7,5},{8,10},{9,11},{10,... | collective-permute-start | bytes 147464 | tf_op jit(solution)/shard_map/ppermute | solution.py:617
  40.0 2.0 %collective-permute-start.11 = (f32[32,384]{1,0:T(8,128)S(1)}, f32[32,384]{1,0:T(8,128)S(1)}, u32[]{:S(2)}, u32[]{:S(2)}) collective-permute-start(f32[32,384]{1,0:T(8,128)S(1)} %add.30), channel_id=1, source_target_pairs={{0,4},{1,5},{2,6},{3,7},{4,0},{5,1},{6,2},{7,3},{8,12},{9,13},{10,... | collective-permute-start | bytes 147464 | tf_op jit(solution)/shard_map/ppermute | solution.py:617
  42.0 1.7 %collective-permute-start.12 = (f32[32,384]{1,0:T(8,128)S(1)}, f32[32,384]{1,0:T(8,128)S(1)}, u32[]{:S(2)}, u32[]{:S(2)}) collective-permute-start(f32[32,384]{1,0:T(8,128)S(1)} %add.30), channel_id=1, source_target_pairs={{0,6},{1,7},{2,4},{3,5},{4,2},{5,3},{6,0},{7,1},{8,14},{9,15},{10,... | collective-permute-start | bytes 147464 | tf_op jit(solution)/shard_map/ppermute | solution.py:617
  43.7 0.1 compare_convert_fusion.hit_ref
  43.8 0.9 %collective-permute-done.5.refs_5_ = f32[64,16,256]{2,1,0:T(8,128)S(1)} collective-permute-done((f32[64,16,256]{2,1,0:T(8,128)S(1)}, f32[64,16,256]{2,1,0:T(8,128)S(1)}, u32[]{:S(2)}, u32[]{:S(2)}) %collective-permute-start.5) | collective-permute-done | bytes 1048608 | tf_op jit(solution)/shard_map/ppermute | solution.py:642
  44.7 0.0 collective-permute-done.4.refs_1_
  44.7 3.8 %finish_most.1 = (f32[8,64,16,256]{3,2,1,0:T(8,128)}, f32[64,16,256]{2,1,0:T(8,128)S(1)}) custom-call(s32[3]{0:T(128)S(1)} %get-tuple-element.25.ids_ref, f32[8,64,16,256]{3,2,1,0:T(8,128)S(1)} %radial_update.1.part_ref, f32[2,3,16,256]{3,2,1,0:T(8,128)S(1)} %collective-permute-done.2.near_ref.refs_0_, f32[6,3,16,256]{3,2,1,0:T(8,128)S(1)} %collective-permute-done.4.refs_1_, ...), custom_call_target="tpu_custom_call" | custom-call | flops 100000000 | bytes 16000000 | tf_op jit(solution)/shard_map/finish_most/pallas_call | solution.py:584
  48.5 0.0 collective-permute-done.10
  48.5 0.3 collective-permute-done.11
  48.8 0.0 collective-permute-done.12
  48.8 0.0 copy-done.5
  48.8 2.2 %finish_last.1 = (f32[8,64,16,256]{3,2,1,0:T(8,128)}, f32[1,200,128]{2,1,0:T(8,128)}) custom-call(s32[3]{0:T(128)S(1)} %get-tuple-element.25.ids_ref, f32[64,16,256]{2,1,0:T(8,128)S(1)} %get-tuple-element.42.cells_ref, f32[8,64,16,256]{3,2,1,0:T(8,128)} %get-tuple-element.45._, ...), custom_call_target="tpu_custom_call", output_to_operand_aliasing={{0}: (2, {})} | custom-call | flops 1000 | bytes 1000 | tf_op jit(solution)/shard_map/finish_last/pallas_call | solution.py:598
  (8 shorter events, 0.1 us)
Async XLA Ops:
  0.6 9.8 %copy-start.2 = (f32[128,8]{1,0:T(8,128)S(1)}, f32[128,8]{1,0:T(8,128)}, u32[]{:S(2)}) copy-start(f32[128,8]{1,0:T(8,128)} %constant.30.clone.pick_ref) | copy-start | bytes 12292
  0.6 9.8 %copy-start.3 = (f32[128,128]{1,0:T(8,128)S(1)}, f32[128,128]{1,0:T(8,128)}, u32[]{:S(2)}) copy-start(f32[128,128]{1,0:T(8,128)} %constant.31.clone.same_ref) | copy-start | bytes 196612
  0.7 16.3 %copy-start.7 = (f32[128,128]{1,0:T(8,128)S(1)}, f32[128,128]{1,0:T(8,128)}, u32[]{:S(2)}) copy-start(f32[128,128]{1,0:T(8,128)} %constant.32.clone.sum_ref) | copy-start | bytes 196612
  0.7 16.3 %copy-start.8 = (f32[128,128]{1,0:T(8,128)S(1)}, f32[128,128]{1,0:T(8,128)}, u32[]{:S(2)}) copy-start(f32[128,128]{1,0:T(8,128)} %constant.33.clone.gap_ref) | copy-start | bytes 196612
  0.7 9.8 %copy-start.4 = (f32[2,8,8]{2,1,0:T(8,128)S(1)}, f32[2,8,8]{2,1,0:T(8,128)}, u32[]{:S(2)}) copy-start(f32[2,8,8]{2,1,0:T(8,128)} %matrix_ref.3) | copy-start | bytes 1540
  0.7 9.8 %copy-start.10 = (f32[2]{0:T(128)S(1)}, f32[2]{0:T(128)}, u32[]{:S(2)}) copy-start(f32[2]{0:T(128)} %speed_ref.5) | copy-start | bytes 28
  0.7 25.8 %copy-start.11 = (s32[32]{0:T(128)S(1)}, s32[32]{0:T(128)}, u32[]{:S(2)}) copy-start(s32[32]{0:T(128)} %param.25) | copy-start | bytes 388
  0.7 25.8 %copy-start.12 = (s32[1,64,1]{1,2,0:T(1,128)S(1)}, s32[1,64,1]{1,2,0:T(1,128)}, u32[]{:S(2)}) copy-start(s32[1,64,1]{1,2,0:T(1,128)} %param.24) | copy-start | bytes 772
  0.7 25.9 %copy-start.13 = (f32[2,200]{1,0:T(2,128)S(1)}, f32[2,200]{1,0:T(2,128)}, u32[]{:S(2)}) copy-start(f32[2,200]{1,0:T(2,128)} %param.27) | copy-start | bytes 4804
  0.7 25.9 %copy-start.14 = (f32[200]{0:T(256)S(1)}, f32[200]{0:T(256)}, u32[]{:S(2)}) copy-start(f32[200]{0:T(256)} %param.29) | copy-start | bytes 2404
  0.8 25.9 %copy-start.15 = (f32[200]{0:T(256)S(1)}, f32[200]{0:T(256)}, u32[]{:S(2)}) copy-start(f32[200]{0:T(256)} %param.28) | copy-start | bytes 2404
  0.8 25.9 %copy-start.1 = (f32[1,200,128]{2,1,0:T(8,128)S(1)}, f32[1,200,128]{2,1,0:T(8,128)}, u32[]{:S(2)}) copy-start(f32[1,200,128]{2,1,0:T(8,128)} %density_ref.3) | copy-start | bytes 307204
  0.8 26.6 %copy-start = (f32[64,16,256]{2,1,0:T(8,128)S(1)}, f32[64,16,256]{2,1,0:T(8,128)}, u32[]{:S(2)}) copy-start(f32[64,16,256]{2,1,0:T(8,128)} %vol_ref.1) | copy-start | bytes 3145732
  0.8 26.6 %copy-start.6 = (bf16[256,128]{1,0:T(8,128)(2,1)S(1)}, bf16[256,128]{1,0:T(8,128)(2,1)}, u32[]{:S(2)}) copy-start(bf16[256,128]{1,0:T(8,128)(2,1)} %constant.34.clone.seg_ref) | copy-start | bytes 196612
  0.8 26.6 %copy-start.9 = (f32[16,128]{1,0:T(8,128)S(1)}, f32[16,128]{1,0:T(8,128)}, u32[]{:S(2)}) copy-start(f32[16,128]{1,0:T(8,128)} %constant.35.clone.spot_ref) | copy-start | bytes 24580
  5.2 22.2 %collective-permute-start = (f32[64,24,256]{2,1,0:T(8,128)S(1)}, f32[64,24,256]{2,1,0:T(8,128)S(1)}, u32[]{:S(2)}, u32[]{:S(2)}) collective-permute-start(f32[64,24,256]{2,1,0:T(8,128)S(1)} %get-tuple-element.31), channel_id=1, source_target_pairs={{0,1},{1,0},{2,3},{3,2},{4,5},{5,4},{6,7},{7,6},{8,9},{9,8},{10,11... | collective-permute-start | bytes 4718600 | tf_op jit(solution)/shard_map/ppermute | solution.py:617
  5.7 21.7 %collective-permute-start.1 = (f32[64,8,256]{2,1,0:T(8,128)S(1)}, f32[64,8,256]{2,1,0:T(8,128)S(1)}, u32[]{:S(2)}, u32[]{:S(2)}) collective-permute-start(f32[64,8,256]{2,1,0:T(8,128)S(1)} %get-tuple-element.32), channel_id=1, source_target_pairs={{0,7},{1,2},{2,1},{3,4},{4,3},{5,6},{6,5},{7,0},{8,15},{9,10},{10,... | collective-permute-start | bytes 1572872 | tf_op jit(solution)/shard_map/ppermute | solution.py:640
  10.4 34.2 %collective-permute-start.5 = (f32[64,16,256]{2,1,0:T(8,128)S(1)}, f32[64,16,256]{2,1,0:T(8,128)S(1)}, u32[]{:S(2)}, u32[]{:S(2)}) collective-permute-start(f32[64,16,256]{2,1,0:T(8,128)S(1)} %get-tuple-element.41), channel_id=1, source_target_pairs={{0,7},{1,2},{2,1},{3,4},{4,3},{5,6},{6,5},{7,0},{8,15},{9,10},{10,... | collective-permute-start | bytes 3145736 | tf_op jit(solution)/shard_map/ppermute | solution.py:642
  12.0 15.4 %collective-permute-start.3 = (f32[8,3,16,256]{3,2,1,0:T(8,128)S(1)}, f32[8,3,16,256]{3,2,1,0:T(8,128)S(1)}, u32[]{:S(2)}, u32[]{:S(2)}) collective-permute-start(f32[8,3,16,256]{3,2,1,0:T(8,128)S(1)} %get-tuple-element.34), channel_id=1, source_target_pairs={{8,16},{16,8},{9,17},{17,9},{10,18},{18,10},{11,19},{19,11},{12,20... | collective-permute-start | bytes 1179656 | tf_op jit(solution)/shard_map/ppermute | solution.py:646
  12.7 14.7 %collective-permute-start.2 = (f32[2,3,16,256]{3,2,1,0:T(8,128)S(1)}, f32[2,3,16,256]{3,2,1,0:T(8,128)S(1)}, u32[]{:S(2)}, u32[]{:S(2)}) collective-permute-start(f32[2,3,16,256]{3,2,1,0:T(8,128)S(1)} %get-tuple-element.33), channel_id=1, source_target_pairs={{0,8},{8,0},{16,24},{24,16},{1,9},{9,1},{17,25},{25,17},{2,10},{10... | collective-permute-start | bytes 294920 | tf_op jit(solution)/shard_map/ppermute | solution.py:617
  29.8 8.1 %collective-permute-start.6 = (f32[32,384]{1,0:T(8,128)S(1)}, f32[32,384]{1,0:T(8,128)S(1)}, u32[]{:S(2)}, u32[]{:S(2)}) collective-permute-start(f32[32,384]{1,0:T(8,128)S(1)} %tile_sums.1), channel_id=1, source_target_pairs={{0,8},{8,0},{16,24},{24,16},{1,9},{9,1},{17,25},{25,17},{2,10},{10... | collective-permute-start | bytes 147464 | tf_op jit(solution)/shard_map/ppermute | solution.py:617
  29.9 8.1 %collective-permute-start.7 = (f32[32,384]{1,0:T(8,128)S(1)}, f32[32,384]{1,0:T(8,128)S(1)}, u32[]{:S(2)}, u32[]{:S(2)}) collective-permute-start(f32[32,384]{1,0:T(8,128)S(1)} %tile_sums.1), channel_id=1, source_target_pairs={{0,16},{8,24},{16,0},{24,8},{1,17},{9,25},{17,1},{25,9},{2,18},{10... | collective-permute-start | bytes 147464 | tf_op jit(solution)/shard_map/ppermute | solution.py:617
  31.8 6.1 %collective-permute-start.8 = (f32[32,384]{1,0:T(8,128)S(1)}, f32[32,384]{1,0:T(8,128)S(1)}, u32[]{:S(2)}, u32[]{:S(2)}) collective-permute-start(f32[32,384]{1,0:T(8,128)S(1)} %tile_sums.1), channel_id=1, source_target_pairs={{0,24},{8,16},{16,8},{24,0},{1,25},{9,17},{17,9},{25,1},{2,26},{10... | collective-permute-start | bytes 147464 | tf_op jit(solution)/shard_map/ppermute | solution.py:617
  37.8 11.0 %copy-start.5 = (bf16[128,256]{1,0:T(8,128)(2,1)S(1)}, bf16[128,256]{1,0:T(8,128)(2,1)}, u32[]{:S(2)}) copy-start(bf16[128,256]{1,0:T(8,128)(2,1)} %constant.36.clone.seg_ref) | copy-start | bytes 196612
  37.8 6.8 %collective-permute-start.4 = (f32[6,3,16,256]{3,2,1,0:T(8,128)S(1)}, f32[6,3,16,256]{3,2,1,0:T(8,128)S(1)}, u32[]{:S(2)}, u32[]{:S(2)}) collective-permute-start(f32[6,3,16,256]{3,2,1,0:T(8,128)S(1)} %get-tuple-element.40), channel_id=1, source_target_pairs={{0,8},{8,0},{16,24},{24,16},{1,9},{9,1},{17,25},{25,17},{2,10},{10... | collective-permute-start | bytes 884744 | tf_op jit(solution)/shard_map/ppermute | solution.py:617
  38.0 1.3 %collective-permute-start.9 = (f32[32,384]{1,0:T(8,128)S(1)}, f32[32,384]{1,0:T(8,128)S(1)}, u32[]{:S(2)}, u32[]{:S(2)}) collective-permute-start(f32[32,384]{1,0:T(8,128)S(1)} %add_add_fusion.1), channel_id=1, source_target_pairs={{0,1},{1,0},{2,3},{3,2},{4,5},{5,4},{6,7},{7,6},{8,9},{9,8},{10,11... | collective-permute-start | bytes 147464 | tf_op jit(solution)/shard_map/ppermute | solution.py:617
  39.3 9.2 %collective-permute-start.10 = (f32[32,384]{1,0:T(8,128)S(1)}, f32[32,384]{1,0:T(8,128)S(1)}, u32[]{:S(2)}, u32[]{:S(2)}) collective-permute-start(f32[32,384]{1,0:T(8,128)S(1)} %add.30), channel_id=1, source_target_pairs={{0,2},{1,3},{2,0},{3,1},{4,6},{5,7},{6,4},{7,5},{8,10},{9,11},{10,... | collective-permute-start | bytes 147464 | tf_op jit(solution)/shard_map/ppermute | solution.py:617
  40.0 8.8 %collective-permute-start.11 = (f32[32,384]{1,0:T(8,128)S(1)}, f32[32,384]{1,0:T(8,128)S(1)}, u32[]{:S(2)}, u32[]{:S(2)}) collective-permute-start(f32[32,384]{1,0:T(8,128)S(1)} %add.30), channel_id=1, source_target_pairs={{0,4},{1,5},{2,6},{3,7},{4,0},{5,1},{6,2},{7,3},{8,12},{9,13},{10,... | collective-permute-start | bytes 147464 | tf_op jit(solution)/shard_map/ppermute | solution.py:617
  42.0 6.8 %collective-permute-start.12 = (f32[32,384]{1,0:T(8,128)S(1)}, f32[32,384]{1,0:T(8,128)S(1)}, u32[]{:S(2)}, u32[]{:S(2)}) collective-permute-start(f32[32,384]{1,0:T(8,128)S(1)} %add.30), channel_id=1, source_target_pairs={{0,6},{1,7},{2,4},{3,5},{4,2},{5,3},{6,0},{7,1},{8,14},{9,15},{10,... | collective-permute-start | bytes 147464 | tf_op jit(solution)/shard_map/ppermute | solution.py:617

commit v3 on v2

--- a/solution.py
+++ b/solution.py
@@ -78,6 +78,7 @@
 LARGE = pltpu.CompilerParams(vmem_limit_bytes=12 * 2**20)
 SMALL = pltpu.CompilerParams(vmem_limit_bytes=5 * 2**20)
 CHUNK = 8
+BLOCK = 16
 AHEAD = 3
 
 
@@ -92,12 +93,12 @@
 def lon_edge_kernel(lon_ref, rad_ref, place_ref, state_hbm, speed_hbm, matrix_hbm, table_hbm, rim, ids_ref, same, *refs):
     *crosses, speed_ref, matrix_ref, table_ref, edges, weights, sem, few_sem = refs
     fields, rows, cols, depth = state_hbm.shape
-    chunks = rows // CHUNK
+    chunks = rows // BLOCK
     size = same.shape[1]
     keep = edges.shape[2] // 2
 
     def loads(c):
-        here = pl.ds(c * CHUNK, CHUNK)
+        here = pl.ds(c * BLOCK, BLOCK)
         return [
             pltpu.make_async_copy(
                 state_hbm.at[:, here, pl.ds(first, keep)], edges.at[:, here, pl.ds(slot, keep)], sem.at[2 * c + i]
@@ -134,8 +135,8 @@
     def step(c, carry):
         for copy in loads(c):
             copy.wait()
-        for j in range(CHUNK):
-            r = c * CHUNK + j
+        for j in range(BLOCK):
+            r = c * BLOCK + j
             high, low = parts_of(edges[:, r].reshape(-1, depth), 2)
             sums = dot(weights[...], jnp.concatenate([high, low, high], axis=0))
             same[r] = sums[:size]
@@ -177,7 +178,7 @@
             pltpu.VMEM(tables.shape, f32),
             pltpu.VMEM((fields, rows, 2 * keep, depth), f32),
             pltpu.VMEM((2 * size, 3 * len(sources)), bf16),
-            pltpu.SemaphoreType.DMA((2 * rows // CHUNK,)),
+            pltpu.SemaphoreType.DMA((2 * rows // BLOCK,)),
             pltpu.SemaphoreType.DMA((5,)),
         ],
         compiler_params=LARGE,
@@ -279,7 +280,8 @@
 
 
 def local_kernel(
-    speed_ref, state_hbm, matrix_ref, pick_ref, same_ref, sum_ref, gap_ref, total, turned, cells, w_ref, sem
+    speed_ref, state_hbm, matrix_ref, pick_ref, same_ref, sum_ref, gap_ref, density_ref, packed_ref,
+    total, turned, cells, rest_ref, spread_ref, w_ref, sem,
 ):
     fields, rows, cols, depth = total.shape
     chunks = rows // CHUNK
@@ -301,6 +303,8 @@
         cells[:, edge : edge + REACH] = jnp.zeros((fields, REACH, cols, depth), f32)
         turned[edge : edge + REACH] = jnp.zeros((REACH, size, depth), f32)
 
+    keep_rest(density_ref, packed_ref, rest_ref, spread_ref)
+
     def rows_of(c, carry):
         load(c).wait()
 
@@ -325,7 +329,7 @@
     lax.fori_loop(0, chunks, radial, 0)
 
 
-def local_update(state, matrices, speed):
+def local_update(state, matrices, speed, density, packed):
     fields, rows, cols, depth = state.shape
     size = fields * cols
     every = [(f, l) for f in range(fields) for l in range(cols)]
@@ -333,15 +337,22 @@
     padded = rows + 2 * REACH
     return pl.pallas_call(
         local_kernel,
-        in_specs=[SMEM, HBM] + [VMEM] * 5,
-        out_specs=[VMEM] * 3,
-        out_shape=[in_vmem(*state.shape), in_vmem(padded, size, depth), in_vmem(fields, padded, cols, depth)],
+        in_specs=[SMEM, HBM] + [VMEM] * 7,
+        out_specs=[VMEM] * 5,
+        out_shape=[
+            in_vmem(*state.shape),
+            in_vmem(padded, size, depth),
+            in_vmem(fields, padded, cols, depth),
+            in_vmem(16, density.shape[2]),
+            in_vmem(3, *density.shape[1:]),
+        ],
         scratch_shapes=[pltpu.VMEM((2 * size, 3 * size), bf16), pltpu.SemaphoreType.DMA((rows // CHUNK,))],
         compiler_params=SMALL,
         cost_estimate=cost(1e3, 1e3),
         name="local_update",
     )(
-        speed, pltpu.with_memory_space_constraint(state, pltpu.HBM), matrices, *turn_tables(fields, cols), summed, gapped
+        speed, pltpu.with_memory_space_constraint(state, pltpu.HBM), matrices, *turn_tables(fields, cols), summed, gapped,
+        density, packed,
     )
 
 
@@ -464,7 +475,7 @@
     return [turned[:channels, i : i + 1] for i in range(4)]
 
 
-def rest_kernel(density_ref, packed_ref, out_ref, spread_ref):
+def keep_rest(density_ref, packed_ref, out_ref, spread_ref):
     _, channels, points = density_ref.shape
     courant, weight, first, second = columns_of(packed_ref, channels)
     rows = []
@@ -480,17 +491,6 @@
     out_ref[...] = jnp.concatenate(rows + [rest] * 8, axis=0)
     for i, column in enumerate((courant, first, second)):
         spread_ref[i] = jnp.broadcast_to(column, (channels, points))
-
-
-def rest_of(density, packed):
-    _, channels, points = density.shape
-    return pl.pallas_call(
-        rest_kernel,
-        out_shape=[in_vmem(16, points), in_vmem(3, channels, points)],
-        compiler_params=SMALL,
-        cost_estimate=cost(1e3, 1e3),
-        name="rest_pressure",
-    )(density, packed)
 
 
 def pressures_of(sums, rest_ref):
@@ -647,9 +647,8 @@
 
     packed = jnp.concatenate([drift_courant[None], energy_weight[None], injection], axis=0)
     packed = jnp.pad(packed, ((0, 4), (0, -packed.shape[1] % 128)))
-    rest, spread = rest_of(phase_density, packed)
-
-    part, turned, cells = local_update(state, flux_matrices, wave_speed)
+
+    part, turned, cells, rest, spread = local_update(state, flux_matrices, wave_speed, phase_density, packed)
 
     targets = block_tile[0, :, 0]
     hits = (tile_of_device[:, None] == targets[None, :]).astype(bf16)

time: 51.2 us -> 50.6 us (0.988)
  Pallas kernels: 29.1 us -> 27.7 us
  waiting for transfers between devices: 2.39 us -> 3.01 us
    pallas_call x2 -> x1, Pallas kernels: 10.3 us -> 9.58 us  [local_update(): pl.pallas_call(local_kernel, in_specs=[SMEM, HBM] + [VMEM] * 7, out_specs...]
    ppermute x1, waiting for transfers between devices: 0.87 us -> 1.5 us  [per_device(): cross_1 = lax.ppermute(crosses[1], 'lon', across)]
    pallas_call x1, Pallas kernels: 4.36 us -> 3.77 us  [lon_edges(): pl.pallas_call(lon_edge_kernel, in_specs=[SMEM] * 3 + [HBM] * 4, out_spec...]
  transfers between devices with their start and end apart: 13 -> 13, of which waited for: 3 -> 3; matrix products, arithmetic and copies ran while one was open for 0% -> 0% of each run, Pallas kernels for 44% -> 43%
where the time goes in v3:
time: 50.6 us; the launch traced here: 50.4 us
  Pallas kernels  27.7 us (55%)
  starting transfers between devices  18.4 us (36%)
  waiting for transfers between devices  3.01 us (6%)
  between operations  0.97 us (2%)
    ppermute x10, starting transfers between devices, swap(): lax.ppermute(x, axis, [(i, i ^ bit) for i in range(lax.axis_size(axis))])  13 us
    pallas_call x1, Pallas kernels, local_update(): pl.pallas_call(local_kernel, in_specs=[SMEM, HBM] + [VMEM] * 7, out_specs...  9.58 us
    ppermute x1, starting transfers between devices, per_device(): cross_0 = lax.ppermute(crosses[0], 'lon', across)  4.71 us
    pallas_call x1, Pallas kernels, radial_update(): pl.pallas_call(functools.partial(radial_kernel, fields), in_specs=[SMEM]...  4.47 us
    pallas_call x1, Pallas kernels, finish_most(): pl.pallas_call(most_kernel, in_specs=[SMEM] + [VMEM] * len(pins), out_spe...  3.81 us
    pallas_call x1, Pallas kernels, lon_edges(): pl.pallas_call(lon_edge_kernel, in_specs=[SMEM] * 3 + [HBM] * 4, out_spec...  3.77 us
    pallas_call x1, Pallas kernels, tile_sums(): pl.pallas_call(tile_sum_kernel, in_specs=[SMEM] + [VMEM] * 10, out_specs=...  2.36 us
    pallas_call x1, Pallas kernels, finish_last(): pl.pallas_call(last_kernel, in_specs=[SMEM, VMEM, HBM] + [VMEM] * 7, out_...  2.23 us
  transfers between devices with their start and end apart: 13, of which 3 were waited for; matrix products, arithmetic and copies ran while one was open for 0% of the time, Pallas kernels for 43%

profile of v3, /device:TPU:0, one launch (start us, length us, event | category | flops | bytes accessed | tf_op | source)
XLA Modules:
  0.0 50.4 jit_solution(16654298452247479544)
XLA Ops:
  0.6 0.0 copy-start.2
  0.6 0.0 copy-start.3
  0.7 0.0 copy-start.7
  0.7 0.0 copy-start.8
  0.7 0.0 copy-start.4
  0.7 0.0 copy-start.10
  0.7 0.0 copy-start.12
  0.7 0.0 copy-start.11
  0.7 0.0 copy-start.15
  0.7 0.0 copy-start.14
  0.7 0.0 copy-start.13
  0.8 0.0 copy-start.1
  0.8 0.0 copy-start
  0.8 0.0 copy-start.6
  0.8 0.0 copy-start.9
  0.8 3.8 %lon_edges.1 = (f32[8,6,16,256]{3,2,1,0:T(8,128)S(1)}, s32[3]{0:T(128)S(1)}, f32[64,24,256]{2,1,0:T(8,128)S(1)}, f32[64,8,256]{2,1,0:T(8,128)S(1)}, f32[64,16,256]{2,1,0:T(8,128)S(1)}) custom-call(s32[1]{0:T(128)} %bitcast.lon_ref, s32[1]{0:T(128)} %bitcast.1.rad_ref, s32[1]{0:T(128)} %bitcast.2.place_ref, f32[8,64,16,256]{3,2,1,0:T(8,128)} %state_hbm.3, ...), custom_call_target="tpu_custom_call" | custom-call | flops 1000 | bytes 1000 | tf_op jit(solution)/shard_map/lon_edges/pallas_call | solution.py:164
  4.6 0.5 %collective-permute-start = (f32[64,24,256]{2,1,0:T(8,128)S(1)}, f32[64,24,256]{2,1,0:T(8,128)S(1)}, u32[]{:S(2)}, u32[]{:S(2)}) collective-permute-start(f32[64,24,256]{2,1,0:T(8,128)S(1)} %get-tuple-element.31), channel_id=1, source_target_pairs={{0,1},{1,0},{2,3},{3,2},{4,5},{5,4},{6,7},{7,6},{8,9},{9,8},{10,11... | collective-permute-start | bytes 4718600 | tf_op jit(solution)/shard_map/ppermute | solution.py:617
  5.1 4.7 %collective-permute-start.1 = (f32[64,8,256]{2,1,0:T(8,128)S(1)}, f32[64,8,256]{2,1,0:T(8,128)S(1)}, u32[]{:S(2)}, u32[]{:S(2)}) collective-permute-start(f32[64,8,256]{2,1,0:T(8,128)S(1)} %get-tuple-element.32), channel_id=1, source_target_pairs={{0,7},{1,2},{2,1},{3,4},{4,3},{5,6},{6,5},{7,0},{8,15},{9,10},{10,... | collective-permute-start | bytes 1572872 | tf_op jit(solution)/shard_map/ppermute | solution.py:640
  9.8 0.0 collective-permute-start.5
  9.9 0.0 copy-done.2
  9.9 0.0 copy-done.3
  9.9 0.0 copy-done.4
  9.9 0.0 copy-done.10
  9.9 1.5 %rad_edges.1 = (f32[2,3,16,256]{3,2,1,0:T(8,128)S(1)}, f32[6,3,16,256]{3,2,1,0:T(8,128)S(1)}, f32[8,3,16,256]{3,2,1,0:T(8,128)S(1)}) custom-call(s32[3]{0:T(128)S(1)} %get-tuple-element.25.ids_ref, f32[2]{0:T(128)S(1)} %copy-done.10, f32[8,6,16,256]{3,2,1,0:T(8,128)S(1)} %get-tuple-element.29.rim_ref, f32[2,8,8]{2,1,0:T(8,128)S(1)} %copy-done.4, ...), custom_call_target="tpu_custom_call" | custom-call | flops 1000 | bytes 1000 | tf_op jit(solution)/shard_map/rad_edges/pallas_call | solution.py:235
  11.4 0.7 %collective-permute-start.3 = (f32[8,3,16,256]{3,2,1,0:T(8,128)S(1)}, f32[8,3,16,256]{3,2,1,0:T(8,128)S(1)}, u32[]{:S(2)}, u32[]{:S(2)}) collective-permute-start(f32[8,3,16,256]{3,2,1,0:T(8,128)S(1)} %get-tuple-element.34), channel_id=1, source_target_pairs={{8,16},{16,8},{9,17},{17,9},{10,18},{18,10},{11,19},{19,11},{12,20... | collective-permute-start | bytes 1179656 | tf_op jit(solution)/shard_map/ppermute | solution.py:646
  12.1 4.3 %collective-permute-start.2 = (f32[2,3,16,256]{3,2,1,0:T(8,128)S(1)}, f32[2,3,16,256]{3,2,1,0:T(8,128)S(1)}, u32[]{:S(2)}, u32[]{:S(2)}) collective-permute-start(f32[2,3,16,256]{3,2,1,0:T(8,128)S(1)} %get-tuple-element.33), channel_id=1, source_target_pairs={{0,8},{8,0},{16,24},{24,16},{1,9},{9,1},{17,25},{25,17},{2,10},{10... | collective-permute-start | bytes 294920 | tf_op jit(solution)/shard_map/ppermute | solution.py:617
  16.4 0.0 copy-done.12
  16.4 0.0 copy-done.11
  16.4 0.1 compare_convert_fusion.1.hit_ref
  16.4 0.0 copy-done.14
  16.5 0.0 copy-done.7
  16.5 0.0 copy-done.8
  16.5 0.0 copy-done.1
  16.5 9.6 %local_update.1 = (f32[8,64,16,256]{3,2,1,0:T(8,128)S(1)}, f32[70,128,256]{2,1,0:T(8,128)S(1)}, f32[8,70,16,256]{3,2,1,0:T(8,128)S(1)}, f32[16,128]{1,0:T(8,128)S(1)}, f32[3,200,128]{2,1,0:T(8,128)S(1)}) custom-call(f32[2]{0:T(128)S(1)} %copy-done.10, f32[8,64,16,256]{3,2,1,0:T(8,128)} %state_hbm.3, f32[2,8,8]{2,1,0:T(8,128)S(1)} %copy-done.4, ...), custom_call_target="tpu_custom_call" | custom-call | flops 1000 | bytes 1000 | tf_op jit(solution)/shard_map/local_update/pallas_call | solution.py:338
  26.1 0.0 collective-permute-done.2.near_ref.refs_0_
  26.1 0.0 collective-permute-done.3.far_ref.refs_2_
  26.1 0.0 collective-permute-done.1.cross_ref.refs_4_
  26.1 0.0 collective-permute-done.same_ref.refs_3_
  26.1 0.0 copy-done
  26.1 0.0 copy-done.6
  26.1 0.0 copy-done.9
  26.2 2.4 %tile_sums.1 = f32[32,384]{1,0:T(8,128)S(1)} custom-call(s32[3]{0:T(128)S(1)} %get-tuple-element.25.ids_ref, f32[8,64,16,256]{3,2,1,0:T(8,128)S(1)} %get-tuple-element.37.part_ref._, f32[64,16,256]{2,1,0:T(8,128)S(1)} %copy-done, f32[64,24,256]{2,1,0:T(8,128)S(1)} %collective-permute-done.same_ref.refs_3_, ...), custom_call_target="tpu_custom_call" | custom-call | flops 1000 | bytes 1000 | tf_op jit(solution)/shard_map/tile_sums/pallas_call | solution.py:455
  28.5 0.1 collective-permute-start.6
  28.7 1.9 %collective-permute-start.7 = (f32[32,384]{1,0:T(8,128)S(1)}, f32[32,384]{1,0:T(8,128)S(1)}, u32[]{:S(2)}, u32[]{:S(2)}) collective-permute-start(f32[32,384]{1,0:T(8,128)S(1)} %tile_sums.1), channel_id=1, source_target_pairs={{0,16},{8,24},{16,0},{24,8},{1,17},{9,25},{17,1},{25,9},{2,18},{10... | collective-permute-start | bytes 147464 | tf_op jit(solution)/shard_map/ppermute | solution.py:617
  30.5 1.5 %collective-permute-start.8 = (f32[32,384]{1,0:T(8,128)S(1)}, f32[32,384]{1,0:T(8,128)S(1)}, u32[]{:S(2)}, u32[]{:S(2)}) collective-permute-start(f32[32,384]{1,0:T(8,128)S(1)} %tile_sums.1), channel_id=1, source_target_pairs={{0,24},{8,16},{16,8},{24,0},{1,25},{9,17},{17,9},{25,1},{2,26},{10... | collective-permute-start | bytes 147464 | tf_op jit(solution)/shard_map/ppermute | solution.py:617
  32.0 4.5 %radial_update.1.part_ref = f32[8,64,16,256]{3,2,1,0:T(8,128)S(1)} custom-call(f32[2]{0:T(128)S(1)} %copy-done.10, f32[8,70,16,256]{3,2,1,0:T(8,128)S(1)} %get-tuple-element.26.cells, f32[70,128,256]{2,1,0:T(8,128)S(1)} %get-tuple-element.27.turned, f32[8,64,16,256]{3,2,1,0:T(8,128)S(1)} %get-tuple-element.37.part_ref._), custom_call_target="tpu_custom_call", output_to_operand_aliasing={{}: (3, {})} | custom-call | flops 100000000 | bytes 6000000 | tf_op jit(solution)/shard_map/radial_update/pallas_call | solution.py:368
  36.5 0.0 copy-start.5
  36.5 0.2 collective-permute-start.4
  36.7 0.0 collective-permute-done.6
  36.7 0.0 collective-permute-done.7
  36.7 0.0 collective-permute-done.8
  36.7 0.1 collective-permute-start.9
  36.8 1.2 %collective-permute-done.9 = f32[32,384]{1,0:T(8,128)S(1)} collective-permute-done((f32[32,384]{1,0:T(8,128)S(1)}, f32[32,384]{1,0:T(8,128)S(1)}, u32[]{:S(2)}, u32[]{:S(2)}) %collective-permute-start.9) | collective-permute-done | bytes 49184 | tf_op jit(solution)/shard_map/ppermute | solution.py:617
  38.1 1.3 %collective-permute-start.10 = (f32[32,384]{1,0:T(8,128)S(1)}, f32[32,384]{1,0:T(8,128)S(1)}, u32[]{:S(2)}, u32[]{:S(2)}) collective-permute-start(f32[32,384]{1,0:T(8,128)S(1)} %add.30), channel_id=1, source_target_pairs={{0,2},{1,3},{2,0},{3,1},{4,6},{5,7},{6,4},{7,5},{8,10},{9,11},{10,... | collective-permute-start | bytes 147464 | tf_op jit(solution)/shard_map/ppermute | solution.py:617
  39.4 2.0 %collective-permute-start.11 = (f32[32,384]{1,0:T(8,128)S(1)}, f32[32,384]{1,0:T(8,128)S(1)}, u32[]{:S(2)}, u32[]{:S(2)}) collective-permute-start(f32[32,384]{1,0:T(8,128)S(1)} %add.30), channel_id=1, source_target_pairs={{0,4},{1,5},{2,6},{3,7},{4,0},{5,1},{6,2},{7,3},{8,12},{9,13},{10,... | collective-permute-start | bytes 147464 | tf_op jit(solution)/shard_map/ppermute | solution.py:617
  41.4 1.1 %collective-permute-start.12 = (f32[32,384]{1,0:T(8,128)S(1)}, f32[32,384]{1,0:T(8,128)S(1)}, u32[]{:S(2)}, u32[]{:S(2)}) collective-permute-start(f32[32,384]{1,0:T(8,128)S(1)} %add.30), channel_id=1, source_target_pairs={{0,6},{1,7},{2,4},{3,5},{4,2},{5,3},{6,0},{7,1},{8,14},{9,15},{10,... | collective-permute-start | bytes 147464 | tf_op jit(solution)/shard_map/ppermute | solution.py:617
  42.5 0.1 compare_convert_fusion.hit_ref
  42.6 1.5 %collective-permute-done.5.refs_5_ = f32[64,16,256]{2,1,0:T(8,128)S(1)} collective-permute-done((f32[64,16,256]{2,1,0:T(8,128)S(1)}, f32[64,16,256]{2,1,0:T(8,128)S(1)}, u32[]{:S(2)}, u32[]{:S(2)}) %collective-permute-start.5) | collective-permute-done | bytes 1048608 | tf_op jit(solution)/shard_map/ppermute | solution.py:642
  44.1 0.0 collective-permute-done.4.refs_1_
  44.1 3.8 %finish_most.1 = (f32[8,64,16,256]{3,2,1,0:T(8,128)}, f32[64,16,256]{2,1,0:T(8,128)S(1)}) custom-call(s32[3]{0:T(128)S(1)} %get-tuple-element.25.ids_ref, f32[8,64,16,256]{3,2,1,0:T(8,128)S(1)} %radial_update.1.part_ref, f32[2,3,16,256]{3,2,1,0:T(8,128)S(1)} %collective-permute-done.2.near_ref.refs_0_, f32[6,3,16,256]{3,2,1,0:T(8,128)S(1)} %collective-permute-done.4.refs_1_, ...), custom_call_target="tpu_custom_call" | custom-call | flops 100000000 | bytes 16000000 | tf_op jit(solution)/shard_map/finish_most/pallas_call | solution.py:584
  47.9 0.0 collective-permute-done.10
  47.9 0.3 collective-permute-done.11
  48.2 0.0 collective-permute-done.12
  48.2 2.2 %finish_last.1 = (f32[8,64,16,256]{3,2,1,0:T(8,128)}, f32[1,200,128]{2,1,0:T(8,128)}) custom-call(s32[3]{0:T(128)S(1)} %get-tuple-element.25.ids_ref, f32[64,16,256]{2,1,0:T(8,128)S(1)} %get-tuple-element.42.cells_ref, f32[8,64,16,256]{3,2,1,0:T(8,128)} %get-tuple-element.45._, ...), custom_call_target="tpu_custom_call", output_to_operand_aliasing={{0}: (2, {})} | custom-call | flops 1000 | bytes 1000 | tf_op jit(solution)/shard_map/finish_last/pallas_call | solution.py:598
  (7 shorter events, 0.1 us)
Async XLA Ops:
  0.6 9.2 %copy-start.2 = (f32[128,8]{1,0:T(8,128)S(1)}, f32[128,8]{1,0:T(8,128)}, u32[]{:S(2)}) copy-start(f32[128,8]{1,0:T(8,128)} %constant.30.clone.pick_ref) | copy-start | bytes 12292
  0.6 9.2 %copy-start.3 = (f32[128,128]{1,0:T(8,128)S(1)}, f32[128,128]{1,0:T(8,128)}, u32[]{:S(2)}) copy-start(f32[128,128]{1,0:T(8,128)} %constant.31.clone.same_ref) | copy-start | bytes 196612
  0.7 15.8 %copy-start.7 = (f32[128,128]{1,0:T(8,128)S(1)}, f32[128,128]{1,0:T(8,128)}, u32[]{:S(2)}) copy-start(f32[128,128]{1,0:T(8,128)} %constant.32.clone.sum_ref) | copy-start | bytes 196612
  0.7 15.8 %copy-start.8 = (f32[128,128]{1,0:T(8,128)S(1)}, f32[128,128]{1,0:T(8,128)}, u32[]{:S(2)}) copy-start(f32[128,128]{1,0:T(8,128)} %constant.33.clone.gap_ref) | copy-start | bytes 196612
  0.7 9.2 %copy-start.4 = (f32[2,8,8]{2,1,0:T(8,128)S(1)}, f32[2,8,8]{2,1,0:T(8,128)}, u32[]{:S(2)}) copy-start(f32[2,8,8]{2,1,0:T(8,128)} %matrix_ref.3) | copy-start | bytes 1540
  0.7 9.2 %copy-start.10 = (f32[2]{0:T(128)S(1)}, f32[2]{0:T(128)}, u32[]{:S(2)}) copy-start(f32[2]{0:T(128)} %speed_ref.5) | copy-start | bytes 28
  0.7 15.6 %copy-start.12 = (s32[1,64,1]{1,2,0:T(1,128)S(1)}, s32[1,64,1]{1,2,0:T(1,128)}, u32[]{:S(2)}) copy-start(s32[1,64,1]{1,2,0:T(1,128)} %param.24) | copy-start | bytes 772
  0.7 15.6 %copy-start.11 = (s32[32]{0:T(128)S(1)}, s32[32]{0:T(128)}, u32[]{:S(2)}) copy-start(s32[32]{0:T(128)} %param.25) | copy-start | bytes 388
  0.7 15.7 %copy-start.15 = (f32[200]{0:T(256)S(1)}, f32[200]{0:T(256)}, u32[]{:S(2)}) copy-start(f32[200]{0:T(256)} %param.28) | copy-start | bytes 2404
  0.7 15.7 %copy-start.14 = (f32[200]{0:T(256)S(1)}, f32[200]{0:T(256)}, u32[]{:S(2)}) copy-start(f32[200]{0:T(256)} %param.29) | copy-start | bytes 2404
  0.7 15.7 %copy-start.13 = (f32[2,200]{1,0:T(2,128)S(1)}, f32[2,200]{1,0:T(2,128)}, u32[]{:S(2)}) copy-start(f32[2,200]{1,0:T(2,128)} %param.27) | copy-start | bytes 4804
  0.8 15.7 %copy-start.1 = (f32[1,200,128]{2,1,0:T(8,128)S(1)}, f32[1,200,128]{2,1,0:T(8,128)}, u32[]{:S(2)}) copy-start(f32[1,200,128]{2,1,0:T(8,128)} %density_ref.3) | copy-start | bytes 307204
  0.8 25.4 %copy-start = (f32[64,16,256]{2,1,0:T(8,128)S(1)}, f32[64,16,256]{2,1,0:T(8,128)}, u32[]{:S(2)}) copy-start(f32[64,16,256]{2,1,0:T(8,128)} %vol_ref.1) | copy-start | bytes 3145732
  0.8 25.4 %copy-start.6 = (bf16[256,128]{1,0:T(8,128)(2,1)S(1)}, bf16[256,128]{1,0:T(8,128)(2,1)}, u32[]{:S(2)}) copy-start(bf16[256,128]{1,0:T(8,128)(2,1)} %constant.34.clone.seg_ref) | copy-start | bytes 196612
  0.8 25.4 %copy-start.9 = (f32[16,128]{1,0:T(8,128)S(1)}, f32[16,128]{1,0:T(8,128)}, u32[]{:S(2)}) copy-start(f32[16,128]{1,0:T(8,128)} %constant.35.clone.spot_ref) | copy-start | bytes 24580
  4.6 21.5 %collective-permute-start = (f32[64,24,256]{2,1,0:T(8,128)S(1)}, f32[64,24,256]{2,1,0:T(8,128)S(1)}, u32[]{:S(2)}, u32[]{:S(2)}) collective-permute-start(f32[64,24,256]{2,1,0:T(8,128)S(1)} %get-tuple-element.31), channel_id=1, source_target_pairs={{0,1},{1,0},{2,3},{3,2},{4,5},{5,4},{6,7},{7,6},{8,9},{9,8},{10,11... | collective-permute-start | bytes 4718600 | tf_op jit(solution)/shard_map/ppermute | solution.py:617
  5.1 21.0 %collective-permute-start.1 = (f32[64,8,256]{2,1,0:T(8,128)S(1)}, f32[64,8,256]{2,1,0:T(8,128)S(1)}, u32[]{:S(2)}, u32[]{:S(2)}) collective-permute-start(f32[64,8,256]{2,1,0:T(8,128)S(1)} %get-tuple-element.32), channel_id=1, source_target_pairs={{0,7},{1,2},{2,1},{3,4},{4,3},{5,6},{6,5},{7,0},{8,15},{9,10},{10,... | collective-permute-start | bytes 1572872 | tf_op jit(solution)/shard_map/ppermute | solution.py:640
  9.8 34.3 %collective-permute-start.5 = (f32[64,16,256]{2,1,0:T(8,128)S(1)}, f32[64,16,256]{2,1,0:T(8,128)S(1)}, u32[]{:S(2)}, u32[]{:S(2)}) collective-permute-start(f32[64,16,256]{2,1,0:T(8,128)S(1)} %get-tuple-element.41), channel_id=1, source_target_pairs={{0,7},{1,2},{2,1},{3,4},{4,3},{5,6},{6,5},{7,0},{8,15},{9,10},{10,... | collective-permute-start | bytes 3145736 | tf_op jit(solution)/shard_map/ppermute | solution.py:642
  11.4 14.7 %collective-permute-start.3 = (f32[8,3,16,256]{3,2,1,0:T(8,128)S(1)}, f32[8,3,16,256]{3,2,1,0:T(8,128)S(1)}, u32[]{:S(2)}, u32[]{:S(2)}) collective-permute-start(f32[8,3,16,256]{3,2,1,0:T(8,128)S(1)} %get-tuple-element.34), channel_id=1, source_target_pairs={{8,16},{16,8},{9,17},{17,9},{10,18},{18,10},{11,19},{19,11},{12,20... | collective-permute-start | bytes 1179656 | tf_op jit(solution)/shard_map/ppermute | solution.py:646
  12.1 14.0 %collective-permute-start.2 = (f32[2,3,16,256]{3,2,1,0:T(8,128)S(1)}, f32[2,3,16,256]{3,2,1,0:T(8,128)S(1)}, u32[]{:S(2)}, u32[]{:S(2)}) collective-permute-start(f32[2,3,16,256]{3,2,1,0:T(8,128)S(1)} %get-tuple-element.33), channel_id=1, source_target_pairs={{0,8},{8,0},{16,24},{24,16},{1,9},{9,1},{17,25},{25,17},{2,10},{10... | collective-permute-start | bytes 294920 | tf_op jit(solution)/shard_map/ppermute | solution.py:617
  28.5 8.2 %collective-permute-start.6 = (f32[32,384]{1,0:T(8,128)S(1)}, f32[32,384]{1,0:T(8,128)S(1)}, u32[]{:S(2)}, u32[]{:S(2)}) collective-permute-start(f32[32,384]{1,0:T(8,128)S(1)} %tile_sums.1), channel_id=1, source_target_pairs={{0,8},{8,0},{16,24},{24,16},{1,9},{9,1},{17,25},{25,17},{2,10},{10... | collective-permute-start | bytes 147464 | tf_op jit(solution)/shard_map/ppermute | solution.py:617
  28.7 8.1 %collective-permute-start.7 = (f32[32,384]{1,0:T(8,128)S(1)}, f32[32,384]{1,0:T(8,128)S(1)}, u32[]{:S(2)}, u32[]{:S(2)}) collective-permute-start(f32[32,384]{1,0:T(8,128)S(1)} %tile_sums.1), channel_id=1, source_target_pairs={{0,16},{8,24},{16,0},{24,8},{1,17},{9,25},{17,1},{25,9},{2,18},{10... | collective-permute-start | bytes 147464 | tf_op jit(solution)/shard_map/ppermute | solution.py:617
  30.5 6.2 %collective-permute-start.8 = (f32[32,384]{1,0:T(8,128)S(1)}, f32[32,384]{1,0:T(8,128)S(1)}, u32[]{:S(2)}, u32[]{:S(2)}) collective-permute-start(f32[32,384]{1,0:T(8,128)S(1)} %tile_sums.1), channel_id=1, source_target_pairs={{0,24},{8,16},{16,8},{24,0},{1,25},{9,17},{17,9},{25,1},{2,26},{10... | collective-permute-start | bytes 147464 | tf_op jit(solution)/shard_map/ppermute | solution.py:617
  36.5 11.7 %copy-start.5 = (bf16[128,256]{1,0:T(8,128)(2,1)S(1)}, bf16[128,256]{1,0:T(8,128)(2,1)}, u32[]{:S(2)}) copy-start(bf16[128,256]{1,0:T(8,128)(2,1)} %constant.36.clone.seg_ref) | copy-start | bytes 196612
  36.5 7.6 %collective-permute-start.4 = (f32[6,3,16,256]{3,2,1,0:T(8,128)S(1)}, f32[6,3,16,256]{3,2,1,0:T(8,128)S(1)}, u32[]{:S(2)}, u32[]{:S(2)}) collective-permute-start(f32[6,3,16,256]{3,2,1,0:T(8,128)S(1)} %get-tuple-element.40), channel_id=1, source_target_pairs={{0,8},{8,0},{16,24},{24,16},{1,9},{9,1},{17,25},{25,17},{2,10},{10... | collective-permute-start | bytes 884744 | tf_op jit(solution)/shard_map/ppermute | solution.py:617
  36.7 1.3 %collective-permute-start.9 = (f32[32,384]{1,0:T(8,128)S(1)}, f32[32,384]{1,0:T(8,128)S(1)}, u32[]{:S(2)}, u32[]{:S(2)}) collective-permute-start(f32[32,384]{1,0:T(8,128)S(1)} %add_add_fusion.1), channel_id=1, source_target_pairs={{0,1},{1,0},{2,3},{3,2},{4,5},{5,4},{6,7},{7,6},{8,9},{9,8},{10,11... | collective-permute-start | bytes 147464 | tf_op jit(solution)/shard_map/ppermute | solution.py:617
  38.1 9.9 %collective-permute-start.10 = (f32[32,384]{1,0:T(8,128)S(1)}, f32[32,384]{1,0:T(8,128)S(1)}, u32[]{:S(2)}, u32[]{:S(2)}) collective-permute-start(f32[32,384]{1,0:T(8,128)S(1)} %add.30), channel_id=1, source_target_pairs={{0,2},{1,3},{2,0},{3,1},{4,6},{5,7},{6,4},{7,5},{8,10},{9,11},{10,... | collective-permute-start | bytes 147464 | tf_op jit(solution)/shard_map/ppermute | solution.py:617
  39.4 8.8 %collective-permute-start.11 = (f32[32,384]{1,0:T(8,128)S(1)}, f32[32,384]{1,0:T(8,128)S(1)}, u32[]{:S(2)}, u32[]{:S(2)}) collective-permute-start(f32[32,384]{1,0:T(8,128)S(1)} %add.30), channel_id=1, source_target_pairs={{0,4},{1,5},{2,6},{3,7},{4,0},{5,1},{6,2},{7,3},{8,12},{9,13},{10,... | collective-permute-start | bytes 147464 | tf_op jit(solution)/shard_map/ppermute | solution.py:617
  41.4 6.8 %collective-permute-start.12 = (f32[32,384]{1,0:T(8,128)S(1)}, f32[32,384]{1,0:T(8,128)S(1)}, u32[]{:S(2)}, u32[]{:S(2)}) collective-permute-start(f32[32,384]{1,0:T(8,128)S(1)} %add.30), channel_id=1, source_target_pairs={{0,6},{1,7},{2,4},{3,5},{4,2},{5,3},{6,0},{7,1},{8,14},{9,15},{10,... | collective-permute-start | bytes 147464 | tf_op jit(solution)/shard_map/ppermute | solution.py:617

commit v4 on v3

--- a/solution.py
+++ b/solution.py
@@ -493,6 +493,35 @@
         spread_ref[i] = jnp.broadcast_to(column, (channels, points))
 
 
+def message_kernel(ids_ref, sums_ref, other_ref, rest_ref, *outs):
+    *outs, total_ref = outs
+    total_ref[...] = sums_ref[...] + other_ref[...]
+    tiles, size = total_ref.shape
+    points = size // 3
+    pressure = pressures_of(total_ref[...], rest_ref)
+    for i, out in enumerate(outs):
+        owner = ids_ref[2] - ids_ref[0] + (ids_ref[0] ^ (2 * i))
+        source = total_ref[pl.ds(owner, 1), :]
+        out[:tiles] = pressure
+        out[tiles:] = jnp.concatenate(
+            [source[:, :points], source[:, points : 2 * points], jnp.zeros((6, points), f32)], axis=0
+        )
+
+
+def messages(ids, sums, other, rest, count):
+    tiles, size = sums.shape
+    return pl.pallas_call(
+        message_kernel,
+        in_specs=[SMEM] + [VMEM] * 3,
+        out_specs=[VMEM] * count,
+        out_shape=[in_vmem(tiles + 8, size // 3)] * count,
+        scratch_shapes=[pltpu.VMEM(sums.shape, f32)],
+        compiler_params=SMALL,
+        cost_estimate=cost(1e3, 1e3),
+        name="messages",
+    )(ids, pinned(sums), pinned(other), pinned(rest))
+
+
 def pressures_of(sums, rest_ref):
     points = sums.shape[1] // 3
     pressure = sums[:, 2 * points :]
@@ -539,13 +568,14 @@
 
 
 def last_kernel(
-    ids_ref, cells_ref, _, hit_ref, sums_ref, rest_ref, spot_ref, seg_ref, density_ref, spread_ref,
+    cells_ref, _, hit_ref, sums_ref, spot_ref, seg_ref, density_ref, spread_ref,
     out_hbm, drifted_hbm, done, back_ref, moved, sem,
 ):
     points = spot_ref.shape[1]
     rows, cols, depth = done.shape
+    tiles = hit_ref.shape[1]
     last = out_hbm.shape[0] - 1
-    back_ref[...] = sum(dot(hit_ref[...], p) for p in parts_of(pressures_of(sums_ref[...], rest_ref), 3))
+    back_ref[...] = sum(dot(hit_ref[...], p) for p in parts_of(sums_ref[:tiles], 3))
     copies = []
     size = 2 * CHUNK
     for first in range(0, rows, size):
@@ -556,15 +586,43 @@
         done[here] = cells + nudge_rate * (returned - cells)
         copies.append(pltpu.make_async_copy(done.at[here], out_hbm.at[last, here], sem.at[len(copies)]))
         copies[-1].start()
-    source = sums_ref[pl.ds(ids_ref[2], 1), :]
     density = density_ref[0] + inner_step * (
-        spread_ref[1] * source[:, :points] + spread_ref[2] * source[:, points : 2 * points]
+        spread_ref[1] * sums_ref[tiles : tiles + 1] + spread_ref[2] * sums_ref[tiles + 1 : tiles + 2]
     )
     moved[0] = drifted(density, spread_ref[0])
     copies.append(pltpu.make_async_copy(moved, drifted_hbm, sem.at[len(copies)]))
     copies[-1].start()
     for copy in copies:
         copy.wait()
+
+
+def message_kernel(ids_ref, sums_ref, other_ref, rest_ref, *outs):
+    *outs, total_ref = outs
+    total_ref[...] = sums_ref[...] + other_ref[...]
+    tiles, size = total_ref.shape
+    points = size // 3
+    pressure = pressures_of(total_ref[...], rest_ref)
+    for i, out in enumerate(outs):
+        owner = ids_ref[2] - ids_ref[0] + (ids_ref[0] ^ (2 * i))
+        source = total_ref[pl.ds(owner, 1), :]
+        out[:tiles] = pressure
+        out[tiles:] = jnp.concatenate(
+            [source[:, :points], source[:, points : 2 * points], jnp.zeros((6, points), f32)], axis=0
+        )
+
+
+def messages(ids, sums, other, rest, count):
+    tiles, size = sums.shape
+    return pl.pallas_call(
+        message_kernel,
+        in_specs=[SMEM] + [VMEM] * 3,
+        out_specs=[VMEM] * count,
+        out_shape=[in_vmem(tiles + 8, size // 3)] * count,
+        scratch_shapes=[pltpu.VMEM(sums.shape, f32)],
+        compiler_params=SMALL,
+        cost_estimate=cost(1e3, 1e3),
+        name="messages",
+    )(ids, pinned(sums), pinned(other), pinned(rest))
 
 
 def pressures_of(sums, rest_ref):
@@ -593,14 +651,14 @@
     )(ids, *pins)
 
 
-def finish_last(ids, cells, most, hits, sums, rest, spot, seg, density, spread):
+def finish_last(cells, most, hits, sums, spot, seg, density, spread):
     rows, cols, depth = cells.shape
     return pl.pallas_call(
         last_kernel,
-        in_specs=[SMEM, VMEM, HBM] + [VMEM] * 7,
+        in_specs=[VMEM, HBM] + [VMEM] * 6,
         out_specs=[HBM, HBM],
         out_shape=[jax.ShapeDtypeStruct(most.shape, f32), jax.ShapeDtypeStruct(density.shape, f32)],
-        input_output_aliases={2: 0},
+        input_output_aliases={1: 0},
         scratch_shapes=[
             pltpu.VMEM(cells.shape, f32),
             pltpu.VMEM((rows, spot.shape[1]), f32),
@@ -610,7 +668,7 @@
         compiler_params=SMALL,
         cost_estimate=cost(1e3, 1e3),
         name="finish_last",
-    )(ids, pinned(cells), most, hits, pinned(sums), pinned(rest), spot, seg, density, pinned(spread))
+    )(pinned(cells), most, hits, pinned(sums), spot, seg, density, pinned(spread))
 
 
 def swap(x, axis, bit):
@@ -666,13 +724,13 @@
     part = radial_update(tuple(range(1, fields - 1)), cells, turned, part, wave_speed)
     part, sums = lax.optimization_barrier((part, sums))
     sums = sum(others, sums)
-    sums = sums + swap(sums, "lon", 1)
-    others = [swap(sums, "lon", step) for step in range(2, n_lon, 2)]
+    sums, *shares = messages(ids, sums, swap(sums, "lon", 1), rest, n_lon // 2)
+    others = [swap(share, "lon", 2 * i + 2) for i, share in enumerate(shares)]
     most, last = finish_most(ids, part, (near_a, near_b, far), same, (cross_0, cross_1))
     sums, most = lax.optimization_barrier((sums, most))
     sums = sum(others, sums)
     done, density = finish_last(
-        ids, last, most, hits_back, sums, rest, jnp.asarray(spot), jnp.asarray(seg.T, bf16), phase_density, spread
+        last, most, hits_back, sums, jnp.asarray(spot), jnp.asarray(seg.T, bf16), phase_density, spread
     )
     return done, density
 

time: 50.6 us -> 49.7 us (0.982)
  waiting for transfers between devices: 3.01 us -> 2.11 us
    ppermute x1, waiting for transfers between devices: 1.5 us -> 0.86 us  [per_device(): cross_1 = lax.ppermute(crosses[1], 'lon', across)]
    pallas_call x1 -> x2, Pallas kernels: 2.23 us -> 2.22 us  [the longest x1 1.58 us: finish_last(): pl.pallas_call(last_kernel, in_specs=[VMEM, HBM] + [VMEM] * 6, out_specs=...]
  transfers between devices with their start and end apart: 13 -> 13, of which waited for: 3 -> 2; matrix products, arithmetic and copies ran while one was open for 0% -> 0% of each run, Pallas kernels for 43% -> 45%
where the time goes in v4:
time: 49.7 us; the launch traced here: 49.5 us
  Pallas kernels  27.7 us (56%)
  starting transfers between devices  18.4 us (37%)
  waiting for transfers between devices  2.11 us (4%)
  between operations  0.99 us (2%)
    ppermute x10, starting transfers between devices, swap(): lax.ppermute(x, axis, [(i, i ^ bit) for i in range(lax.axis_size(axis))])  13 us
    pallas_call x1, Pallas kernels, local_update(): pl.pallas_call(local_kernel, in_specs=[SMEM, HBM] + [VMEM] * 7, out_specs...  9.58 us
    ppermute x1, starting transfers between devices, per_device(): cross_0 = lax.ppermute(crosses[0], 'lon', across)  4.71 us
    pallas_call x1, Pallas kernels, radial_update(): pl.pallas_call(functools.partial(radial_kernel, fields), in_specs=[SMEM]...  4.47 us
    pallas_call x1, Pallas kernels, finish_most(): pl.pallas_call(most_kernel, in_specs=[SMEM] + [VMEM] * len(pins), out_spe...  3.81 us
    pallas_call x1, Pallas kernels, lon_edges(): pl.pallas_call(lon_edge_kernel, in_specs=[SMEM] * 3 + [HBM] * 4, out_spec...  3.77 us
    pallas_call x1, Pallas kernels, tile_sums(): pl.pallas_call(tile_sum_kernel, in_specs=[SMEM] + [VMEM] * 10, out_specs=...  2.36 us
    pallas_call x1, Pallas kernels, finish_last(): pl.pallas_call(last_kernel, in_specs=[VMEM, HBM] + [VMEM] * 6, out_specs=...  1.58 us
  transfers between devices with their start and end apart: 13, of which 2 were waited for; matrix products, arithmetic and copies ran while one was open for 0% of the time, Pallas kernels for 45%

profile of v4, /device:TPU:0, one launch (start us, length us, event | category | flops | bytes accessed | tf_op | source)
XLA Modules:
  0.0 49.5 jit_solution(6809906199214148444)
XLA Ops:
  0.6 0.0 copy-start.2
  0.6 0.0 copy-start.3
  0.7 0.0 copy-start.7
  0.7 0.0 copy-start.8
  0.7 0.0 copy-start.4
  0.7 0.0 copy-start.10
  0.7 0.0 copy-start.12
  0.7 0.0 copy-start.11
  0.7 0.0 copy-start.15
  0.7 0.0 copy-start.14
  0.7 0.0 copy-start.13
  0.8 0.0 copy-start.1
  0.8 0.0 copy-start
  0.8 0.0 copy-start.6
  0.8 0.0 copy-start.9
  0.8 3.8 %lon_edges.1 = (f32[8,6,16,256]{3,2,1,0:T(8,128)S(1)}, s32[3]{0:T(128)S(1)}, f32[64,24,256]{2,1,0:T(8,128)S(1)}, f32[64,8,256]{2,1,0:T(8,128)S(1)}, f32[64,16,256]{2,1,0:T(8,128)S(1)}) custom-call(s32[1]{0:T(128)} %bitcast.lon_ref, s32[1]{0:T(128)} %bitcast.1.rad_ref, s32[1]{0:T(128)} %bitcast.2.place_ref, f32[8,64,16,256]{3,2,1,0:T(8,128)} %state_hbm.3, ...), custom_call_target="tpu_custom_call" | custom-call | flops 1000 | bytes 1000 | tf_op jit(solution)/shard_map/lon_edges/pallas_call | solution.py:164
  4.6 0.5 %collective-permute-start = (f32[64,24,256]{2,1,0:T(8,128)S(1)}, f32[64,24,256]{2,1,0:T(8,128)S(1)}, u32[]{:S(2)}, u32[]{:S(2)}) collective-permute-start(f32[64,24,256]{2,1,0:T(8,128)S(1)} %get-tuple-element.35), channel_id=1, source_target_pairs={{0,1},{1,0},{2,3},{3,2},{4,5},{5,4},{6,7},{7,6},{8,9},{9,8},{10,11... | collective-permute-start | bytes 4718600 | tf_op jit(solution)/shard_map/ppermute | solution.py:675
  5.1 4.7 %collective-permute-start.1 = (f32[64,8,256]{2,1,0:T(8,128)S(1)}, f32[64,8,256]{2,1,0:T(8,128)S(1)}, u32[]{:S(2)}, u32[]{:S(2)}) collective-permute-start(f32[64,8,256]{2,1,0:T(8,128)S(1)} %get-tuple-element.36), channel_id=1, source_target_pairs={{0,7},{1,2},{2,1},{3,4},{4,3},{5,6},{6,5},{7,0},{8,15},{9,10},{10,... | collective-permute-start | bytes 1572872 | tf_op jit(solution)/shard_map/ppermute | solution.py:698
  9.8 0.0 collective-permute-start.5
  9.9 0.0 copy-done.2
  9.9 0.0 copy-done.3
  9.9 0.0 copy-done.4
  9.9 0.0 copy-done.10
  9.9 1.5 %rad_edges.1 = (f32[2,3,16,256]{3,2,1,0:T(8,128)S(1)}, f32[6,3,16,256]{3,2,1,0:T(8,128)S(1)}, f32[8,3,16,256]{3,2,1,0:T(8,128)S(1)}) custom-call(s32[3]{0:T(128)S(1)} %get-tuple-element.29.ids_ref, f32[2]{0:T(128)S(1)} %copy-done.10, f32[8,6,16,256]{3,2,1,0:T(8,128)S(1)} %get-tuple-element.33.rim_ref, f32[2,8,8]{2,1,0:T(8,128)S(1)} %copy-done.4, ...), custom_call_target="tpu_custom_call" | custom-call | flops 1000 | bytes 1000 | tf_op jit(solution)/shard_map/rad_edges/pallas_call | solution.py:235
  11.4 0.7 %collective-permute-start.3 = (f32[8,3,16,256]{3,2,1,0:T(8,128)S(1)}, f32[8,3,16,256]{3,2,1,0:T(8,128)S(1)}, u32[]{:S(2)}, u32[]{:S(2)}) collective-permute-start(f32[8,3,16,256]{3,2,1,0:T(8,128)S(1)} %get-tuple-element.38), channel_id=1, source_target_pairs={{8,16},{16,8},{9,17},{17,9},{10,18},{18,10},{11,19},{19,11},{12,20... | collective-permute-start | bytes 1179656 | tf_op jit(solution)/shard_map/ppermute | solution.py:704
  12.1 4.3 %collective-permute-start.2 = (f32[2,3,16,256]{3,2,1,0:T(8,128)S(1)}, f32[2,3,16,256]{3,2,1,0:T(8,128)S(1)}, u32[]{:S(2)}, u32[]{:S(2)}) collective-permute-start(f32[2,3,16,256]{3,2,1,0:T(8,128)S(1)} %get-tuple-element.37), channel_id=1, source_target_pairs={{0,8},{8,0},{16,24},{24,16},{1,9},{9,1},{17,25},{25,17},{2,10},{10... | collective-permute-start | bytes 294920 | tf_op jit(solution)/shard_map/ppermute | solution.py:675
  16.4 0.0 copy-done.12
  16.4 0.0 copy-done.11
  16.4 0.1 compare_convert_fusion.1.hit_ref
  16.4 0.0 copy-done.15
  16.4 0.0 copy-done.14
  16.4 0.0 copy-done.13
  16.5 9.6 %local_update.1 = (f32[8,64,16,256]{3,2,1,0:T(8,128)S(1)}, f32[70,128,256]{2,1,0:T(8,128)S(1)}, f32[8,70,16,256]{3,2,1,0:T(8,128)S(1)}, f32[16,128]{1,0:T(8,128)S(1)}, f32[3,200,128]{2,1,0:T(8,128)S(1)}) custom-call(f32[2]{0:T(128)S(1)} %copy-done.10, f32[8,64,16,256]{3,2,1,0:T(8,128)} %state_hbm.3, f32[2,8,8]{2,1,0:T(8,128)S(1)} %copy-done.4, ...), custom_call_target="tpu_custom_call" | custom-call | flops 1000 | bytes 1000 | tf_op jit(solution)/shard_map/local_update/pallas_call | solution.py:338
  26.1 0.0 collective-permute-done.2.near_ref.refs_0_
  26.1 0.0 collective-permute-done.3.far_ref.refs_2_
  26.1 0.0 collective-permute-done.1.cross_ref.refs_4_
  26.1 0.0 collective-permute-done.same_ref.refs_3_
  26.1 0.0 copy-done
  26.1 0.0 copy-done.6
  26.1 0.0 copy-done.9
  26.2 2.4 %tile_sums.1 = f32[32,384]{1,0:T(8,128)S(1)} custom-call(s32[3]{0:T(128)S(1)} %get-tuple-element.29.ids_ref, f32[8,64,16,256]{3,2,1,0:T(8,128)S(1)} %get-tuple-element.41.part_ref._, f32[64,16,256]{2,1,0:T(8,128)S(1)} %copy-done, f32[64,24,256]{2,1,0:T(8,128)S(1)} %collective-permute-done.same_ref.refs_3_, ...), custom_call_target="tpu_custom_call" | custom-call | flops 1000 | bytes 1000 | tf_op jit(solution)/shard_map/tile_sums/pallas_call | solution.py:455
  28.5 0.1 collective-permute-start.6
  28.7 1.9 %collective-permute-start.7 = (f32[32,384]{1,0:T(8,128)S(1)}, f32[32,384]{1,0:T(8,128)S(1)}, u32[]{:S(2)}, u32[]{:S(2)}) collective-permute-start(f32[32,384]{1,0:T(8,128)S(1)} %tile_sums.1), channel_id=1, source_target_pairs={{0,16},{8,24},{16,0},{24,8},{1,17},{9,25},{17,1},{25,9},{2,18},{10... | collective-permute-start | bytes 147464 | tf_op jit(solution)/shard_map/ppermute | solution.py:675
  30.5 1.5 %collective-permute-start.8 = (f32[32,384]{1,0:T(8,128)S(1)}, f32[32,384]{1,0:T(8,128)S(1)}, u32[]{:S(2)}, u32[]{:S(2)}) collective-permute-start(f32[32,384]{1,0:T(8,128)S(1)} %tile_sums.1), channel_id=1, source_target_pairs={{0,24},{8,16},{16,8},{24,0},{1,25},{9,17},{17,9},{25,1},{2,26},{10... | collective-permute-start | bytes 147464 | tf_op jit(solution)/shard_map/ppermute | solution.py:675
  32.0 4.5 %radial_update.1.part_ref = f32[8,64,16,256]{3,2,1,0:T(8,128)S(1)} custom-call(f32[2]{0:T(128)S(1)} %copy-done.10, f32[8,70,16,256]{3,2,1,0:T(8,128)S(1)} %get-tuple-element.30.cells, f32[70,128,256]{2,1,0:T(8,128)S(1)} %get-tuple-element.31.turned, f32[8,64,16,256]{3,2,1,0:T(8,128)S(1)} %get-tuple-element.41.part_ref._), custom_call_target="tpu_custom_call", output_to_operand_aliasing={{}: (3, {})} | custom-call | flops 100000000 | bytes 6000000 | tf_op jit(solution)/shard_map/radial_update/pallas_call | solution.py:368
  36.5 0.0 copy-start.5
  36.5 0.2 collective-permute-start.4
  36.7 0.0 collective-permute-done.6
  36.7 0.0 collective-permute-done.7
  36.7 0.0 collective-permute-done.8
  36.7 0.1 collective-permute-start.9
  36.8 1.2 %collective-permute-done.9.other_ref = f32[32,384]{1,0:T(8,128)S(1)} collective-permute-done((f32[32,384]{1,0:T(8,128)S(1)}, f32[32,384]{1,0:T(8,128)S(1)}, u32[]{:S(2)}, u32[]{:S(2)}) %collective-permute-start.9) | collective-permute-done | bytes 49184 | tf_op jit(solution)/shard_map/ppermute | solution.py:675
  38.0 0.6 %messages.1 = (f32[40,128]{1,0:T(8,128)S(1)}, f32[40,128]{1,0:T(8,128)S(1)}, f32[40,128]{1,0:T(8,128)S(1)}, f32[40,128]{1,0:T(8,128)S(1)}) custom-call(s32[3]{0:T(128)S(1)} %get-tuple-element.29.ids_ref, f32[32,384]{1,0:T(8,128)S(1)} %add_add_fusion.sums_ref, f32[32,384]{1,0:T(8,128)S(1)} %collective-permute-done.9.other_ref, ...), custom_call_target="tpu_custom_call" | custom-call | flops 1000 | bytes 1000 | tf_op jit(solution)/shard_map/messages/pallas_call | solution.py:616
  38.7 1.3 %collective-permute-start.10 = (f32[40,128]{1,0:T(8,128)S(1)}, f32[40,128]{1,0:T(8,128)S(1)}, u32[]{:S(2)}, u32[]{:S(2)}) collective-permute-start(f32[40,128]{1,0:T(8,128)S(1)} %get-tuple-element.52), channel_id=1, source_target_pairs={{0,2},{1,3},{2,0},{3,1},{4,6},{5,7},{6,4},{7,5},{8,10},{9,11},{10,... | collective-permute-start | bytes 61448 | tf_op jit(solution)/shard_map/ppermute | solution.py:675
  40.0 2.0 %collective-permute-start.11 = (f32[40,128]{1,0:T(8,128)S(1)}, f32[40,128]{1,0:T(8,128)S(1)}, u32[]{:S(2)}, u32[]{:S(2)}) collective-permute-start(f32[40,128]{1,0:T(8,128)S(1)} %get-tuple-element.53), channel_id=1, source_target_pairs={{0,4},{1,5},{2,6},{3,7},{4,0},{5,1},{6,2},{7,3},{8,12},{9,13},{10,... | collective-permute-start | bytes 61448 | tf_op jit(solution)/shard_map/ppermute | solution.py:675
  42.0 1.1 %collective-permute-start.12 = (f32[40,128]{1,0:T(8,128)S(1)}, f32[40,128]{1,0:T(8,128)S(1)}, u32[]{:S(2)}, u32[]{:S(2)}) collective-permute-start(f32[40,128]{1,0:T(8,128)S(1)} %get-tuple-element.54), channel_id=1, source_target_pairs={{0,6},{1,7},{2,4},{3,5},{4,2},{5,3},{6,0},{7,1},{8,14},{9,15},{10,... | collective-permute-start | bytes 61448 | tf_op jit(solution)/shard_map/ppermute | solution.py:675
  43.1 0.1 compare_convert_fusion.hit_ref
  43.2 0.9 %collective-permute-done.5.refs_5_ = f32[64,16,256]{2,1,0:T(8,128)S(1)} collective-permute-done((f32[64,16,256]{2,1,0:T(8,128)S(1)}, f32[64,16,256]{2,1,0:T(8,128)S(1)}, u32[]{:S(2)}, u32[]{:S(2)}) %collective-permute-start.5) | collective-permute-done | bytes 1048608 | tf_op jit(solution)/shard_map/ppermute | solution.py:700
  44.1 0.0 collective-permute-done.4.refs_1_
  44.1 3.8 %finish_most.1 = (f32[8,64,16,256]{3,2,1,0:T(8,128)}, f32[64,16,256]{2,1,0:T(8,128)S(1)}) custom-call(s32[3]{0:T(128)S(1)} %get-tuple-element.29.ids_ref, f32[8,64,16,256]{3,2,1,0:T(8,128)S(1)} %radial_update.1.part_ref, f32[2,3,16,256]{3,2,1,0:T(8,128)S(1)} %collective-permute-done.2.near_ref.refs_0_, f32[6,3,16,256]{3,2,1,0:T(8,128)S(1)} %collective-permute-done.4.refs_1_, ...), custom_call_target="tpu_custom_call" | custom-call | flops 100000000 | bytes 16000000 | tf_op jit(solution)/shard_map/finish_most/pallas_call | solution.py:642
  47.9 0.0 collective-permute-done.10
  47.9 0.0 collective-permute-done.11
  47.9 0.0 collective-permute-done.12
  48.0 1.6 %finish_last.1 = (f32[8,64,16,256]{3,2,1,0:T(8,128)}, f32[1,200,128]{2,1,0:T(8,128)}) custom-call(f32[64,16,256]{2,1,0:T(8,128)S(1)} %get-tuple-element.46.cells_ref, f32[8,64,16,256]{3,2,1,0:T(8,128)} %get-tuple-element.50._, bf16[64,32]{1,0:T(8,128)(2,1)S(1)} %compare_convert_fusion.hit_ref, ...), custom_call_target="tpu_custom_call", output_to_operand_aliasing={{0}: (1, {})} | custom-call | flops 1000 | bytes 1000 | tf_op jit(solution)/shard_map/finish_last/pallas_call | solution.py:656
  (7 shorter events, 0.0 us)
Async XLA Ops:
  0.6 9.2 %copy-start.2 = (f32[128,8]{1,0:T(8,128)S(1)}, f32[128,8]{1,0:T(8,128)}, u32[]{:S(2)}) copy-start(f32[128,8]{1,0:T(8,128)} %constant.30.clone.pick_ref) | copy-start | bytes 12292
  0.6 9.2 %copy-start.3 = (f32[128,128]{1,0:T(8,128)S(1)}, f32[128,128]{1,0:T(8,128)}, u32[]{:S(2)}) copy-start(f32[128,128]{1,0:T(8,128)} %constant.31.clone.same_ref) | copy-start | bytes 196612
  0.7 15.8 %copy-start.7 = (f32[128,128]{1,0:T(8,128)S(1)}, f32[128,128]{1,0:T(8,128)}, u32[]{:S(2)}) copy-start(f32[128,128]{1,0:T(8,128)} %constant.32.clone.sum_ref) | copy-start | bytes 196612
  0.7 15.8 %copy-start.8 = (f32[128,128]{1,0:T(8,128)S(1)}, f32[128,128]{1,0:T(8,128)}, u32[]{:S(2)}) copy-start(f32[128,128]{1,0:T(8,128)} %constant.33.clone.gap_ref) | copy-start | bytes 196612
  0.7 9.2 %copy-start.4 = (f32[2,8,8]{2,1,0:T(8,128)S(1)}, f32[2,8,8]{2,1,0:T(8,128)}, u32[]{:S(2)}) copy-start(f32[2,8,8]{2,1,0:T(8,128)} %matrix_ref.3) | copy-start | bytes 1540
  0.7 9.2 %copy-start.10 = (f32[2]{0:T(128)S(1)}, f32[2]{0:T(128)}, u32[]{:S(2)}) copy-start(f32[2]{0:T(128)} %speed_ref.5) | copy-start | bytes 28
  0.7 15.6 %copy-start.12 = (s32[1,64,1]{1,2,0:T(1,128)S(1)}, s32[1,64,1]{1,2,0:T(1,128)}, u32[]{:S(2)}) copy-start(s32[1,64,1]{1,2,0:T(1,128)} %param.24) | copy-start | bytes 772
  0.7 15.6 %copy-start.11 = (s32[32]{0:T(128)S(1)}, s32[32]{0:T(128)}, u32[]{:S(2)}) copy-start(s32[32]{0:T(128)} %param.25) | copy-start | bytes 388
  0.7 15.7 %copy-start.15 = (f32[200]{0:T(256)S(1)}, f32[200]{0:T(256)}, u32[]{:S(2)}) copy-start(f32[200]{0:T(256)} %param.28) | copy-start | bytes 2404
  0.7 15.7 %copy-start.14 = (f32[200]{0:T(256)S(1)}, f32[200]{0:T(256)}, u32[]{:S(2)}) copy-start(f32[200]{0:T(256)} %param.29) | copy-start | bytes 2404
  0.7 15.7 %copy-start.13 = (f32[2,200]{1,0:T(2,128)S(1)}, f32[2,200]{1,0:T(2,128)}, u32[]{:S(2)}) copy-start(f32[2,200]{1,0:T(2,128)} %param.27) | copy-start | bytes 4804
  0.8 15.7 %copy-start.1 = (f32[1,200,128]{2,1,0:T(8,128)S(1)}, f32[1,200,128]{2,1,0:T(8,128)}, u32[]{:S(2)}) copy-start(f32[1,200,128]{2,1,0:T(8,128)} %density_ref.3) | copy-start | bytes 307204
  0.8 25.4 %copy-start = (f32[64,16,256]{2,1,0:T(8,128)S(1)}, f32[64,16,256]{2,1,0:T(8,128)}, u32[]{:S(2)}) copy-start(f32[64,16,256]{2,1,0:T(8,128)} %vol_ref.1) | copy-start | bytes 3145732
  0.8 25.4 %copy-start.6 = (bf16[256,128]{1,0:T(8,128)(2,1)S(1)}, bf16[256,128]{1,0:T(8,128)(2,1)}, u32[]{:S(2)}) copy-start(bf16[256,128]{1,0:T(8,128)(2,1)} %constant.34.clone.seg_ref) | copy-start | bytes 196612
  0.8 25.4 %copy-start.9 = (f32[16,128]{1,0:T(8,128)S(1)}, f32[16,128]{1,0:T(8,128)}, u32[]{:S(2)}) copy-start(f32[16,128]{1,0:T(8,128)} %constant.35.clone.spot_ref) | copy-start | bytes 24580
  4.6 21.5 %collective-permute-start = (f32[64,24,256]{2,1,0:T(8,128)S(1)}, f32[64,24,256]{2,1,0:T(8,128)S(1)}, u32[]{:S(2)}, u32[]{:S(2)}) collective-permute-start(f32[64,24,256]{2,1,0:T(8,128)S(1)} %get-tuple-element.35), channel_id=1, source_target_pairs={{0,1},{1,0},{2,3},{3,2},{4,5},{5,4},{6,7},{7,6},{8,9},{9,8},{10,11... | collective-permute-start | bytes 4718600 | tf_op jit(solution)/shard_map/ppermute | solution.py:675
  5.1 21.0 %collective-permute-start.1 = (f32[64,8,256]{2,1,0:T(8,128)S(1)}, f32[64,8,256]{2,1,0:T(8,128)S(1)}, u32[]{:S(2)}, u32[]{:S(2)}) collective-permute-start(f32[64,8,256]{2,1,0:T(8,128)S(1)} %get-tuple-element.36), channel_id=1, source_target_pairs={{0,7},{1,2},{2,1},{3,4},{4,3},{5,6},{6,5},{7,0},{8,15},{9,10},{10,... | collective-permute-start | bytes 1572872 | tf_op jit(solution)/shard_map/ppermute | solution.py:698
  9.8 34.3 %collective-permute-start.5 = (f32[64,16,256]{2,1,0:T(8,128)S(1)}, f32[64,16,256]{2,1,0:T(8,128)S(1)}, u32[]{:S(2)}, u32[]{:S(2)}) collective-permute-start(f32[64,16,256]{2,1,0:T(8,128)S(1)} %get-tuple-element.45), channel_id=1, source_target_pairs={{0,7},{1,2},{2,1},{3,4},{4,3},{5,6},{6,5},{7,0},{8,15},{9,10},{10,... | collective-permute-start | bytes 3145736 | tf_op jit(solution)/shard_map/ppermute | solution.py:700
  11.4 14.7 %collective-permute-start.3 = (f32[8,3,16,256]{3,2,1,0:T(8,128)S(1)}, f32[8,3,16,256]{3,2,1,0:T(8,128)S(1)}, u32[]{:S(2)}, u32[]{:S(2)}) collective-permute-start(f32[8,3,16,256]{3,2,1,0:T(8,128)S(1)} %get-tuple-element.38), channel_id=1, source_target_pairs={{8,16},{16,8},{9,17},{17,9},{10,18},{18,10},{11,19},{19,11},{12,20... | collective-permute-start | bytes 1179656 | tf_op jit(solution)/shard_map/ppermute | solution.py:704
  12.1 14.0 %collective-permute-start.2 = (f32[2,3,16,256]{3,2,1,0:T(8,128)S(1)}, f32[2,3,16,256]{3,2,1,0:T(8,128)S(1)}, u32[]{:S(2)}, u32[]{:S(2)}) collective-permute-start(f32[2,3,16,256]{3,2,1,0:T(8,128)S(1)} %get-tuple-element.37), channel_id=1, source_target_pairs={{0,8},{8,0},{16,24},{24,16},{1,9},{9,1},{17,25},{25,17},{2,10},{10... | collective-permute-start | bytes 294920 | tf_op jit(solution)/shard_map/ppermute | solution.py:675
  28.5 8.2 %collective-permute-start.6 = (f32[32,384]{1,0:T(8,128)S(1)}, f32[32,384]{1,0:T(8,128)S(1)}, u32[]{:S(2)}, u32[]{:S(2)}) collective-permute-start(f32[32,384]{1,0:T(8,128)S(1)} %tile_sums.1), channel_id=1, source_target_pairs={{0,8},{8,0},{16,24},{24,16},{1,9},{9,1},{17,25},{25,17},{2,10},{10... | collective-permute-start | bytes 147464 | tf_op jit(solution)/shard_map/ppermute | solution.py:675
  28.7 8.1 %collective-permute-start.7 = (f32[32,384]{1,0:T(8,128)S(1)}, f32[32,384]{1,0:T(8,128)S(1)}, u32[]{:S(2)}, u32[]{:S(2)}) collective-permute-start(f32[32,384]{1,0:T(8,128)S(1)} %tile_sums.1), channel_id=1, source_target_pairs={{0,16},{8,24},{16,0},{24,8},{1,17},{9,25},{17,1},{25,9},{2,18},{10... | collective-permute-start | bytes 147464 | tf_op jit(solution)/shard_map/ppermute | solution.py:675
  30.5 6.2 %collective-permute-start.8 = (f32[32,384]{1,0:T(8,128)S(1)}, f32[32,384]{1,0:T(8,128)S(1)}, u32[]{:S(2)}, u32[]{:S(2)}) collective-permute-start(f32[32,384]{1,0:T(8,128)S(1)} %tile_sums.1), channel_id=1, source_target_pairs={{0,24},{8,16},{16,8},{24,0},{1,25},{9,17},{17,9},{25,1},{2,26},{10... | collective-permute-start | bytes 147464 | tf_op jit(solution)/shard_map/ppermute | solution.py:675
  36.5 11.4 %copy-start.5 = (bf16[128,256]{1,0:T(8,128)(2,1)S(1)}, bf16[128,256]{1,0:T(8,128)(2,1)}, u32[]{:S(2)}) copy-start(bf16[128,256]{1,0:T(8,128)(2,1)} %constant.36.clone.seg_ref) | copy-start | bytes 196612
  36.5 7.6 %collective-permute-start.4 = (f32[6,3,16,256]{3,2,1,0:T(8,128)S(1)}, f32[6,3,16,256]{3,2,1,0:T(8,128)S(1)}, u32[]{:S(2)}, u32[]{:S(2)}) collective-permute-start(f32[6,3,16,256]{3,2,1,0:T(8,128)S(1)} %get-tuple-element.44), channel_id=1, source_target_pairs={{0,8},{8,0},{16,24},{24,16},{1,9},{9,1},{17,25},{25,17},{2,10},{10... | collective-permute-start | bytes 884744 | tf_op jit(solution)/shard_map/ppermute | solution.py:675
  36.7 1.3 %collective-permute-start.9 = (f32[32,384]{1,0:T(8,128)S(1)}, f32[32,384]{1,0:T(8,128)S(1)}, u32[]{:S(2)}, u32[]{:S(2)}) collective-permute-start(f32[32,384]{1,0:T(8,128)S(1)} %add_add_fusion.sums_ref), channel_id=1, source_target_pairs={{0,1},{1,0},{2,3},{3,2},{4,5},{5,4},{6,7},{7,6},{8,9},{9,8},{10,11... | collective-permute-start | bytes 147464 | tf_op jit(solution)/shard_map/ppermute | solution.py:675
  38.7 9.2 %collective-permute-start.10 = (f32[40,128]{1,0:T(8,128)S(1)}, f32[40,128]{1,0:T(8,128)S(1)}, u32[]{:S(2)}, u32[]{:S(2)}) collective-permute-start(f32[40,128]{1,0:T(8,128)S(1)} %get-tuple-element.52), channel_id=1, source_target_pairs={{0,2},{1,3},{2,0},{3,1},{4,6},{5,7},{6,4},{7,5},{8,10},{9,11},{10,... | collective-permute-start | bytes 61448 | tf_op jit(solution)/shard_map/ppermute | solution.py:675
  40.0 7.9 %collective-permute-start.11 = (f32[40,128]{1,0:T(8,128)S(1)}, f32[40,128]{1,0:T(8,128)S(1)}, u32[]{:S(2)}, u32[]{:S(2)}) collective-permute-start(f32[40,128]{1,0:T(8,128)S(1)} %get-tuple-element.53), channel_id=1, source_target_pairs={{0,4},{1,5},{2,6},{3,7},{4,0},{5,1},{6,2},{7,3},{8,12},{9,13},{10,... | collective-permute-start | bytes 61448 | tf_op jit(solution)/shard_map/ppermute | solution.py:675
  42.0 5.9 %collective-permute-start.12 = (f32[40,128]{1,0:T(8,128)S(1)}, f32[40,128]{1,0:T(8,128)S(1)}, u32[]{:S(2)}, u32[]{:S(2)}) collective-permute-start(f32[40,128]{1,0:T(8,128)S(1)} %get-tuple-element.54), channel_id=1, source_target_pairs={{0,6},{1,7},{2,4},{3,5},{4,2},{5,3},{6,0},{7,1},{8,14},{9,15},{10,... | collective-permute-start | bytes 61448 | tf_op jit(solution)/shard_map/ppermute | solution.py:675

commit v5 on v4

--- a/solution.py
+++ b/solution.py
@@ -356,25 +356,32 @@
     )
 
 
-def radial_kernel(fields, speed_ref, cells, turned, _, total):
+def radial_kernel(fields, speed_ref, ids_ref, cells, turned, near_a, far_ref, same_ref, cross_ref, _, total, out_hbm, done, sem):
+    finish_field(0, (ids_ref, near_a, None, far_ref, same_ref, cross_ref), total, done)
+    store = pltpu.make_async_copy(done, out_hbm.at[0], sem)
+    store.start()
+
     def radial(c, carry):
         add_radial(speed_ref, cells, turned, total, fields, c * CHUNK)
         return carry
 
     lax.fori_loop(0, total.shape[1] // CHUNK, radial, 0)
-
-
-def radial_update(fields, cells, turned, part, speed):
+    store.wait()
+
+
+def radial_update(fields, ids, cells, turned, part, speed, near_a, far, same, cross_0):
+    pins = [pinned(x) for x in (cells, turned, near_a, far, same, cross_0, part)]
     return pl.pallas_call(
         functools.partial(radial_kernel, fields),
-        in_specs=[SMEM] + [VMEM] * 3,
-        out_specs=VMEM,
-        out_shape=in_vmem(*part.shape),
-        input_output_aliases={3: 0},
+        in_specs=[SMEM] * 2 + [VMEM] * len(pins),
+        out_specs=[VMEM, HBM],
+        out_shape=[in_vmem(*part.shape), jax.ShapeDtypeStruct(part.shape, f32)],
+        input_output_aliases={1 + len(pins): 0},
+        scratch_shapes=[pltpu.VMEM(part.shape[1:], f32), pltpu.SemaphoreType.DMA],
         compiler_params=SMALL,
         cost_estimate=cost(1e8, 6e6),
         name="radial_update",
-    )(speed, pinned(cells), pinned(turned), pinned(part))
+    )(speed, ids, *pins)
 
 
 def placed(tiles, field, from_left):
@@ -533,7 +540,7 @@
     return pressure
 
 
-def finish_field(field, refs, part_ref, out):
+def finish_field(field, refs, part_ref, out, scale=None):
     ids_ref, near_a, near_b, far_ref, same_ref, *cross_refs = refs
     rows = 2 * CHUNK
     steps = out.shape[0] // rows
@@ -549,20 +556,21 @@
             lefts[t], rights[t] = one[0][0], one[1][0]
         near = near_a[field // last_field] if field in (0, last_field) else near_b[field - 1]
         cells = with_sides(part_ref[field, here], lefts, rights, field)
-        out[here] = with_ends(cells, i, steps, ids_ref[1], near, far_ref[field])
+        cells = with_ends(cells, i, steps, ids_ref[1], near, far_ref[field])
+        out[here] = cells if scale is None else scale * cells
         return carry
 
     lax.fori_loop(0, steps, step, 0)
 
 
 def most_kernel(ids_ref, part_ref, *refs):
-    *sides, out_hbm, last_ref, done, sem = refs
+    *sides, _, out_hbm, last_ref, done, sem = refs
     copies = []
-    for field in range(done.shape[0]):
-        finish_field(field, (ids_ref, *sides), part_ref, done.at[field])
-        copies.append(pltpu.make_async_copy(done.at[field], out_hbm.at[field], sem.at[field]))
+    for i in range(done.shape[0]):
+        finish_field(i + 1, (ids_ref, *sides), part_ref, done.at[i])
+        copies.append(pltpu.make_async_copy(done.at[i], out_hbm.at[i + 1], sem.at[i]))
         copies[-1].start()
-    finish_field(done.shape[0], (ids_ref, *sides), part_ref, last_ref)
+    finish_field(done.shape[0] + 1, (ids_ref, *sides), part_ref, last_ref, 1.0 - nudge_rate)
     for copy in copies:
         copy.wait()
 
@@ -575,15 +583,16 @@
     rows, cols, depth = done.shape
     tiles = hit_ref.shape[1]
     last = out_hbm.shape[0] - 1
-    back_ref[...] = sum(dot(hit_ref[...], p) for p in parts_of(sums_ref[:tiles], 3))
+    back = sum(dot(hit_ref[...], p) for p in parts_of(sums_ref[:tiles], 3))
+    for i, part in enumerate(parts_of(nudge_rate * back, 3)):
+        back_ref[i] = part.astype(f32)
     copies = []
     size = 2 * CHUNK
     for first in range(0, rows, size):
         here = pl.ds(first, size)
-        spread = (back_ref[here][:, None, :] * spot_ref[...][None]).reshape(-1, points)
-        returned = exact_dot(spread, seg_ref[...]).reshape(-1, cols, depth)
-        cells = cells_ref[here]
-        done[here] = cells + nudge_rate * (returned - cells)
+        spread = [(back_ref[i, here][:, None, :] * spot_ref[...][None]).reshape(-1, points) for i in range(3)]
+        returned = dot(jnp.concatenate(spread, axis=1).astype(bf16), seg_ref[...])
+        done[here] = cells_ref[here] + returned.reshape(-1, cols, depth)
         copies.append(pltpu.make_async_copy(done.at[here], out_hbm.at[last, here], sem.at[len(copies)]))
         copies[-1].start()
     density = density_ref[0] + inner_step * (
@@ -636,19 +645,20 @@
     return pressure
 
 
-def finish_most(ids, part, rad, same, crosses):
+def finish_most(ids, part, rad, same, crosses, result):
     fields, rows, cols, depth = part.shape
     pins = [pinned(x) for x in (part, *rad, same, *crosses)]
     return pl.pallas_call(
         most_kernel,
-        in_specs=[SMEM] + [VMEM] * len(pins),
+        in_specs=[SMEM] + [VMEM] * len(pins) + [HBM],
         out_specs=[HBM, VMEM],
         out_shape=[jax.ShapeDtypeStruct(part.shape, f32), in_vmem(rows, cols, depth)],
-        scratch_shapes=[pltpu.VMEM((fields - 1, rows, cols, depth), f32), pltpu.SemaphoreType.DMA((fields - 1,))],
+        input_output_aliases={1 + len(pins): 0},
+        scratch_shapes=[pltpu.VMEM((fields - 2, rows, cols, depth), f32), pltpu.SemaphoreType.DMA((fields - 2,))],
         compiler_params=LARGE,
         cost_estimate=cost(1e8, 1.6e7),
         name="finish_most",
-    )(ids, *pins)
+    )(ids, *pins, result)
 
 
 def finish_last(cells, most, hits, sums, spot, seg, density, spread):
@@ -661,7 +671,7 @@
         input_output_aliases={1: 0},
         scratch_shapes=[
             pltpu.VMEM(cells.shape, f32),
-            pltpu.VMEM((rows, spot.shape[1]), f32),
+            pltpu.VMEM((3, rows, spot.shape[1]), f32),
             pltpu.VMEM(density.shape, f32),
             pltpu.SemaphoreType.DMA((rows // (2 * CHUNK) + 1,)),
         ],
@@ -721,16 +731,18 @@
     near_b = swap(near_b, "rad", 1)
     part, sums = lax.optimization_barrier((part, sums))
     others = [swap(sums, "rad", step) for step in range(1, n_rad)]
-    part = radial_update(tuple(range(1, fields - 1)), cells, turned, part, wave_speed)
+    part, result = radial_update(
+        tuple(range(1, fields - 1)), ids, cells, turned, part, wave_speed, near_a, far, same, cross_0
+    )
     part, sums = lax.optimization_barrier((part, sums))
     sums = sum(others, sums)
     sums, *shares = messages(ids, sums, swap(sums, "lon", 1), rest, n_lon // 2)
     others = [swap(share, "lon", 2 * i + 2) for i, share in enumerate(shares)]
-    most, last = finish_most(ids, part, (near_a, near_b, far), same, (cross_0, cross_1))
+    most, last = finish_most(ids, part, (near_a, near_b, far), same, (cross_0, cross_1), result)
     sums, most = lax.optimization_barrier((sums, most))
     sums = sum(others, sums)
     done, density = finish_last(
-        last, most, hits_back, sums, jnp.asarray(spot), jnp.asarray(seg.T, bf16), phase_density, spread
+        last, most, hits_back, sums, jnp.asarray(spot), jnp.asarray(np.tile(seg.T, (3, 1)), bf16), phase_density, spread
     )
     return done, density
 

time: 49.7 us -> 49.5 us (level)
  transfers between devices with their start and end apart: 13 -> 13, of which waited for: 2 -> 3; matrix products, arithmetic and copies ran while one was open for 0% -> 0% of each run, Pallas kernels for 45% -> 46%
where the time goes in v5:
time: 49.5 us; the launch traced here: 49.3 us
  Pallas kernels  27.7 us (56%)
  starting transfers between devices  18.4 us (37%)
  waiting for transfers between devices  2.03 us (4%)
  between operations  0.97 us (2%)
    ppermute x10, starting transfers between devices, swap(): lax.ppermute(x, axis, [(i, i ^ bit) for i in range(lax.axis_size(axis))])  12.9 us
    pallas_call x1, Pallas kernels, local_update(): pl.pallas_call(local_kernel, in_specs=[SMEM, HBM] + [VMEM] * 7, out_specs...  9.64 us
    ppermute x1, starting transfers between devices, per_device(): cross_0 = lax.ppermute(crosses[0], 'lon', across)  4.71 us
    pallas_call x1, Pallas kernels, radial_update(): pl.pallas_call(functools.partial(radial_kernel, fields), in_specs=[SMEM]...  4.7 us
    pallas_call x1, Pallas kernels, lon_edges(): pl.pallas_call(lon_edge_kernel, in_specs=[SMEM] * 3 + [HBM] * 4, out_spec...  3.77 us
    pallas_call x1, Pallas kernels, finish_most(): pl.pallas_call(most_kernel, in_specs=[SMEM] + [VMEM] * len(pins) + [HBM],...  3.58 us
    pallas_call x1, Pallas kernels, tile_sums(): pl.pallas_call(tile_sum_kernel, in_specs=[SMEM] + [VMEM] * 10, out_specs=...  2.38 us
    pallas_call x1, Pallas kernels, rad_edges(): pl.pallas_call(rad_edge_kernel, in_specs=[SMEM] * 2 + [VMEM] * (2 + len(t...  1.51 us
  transfers between devices with their start and end apart: 13, of which 3 were waited for; matrix products, arithmetic and copies ran while one was open for 0% of the time, Pallas kernels for 46%

profile of v5, /device:TPU:0, one launch (start us, length us, event | category | flops | bytes accessed | tf_op | source)
XLA Modules:
  0.0 49.3 jit_solution(8673214517061958181)
XLA Ops:
  0.6 0.0 copy-start.2
  0.6 0.0 copy-start.3
  0.7 0.0 copy-start.7
  0.7 0.0 copy-start.8
  0.7 0.0 copy-start.5
  0.7 0.0 copy-start.10
  0.7 0.0 copy-start.12
  0.7 0.0 copy-start.11
  0.7 0.0 copy-start.15
  0.7 0.0 copy-start.14
  0.7 0.0 copy-start.13
  0.8 0.0 copy-start.1
  0.8 0.0 copy-start
  0.8 0.0 copy-start.6
  0.8 0.0 copy-start.9
  0.8 3.8 %lon_edges.1 = (f32[8,6,16,256]{3,2,1,0:T(8,128)S(1)}, s32[3]{0:T(128)S(1)}, f32[64,24,256]{2,1,0:T(8,128)S(1)}, f32[64,8,256]{2,1,0:T(8,128)S(1)}, f32[64,16,256]{2,1,0:T(8,128)S(1)}) custom-call(s32[1]{0:T(128)} %bitcast.lon_ref, s32[1]{0:T(128)} %bitcast.1.rad_ref, s32[1]{0:T(128)} %bitcast.2.place_ref, f32[8,64,16,256]{3,2,1,0:T(8,128)} %state_hbm.3, ...), custom_call_target="tpu_custom_call" | custom-call | flops 1000 | bytes 1000 | tf_op jit(solution)/shard_map/lon_edges/pallas_call | solution.py:164
  4.6 0.5 %collective-permute-start.2 = (f32[64,24,256]{2,1,0:T(8,128)S(1)}, f32[64,24,256]{2,1,0:T(8,128)S(1)}, u32[]{:S(2)}, u32[]{:S(2)}) collective-permute-start(f32[64,24,256]{2,1,0:T(8,128)S(1)} %get-tuple-element.37), channel_id=1, source_target_pairs={{0,1},{1,0},{2,3},{3,2},{4,5},{5,4},{6,7},{7,6},{8,9},{9,8},{10,11... | collective-permute-start | bytes 4718600 | tf_op jit(solution)/shard_map/ppermute | solution.py:685
  5.1 4.7 %collective-permute-start.3 = (f32[64,8,256]{2,1,0:T(8,128)S(1)}, f32[64,8,256]{2,1,0:T(8,128)S(1)}, u32[]{:S(2)}, u32[]{:S(2)}) collective-permute-start(f32[64,8,256]{2,1,0:T(8,128)S(1)} %get-tuple-element.38), channel_id=1, source_target_pairs={{0,7},{1,2},{2,1},{3,4},{4,3},{5,6},{6,5},{7,0},{8,15},{9,10},{10,... | collective-permute-start | bytes 1572872 | tf_op jit(solution)/shard_map/ppermute | solution.py:708
  9.8 0.0 collective-permute-start.5
  9.9 0.0 copy-done.2
  9.9 0.0 copy-done.3
  9.9 0.0 copy-done.5
  9.9 0.0 copy-done.10
  9.9 1.5 %rad_edges.1 = (f32[2,3,16,256]{3,2,1,0:T(8,128)S(1)}, f32[6,3,16,256]{3,2,1,0:T(8,128)S(1)}, f32[8,3,16,256]{3,2,1,0:T(8,128)S(1)}) custom-call(s32[3]{0:T(128)S(1)} %get-tuple-element.31.ids_ref, f32[2]{0:T(128)S(1)} %copy-done.10, f32[8,6,16,256]{3,2,1,0:T(8,128)S(1)} %get-tuple-element.34.rim_ref, f32[2,8,8]{2,1,0:T(8,128)S(1)} %copy-done.5, ...), custom_call_target="tpu_custom_call" | custom-call | flops 1000 | bytes 1000 | tf_op jit(solution)/shard_map/rad_edges/pallas_call | solution.py:235
  11.4 0.7 %collective-permute-start.1 = (f32[8,3,16,256]{3,2,1,0:T(8,128)S(1)}, f32[8,3,16,256]{3,2,1,0:T(8,128)S(1)}, u32[]{:S(2)}, u32[]{:S(2)}) collective-permute-start(f32[8,3,16,256]{3,2,1,0:T(8,128)S(1)} %get-tuple-element.36), channel_id=1, source_target_pairs={{8,16},{16,8},{9,17},{17,9},{10,18},{18,10},{11,19},{19,11},{12,20... | collective-permute-start | bytes 1179656 | tf_op jit(solution)/shard_map/ppermute | solution.py:714
  12.1 4.3 %collective-permute-start = (f32[2,3,16,256]{3,2,1,0:T(8,128)S(1)}, f32[2,3,16,256]{3,2,1,0:T(8,128)S(1)}, u32[]{:S(2)}, u32[]{:S(2)}) collective-permute-start(f32[2,3,16,256]{3,2,1,0:T(8,128)S(1)} %get-tuple-element.35), channel_id=1, source_target_pairs={{0,8},{8,0},{16,24},{24,16},{1,9},{9,1},{17,25},{25,17},{2,10},{10... | collective-permute-start | bytes 294920 | tf_op jit(solution)/shard_map/ppermute | solution.py:685
  16.4 0.0 copy-done.12
  16.4 0.0 copy-done.11
  16.4 0.1 compare_convert_fusion.1.hit_ref
  16.4 0.0 copy-done.15
  16.4 0.0 copy-done.14
  16.4 0.0 copy-done.13
  16.5 0.0 copy-done.7
  16.5 0.0 copy-done.8
  16.5 0.0 copy-done.1
  16.5 9.6 %local_update.1 = (f32[8,64,16,256]{3,2,1,0:T(8,128)S(1)}, f32[70,128,256]{2,1,0:T(8,128)S(1)}, f32[8,70,16,256]{3,2,1,0:T(8,128)S(1)}, f32[16,128]{1,0:T(8,128)S(1)}, f32[3,200,128]{2,1,0:T(8,128)S(1)}) custom-call(f32[2]{0:T(128)S(1)} %copy-done.10, f32[8,64,16,256]{3,2,1,0:T(8,128)} %state_hbm.3, f32[2,8,8]{2,1,0:T(8,128)S(1)} %copy-done.5, ...), custom_call_target="tpu_custom_call" | custom-call | flops 1000 | bytes 1000 | tf_op jit(solution)/shard_map/local_update/pallas_call | solution.py:338
  26.1 0.0 collective-permute-done.near_ref.near_a.refs_0_
  26.2 0.0 collective-permute-done.1.far_ref.refs_2_
  26.2 0.0 collective-permute-done.3.cross_ref.refs_4_
  26.2 0.0 collective-permute-done.2.same_ref.refs_3_
  26.2 0.0 copy-done
  26.2 2.4 %tile_sums.1 = f32[32,384]{1,0:T(8,128)S(1)} custom-call(s32[3]{0:T(128)S(1)} %get-tuple-element.31.ids_ref, f32[8,64,16,256]{3,2,1,0:T(8,128)S(1)} %get-tuple-element.43.part_ref._, f32[64,16,256]{2,1,0:T(8,128)S(1)} %copy-done, f32[64,24,256]{2,1,0:T(8,128)S(1)} %collective-permute-done.2.same_ref.refs_3_, ...), custom_call_target="tpu_custom_call" | custom-call | flops 1000 | bytes 1000 | tf_op jit(solution)/shard_map/tile_sums/pallas_call | solution.py:462
  28.6 0.1 collective-permute-start.6
  28.7 1.9 %collective-permute-start.7 = (f32[32,384]{1,0:T(8,128)S(1)}, f32[32,384]{1,0:T(8,128)S(1)}, u32[]{:S(2)}, u32[]{:S(2)}) collective-permute-start(f32[32,384]{1,0:T(8,128)S(1)} %tile_sums.1), channel_id=1, source_target_pairs={{0,16},{8,24},{16,0},{24,8},{1,17},{9,25},{17,1},{25,9},{2,18},{10... | collective-permute-start | bytes 147464 | tf_op jit(solution)/shard_map/ppermute | solution.py:685
  30.6 1.5 %collective-permute-start.8 = (f32[32,384]{1,0:T(8,128)S(1)}, f32[32,384]{1,0:T(8,128)S(1)}, u32[]{:S(2)}, u32[]{:S(2)}) collective-permute-start(f32[32,384]{1,0:T(8,128)S(1)} %tile_sums.1), channel_id=1, source_target_pairs={{0,24},{8,16},{16,8},{24,0},{1,25},{9,17},{17,9},{25,1},{2,26},{10... | collective-permute-start | bytes 147464 | tf_op jit(solution)/shard_map/ppermute | solution.py:685
  32.1 4.7 %radial_update.1 = (f32[8,64,16,256]{3,2,1,0:T(8,128)S(1)}, f32[8,64,16,256]{3,2,1,0:T(8,128)}) custom-call(f32[2]{0:T(128)S(1)} %copy-done.10, s32[3]{0:T(128)S(1)} %get-tuple-element.31.ids_ref, f32[8,70,16,256]{3,2,1,0:T(8,128)S(1)} %get-tuple-element.32.cells, f32[70,128,256]{2,1,0:T(8,128)S(1)} %get-tuple-element.33.turned, ...), custom_call_target="tpu_custom_call", output_to_operand_aliasing={{0}: (8, {})} | custom-call | flops 100000000 | bytes 6000000 | tf_op jit(solution)/shard_map/radial_update/pallas_call | solution.py:374
  36.8 0.1 collective-permute-start.4
  36.9 0.0 collective-permute-done.6
  37.0 0.0 collective-permute-done.7
  37.0 0.0 collective-permute-done.8
  37.0 0.1 collective-permute-start.9
  37.1 1.2 %collective-permute-done.9.other_ref = f32[32,384]{1,0:T(8,128)S(1)} collective-permute-done((f32[32,384]{1,0:T(8,128)S(1)}, f32[32,384]{1,0:T(8,128)S(1)}, u32[]{:S(2)}, u32[]{:S(2)}) %collective-permute-start.9) | collective-permute-done | bytes 49184 | tf_op jit(solution)/shard_map/ppermute | solution.py:685
  38.3 0.6 %messages.1 = (f32[40,128]{1,0:T(8,128)S(1)}, f32[40,128]{1,0:T(8,128)S(1)}, f32[40,128]{1,0:T(8,128)S(1)}, f32[40,128]{1,0:T(8,128)S(1)}) custom-call(s32[3]{0:T(128)S(1)} %get-tuple-element.31.ids_ref, f32[32,384]{1,0:T(8,128)S(1)} %add_add_fusion.sums_ref, f32[32,384]{1,0:T(8,128)S(1)} %collective-permute-done.9.other_ref, ...), custom_call_target="tpu_custom_call" | custom-call | flops 1000 | bytes 1000 | tf_op jit(solution)/shard_map/messages/pallas_call | solution.py:625
  38.9 1.3 %collective-permute-start.10 = (f32[40,128]{1,0:T(8,128)S(1)}, f32[40,128]{1,0:T(8,128)S(1)}, u32[]{:S(2)}, u32[]{:S(2)}) collective-permute-start(f32[40,128]{1,0:T(8,128)S(1)} %get-tuple-element.56), channel_id=1, source_target_pairs={{0,2},{1,3},{2,0},{3,1},{4,6},{5,7},{6,4},{7,5},{8,10},{9,11},{10,... | collective-permute-start | bytes 61448 | tf_op jit(solution)/shard_map/ppermute | solution.py:685
  40.2 2.0 %collective-permute-start.11 = (f32[40,128]{1,0:T(8,128)S(1)}, f32[40,128]{1,0:T(8,128)S(1)}, u32[]{:S(2)}, u32[]{:S(2)}) collective-permute-start(f32[40,128]{1,0:T(8,128)S(1)} %get-tuple-element.57), channel_id=1, source_target_pairs={{0,4},{1,5},{2,6},{3,7},{4,0},{5,1},{6,2},{7,3},{8,12},{9,13},{10,... | collective-permute-start | bytes 61448 | tf_op jit(solution)/shard_map/ppermute | solution.py:685
  42.3 1.1 %collective-permute-start.12 = (f32[40,128]{1,0:T(8,128)S(1)}, f32[40,128]{1,0:T(8,128)S(1)}, u32[]{:S(2)}, u32[]{:S(2)}) collective-permute-start(f32[40,128]{1,0:T(8,128)S(1)} %get-tuple-element.58), channel_id=1, source_target_pairs={{0,6},{1,7},{2,4},{3,5},{4,2},{5,3},{6,0},{7,1},{8,14},{9,15},{10,... | collective-permute-start | bytes 61448 | tf_op jit(solution)/shard_map/ppermute | solution.py:685
  43.4 0.1 compare_convert_fusion.hit_ref
  43.4 0.6 %collective-permute-done.5.refs_5_ = f32[64,16,256]{2,1,0:T(8,128)S(1)} collective-permute-done((f32[64,16,256]{2,1,0:T(8,128)S(1)}, f32[64,16,256]{2,1,0:T(8,128)S(1)}, u32[]{:S(2)}, u32[]{:S(2)}) %collective-permute-start.5) | collective-permute-done | bytes 1048608 | tf_op jit(solution)/shard_map/ppermute | solution.py:710
  44.1 0.0 collective-permute-done.4.refs_1_
  44.1 3.6 %finish_most.1 = (f32[8,64,16,256]{3,2,1,0:T(8,128)}, f32[64,16,256]{2,1,0:T(8,128)S(1)}) custom-call(s32[3]{0:T(128)S(1)} %get-tuple-element.31.ids_ref, f32[8,64,16,256]{3,2,1,0:T(8,128)S(1)} %get-tuple-element.46.part_ref, f32[2,3,16,256]{3,2,1,0:T(8,128)S(1)} %collective-permute-done.near_ref.near_a.refs_0_, ...), custom_call_target="tpu_custom_call", output_to_operand_aliasing={{0}: (8, {})} | custom-call | flops 100000000 | bytes 16000000 | tf_op jit(solution)/shard_map/finish_most/pallas_call | solution.py:651
  47.7 0.0 collective-permute-done.10
  47.7 0.0 collective-permute-done.11
  47.7 0.2 collective-permute-done.12
  47.9 1.5 %finish_last.1 = (f32[8,64,16,256]{3,2,1,0:T(8,128)}, f32[1,200,128]{2,1,0:T(8,128)}) custom-call(f32[64,16,256]{2,1,0:T(8,128)S(1)} %get-tuple-element.50.cells_ref, f32[8,64,16,256]{3,2,1,0:T(8,128)} %get-tuple-element.54._, bf16[64,32]{1,0:T(8,128)(2,1)S(1)} %compare_convert_fusion.hit_ref, ...), custom_call_target="tpu_custom_call", output_to_operand_aliasing={{0}: (1, {})} | custom-call | flops 1000 | bytes 1000 | tf_op jit(solution)/shard_map/finish_last/pallas_call | solution.py:666
  (7 shorter events, 0.0 us)
Async XLA Ops:
  0.6 9.2 %copy-start.2 = (f32[128,8]{1,0:T(8,128)S(1)}, f32[128,8]{1,0:T(8,128)}, u32[]{:S(2)}) copy-start(f32[128,8]{1,0:T(8,128)} %constant.30.clone.pick_ref) | copy-start | bytes 12292
  0.6 9.2 %copy-start.3 = (f32[128,128]{1,0:T(8,128)S(1)}, f32[128,128]{1,0:T(8,128)}, u32[]{:S(2)}) copy-start(f32[128,128]{1,0:T(8,128)} %constant.31.clone.same_ref) | copy-start | bytes 196612
  0.7 15.8 %copy-start.7 = (f32[128,128]{1,0:T(8,128)S(1)}, f32[128,128]{1,0:T(8,128)}, u32[]{:S(2)}) copy-start(f32[128,128]{1,0:T(8,128)} %constant.32.clone.sum_ref) | copy-start | bytes 196612
  0.7 15.8 %copy-start.8 = (f32[128,128]{1,0:T(8,128)S(1)}, f32[128,128]{1,0:T(8,128)}, u32[]{:S(2)}) copy-start(f32[128,128]{1,0:T(8,128)} %constant.33.clone.gap_ref) | copy-start | bytes 196612
  0.7 9.2 %copy-start.5 = (f32[2,8,8]{2,1,0:T(8,128)S(1)}, f32[2,8,8]{2,1,0:T(8,128)}, u32[]{:S(2)}) copy-start(f32[2,8,8]{2,1,0:T(8,128)} %matrix_ref.3) | copy-start | bytes 1540
  0.7 9.2 %copy-start.10 = (f32[2]{0:T(128)S(1)}, f32[2]{0:T(128)}, u32[]{:S(2)}) copy-start(f32[2]{0:T(128)} %speed_ref.5) | copy-start | bytes 28
  0.7 15.6 %copy-start.12 = (s32[1,64,1]{1,2,0:T(1,128)S(1)}, s32[1,64,1]{1,2,0:T(1,128)}, u32[]{:S(2)}) copy-start(s32[1,64,1]{1,2,0:T(1,128)} %param.24) | copy-start | bytes 772
  0.7 15.6 %copy-start.11 = (s32[32]{0:T(128)S(1)}, s32[32]{0:T(128)}, u32[]{:S(2)}) copy-start(s32[32]{0:T(128)} %param.25) | copy-start | bytes 388
  0.7 15.7 %copy-start.15 = (f32[200]{0:T(256)S(1)}, f32[200]{0:T(256)}, u32[]{:S(2)}) copy-start(f32[200]{0:T(256)} %param.28) | copy-start | bytes 2404
  0.7 15.7 %copy-start.14 = (f32[200]{0:T(256)S(1)}, f32[200]{0:T(256)}, u32[]{:S(2)}) copy-start(f32[200]{0:T(256)} %param.29) | copy-start | bytes 2404
  0.7 15.7 %copy-start.13 = (f32[2,200]{1,0:T(2,128)S(1)}, f32[2,200]{1,0:T(2,128)}, u32[]{:S(2)}) copy-start(f32[2,200]{1,0:T(2,128)} %param.27) | copy-start | bytes 4804
  0.8 15.7 %copy-start.1 = (f32[1,200,128]{2,1,0:T(8,128)S(1)}, f32[1,200,128]{2,1,0:T(8,128)}, u32[]{:S(2)}) copy-start(f32[1,200,128]{2,1,0:T(8,128)} %density_ref.3) | copy-start | bytes 307204
  0.8 25.4 %copy-start = (f32[64,16,256]{2,1,0:T(8,128)S(1)}, f32[64,16,256]{2,1,0:T(8,128)}, u32[]{:S(2)}) copy-start(f32[64,16,256]{2,1,0:T(8,128)} %vol_ref.1) | copy-start | bytes 3145732
  0.8 25.4 %copy-start.6 = (bf16[256,128]{1,0:T(8,128)(2,1)S(1)}, bf16[256,128]{1,0:T(8,128)(2,1)}, u32[]{:S(2)}) copy-start(bf16[256,128]{1,0:T(8,128)(2,1)} %constant.34.clone.seg_ref) | copy-start | bytes 196612
  0.8 25.4 %copy-start.9 = (f32[16,128]{1,0:T(8,128)S(1)}, f32[16,128]{1,0:T(8,128)}, u32[]{:S(2)}) copy-start(f32[16,128]{1,0:T(8,128)} %constant.35.clone.spot_ref) | copy-start | bytes 24580
  4.6 21.6 %collective-permute-start.2 = (f32[64,24,256]{2,1,0:T(8,128)S(1)}, f32[64,24,256]{2,1,0:T(8,128)S(1)}, u32[]{:S(2)}, u32[]{:S(2)}) collective-permute-start(f32[64,24,256]{2,1,0:T(8,128)S(1)} %get-tuple-element.37), channel_id=1, source_target_pairs={{0,1},{1,0},{2,3},{3,2},{4,5},{5,4},{6,7},{7,6},{8,9},{9,8},{10,11... | collective-permute-start | bytes 4718600 | tf_op jit(solution)/shard_map/ppermute | solution.py:685
  5.1 21.1 %collective-permute-start.3 = (f32[64,8,256]{2,1,0:T(8,128)S(1)}, f32[64,8,256]{2,1,0:T(8,128)S(1)}, u32[]{:S(2)}, u32[]{:S(2)}) collective-permute-start(f32[64,8,256]{2,1,0:T(8,128)S(1)} %get-tuple-element.38), channel_id=1, source_target_pairs={{0,7},{1,2},{2,1},{3,4},{4,3},{5,6},{6,5},{7,0},{8,15},{9,10},{10,... | collective-permute-start | bytes 1572872 | tf_op jit(solution)/shard_map/ppermute | solution.py:708
  9.8 34.3 %collective-permute-start.5 = (f32[64,16,256]{2,1,0:T(8,128)S(1)}, f32[64,16,256]{2,1,0:T(8,128)S(1)}, u32[]{:S(2)}, u32[]{:S(2)}) collective-permute-start(f32[64,16,256]{2,1,0:T(8,128)S(1)} %get-tuple-element.48), channel_id=1, source_target_pairs={{0,7},{1,2},{2,1},{3,4},{4,3},{5,6},{6,5},{7,0},{8,15},{9,10},{10,... | collective-permute-start | bytes 3145736 | tf_op jit(solution)/shard_map/ppermute | solution.py:710
  11.4 14.8 %collective-permute-start.1 = (f32[8,3,16,256]{3,2,1,0:T(8,128)S(1)}, f32[8,3,16,256]{3,2,1,0:T(8,128)S(1)}, u32[]{:S(2)}, u32[]{:S(2)}) collective-permute-start(f32[8,3,16,256]{3,2,1,0:T(8,128)S(1)} %get-tuple-element.36), channel_id=1, source_target_pairs={{8,16},{16,8},{9,17},{17,9},{10,18},{18,10},{11,19},{19,11},{12,20... | collective-permute-start | bytes 1179656 | tf_op jit(solution)/shard_map/ppermute | solution.py:714
  12.1 14.1 %collective-permute-start = (f32[2,3,16,256]{3,2,1,0:T(8,128)S(1)}, f32[2,3,16,256]{3,2,1,0:T(8,128)S(1)}, u32[]{:S(2)}, u32[]{:S(2)}) collective-permute-start(f32[2,3,16,256]{3,2,1,0:T(8,128)S(1)} %get-tuple-element.35), channel_id=1, source_target_pairs={{0,8},{8,0},{16,24},{24,16},{1,9},{9,1},{17,25},{25,17},{2,10},{10... | collective-permute-start | bytes 294920 | tf_op jit(solution)/shard_map/ppermute | solution.py:685
  28.6 8.4 %collective-permute-start.6 = (f32[32,384]{1,0:T(8,128)S(1)}, f32[32,384]{1,0:T(8,128)S(1)}, u32[]{:S(2)}, u32[]{:S(2)}) collective-permute-start(f32[32,384]{1,0:T(8,128)S(1)} %tile_sums.1), channel_id=1, source_target_pairs={{0,8},{8,0},{16,24},{24,16},{1,9},{9,1},{17,25},{25,17},{2,10},{10... | collective-permute-start | bytes 147464 | tf_op jit(solution)/shard_map/ppermute | solution.py:685
  28.7 8.3 %collective-permute-start.7 = (f32[32,384]{1,0:T(8,128)S(1)}, f32[32,384]{1,0:T(8,128)S(1)}, u32[]{:S(2)}, u32[]{:S(2)}) collective-permute-start(f32[32,384]{1,0:T(8,128)S(1)} %tile_sums.1), channel_id=1, source_target_pairs={{0,16},{8,24},{16,0},{24,8},{1,17},{9,25},{17,1},{25,9},{2,18},{10... | collective-permute-start | bytes 147464 | tf_op jit(solution)/shard_map/ppermute | solution.py:685
  30.6 6.3 %collective-permute-start.8 = (f32[32,384]{1,0:T(8,128)S(1)}, f32[32,384]{1,0:T(8,128)S(1)}, u32[]{:S(2)}, u32[]{:S(2)}) collective-permute-start(f32[32,384]{1,0:T(8,128)S(1)} %tile_sums.1), channel_id=1, source_target_pairs={{0,24},{8,16},{16,8},{24,0},{1,25},{9,17},{17,9},{25,1},{2,26},{10... | collective-permute-start | bytes 147464 | tf_op jit(solution)/shard_map/ppermute | solution.py:685
  36.8 7.3 %collective-permute-start.4 = (f32[6,3,16,256]{3,2,1,0:T(8,128)S(1)}, f32[6,3,16,256]{3,2,1,0:T(8,128)S(1)}, u32[]{:S(2)}, u32[]{:S(2)}) collective-permute-start(f32[6,3,16,256]{3,2,1,0:T(8,128)S(1)} %get-tuple-element.47), channel_id=1, source_target_pairs={{0,8},{8,0},{16,24},{24,16},{1,9},{9,1},{17,25},{25,17},{2,10},{10... | collective-permute-start | bytes 884744 | tf_op jit(solution)/shard_map/ppermute | solution.py:685
  37.0 1.3 %collective-permute-start.9 = (f32[32,384]{1,0:T(8,128)S(1)}, f32[32,384]{1,0:T(8,128)S(1)}, u32[]{:S(2)}, u32[]{:S(2)}) collective-permute-start(f32[32,384]{1,0:T(8,128)S(1)} %add_add_fusion.sums_ref), channel_id=1, source_target_pairs={{0,1},{1,0},{2,3},{3,2},{4,5},{5,4},{6,7},{7,6},{8,9},{9,8},{10,11... | collective-permute-start | bytes 147464 | tf_op jit(solution)/shard_map/ppermute | solution.py:685
  38.9 8.8 %collective-permute-start.10 = (f32[40,128]{1,0:T(8,128)S(1)}, f32[40,128]{1,0:T(8,128)S(1)}, u32[]{:S(2)}, u32[]{:S(2)}) collective-permute-start(f32[40,128]{1,0:T(8,128)S(1)} %get-tuple-element.56), channel_id=1, source_target_pairs={{0,2},{1,3},{2,0},{3,1},{4,6},{5,7},{6,4},{7,5},{8,10},{9,11},{10,... | collective-permute-start | bytes 61448 | tf_op jit(solution)/shard_map/ppermute | solution.py:685
  40.2 7.4 %collective-permute-start.11 = (f32[40,128]{1,0:T(8,128)S(1)}, f32[40,128]{1,0:T(8,128)S(1)}, u32[]{:S(2)}, u32[]{:S(2)}) collective-permute-start(f32[40,128]{1,0:T(8,128)S(1)} %get-tuple-element.57), channel_id=1, source_target_pairs={{0,4},{1,5},{2,6},{3,7},{4,0},{5,1},{6,2},{7,3},{8,12},{9,13},{10,... | collective-permute-start | bytes 61448 | tf_op jit(solution)/shard_map/ppermute | solution.py:685
  42.3 5.6 %collective-permute-start.12 = (f32[40,128]{1,0:T(8,128)S(1)}, f32[40,128]{1,0:T(8,128)S(1)}, u32[]{:S(2)}, u32[]{:S(2)}) collective-permute-start(f32[40,128]{1,0:T(8,128)S(1)} %get-tuple-element.58), channel_id=1, source_target_pairs={{0,6},{1,7},{2,4},{3,5},{4,2},{5,3},{6,0},{7,1},{8,14},{9,15},{10,... | collective-permute-start | bytes 61448 | tf_op jit(solution)/shard_map/ppermute | solution.py:685
  44.1 3.8 %copy-start.4 = (bf16[384,256]{1,0:T(8,128)(2,1)S(1)}, bf16[384,256]{1,0:T(8,128)(2,1)}, u32[]{:S(2)}) copy-start(bf16[384,256]{1,0:T(8,128)(2,1)} %constant.36.clone.seg_ref) | copy-start | bytes 589828

commit v6 on v5

--- a/solution.py
+++ b/solution.py
@@ -587,6 +587,12 @@
     for i, part in enumerate(parts_of(nudge_rate * back, 3)):
         back_ref[i] = part.astype(f32)
     copies = []
+    density = density_ref[0] + inner_step * (
+        spread_ref[1] * sums_ref[tiles : tiles + 1] + spread_ref[2] * sums_ref[tiles + 1 : tiles + 2]
+    )
+    moved[0] = drifted(density, spread_ref[0])
+    copies.append(pltpu.make_async_copy(moved, drifted_hbm, sem.at[len(copies)]))
+    copies[-1].start()
     size = 2 * CHUNK
     for first in range(0, rows, size):
         here = pl.ds(first, size)
@@ -595,12 +601,6 @@
         done[here] = cells_ref[here] + returned.reshape(-1, cols, depth)
         copies.append(pltpu.make_async_copy(done.at[here], out_hbm.at[last, here], sem.at[len(copies)]))
         copies[-1].start()
-    density = density_ref[0] + inner_step * (
-        spread_ref[1] * sums_ref[tiles : tiles + 1] + spread_ref[2] * sums_ref[tiles + 1 : tiles + 2]
-    )
-    moved[0] = drifted(density, spread_ref[0])
-    copies.append(pltpu.make_async_copy(moved, drifted_hbm, sem.at[len(copies)]))
-    copies[-1].start()
     for copy in copies:
         copy.wait()
 

time: 49.5 us -> 49.5 us (level)
  no operation moved by 1% of the time
where the time goes in v6:
time: 49.5 us; the launch traced here: 49.3 us
  Pallas kernels  27.7 us (56%)
  starting transfers between devices  18.4 us (37%)
  waiting for transfers between devices  2.03 us (4%)
  between operations  0.97 us (2%)
    ppermute x10, starting transfers between devices, swap(): lax.ppermute(x, axis, [(i, i ^ bit) for i in range(lax.axis_size(axis))])  12.9 us
    pallas_call x1, Pallas kernels, local_update(): pl.pallas_call(local_kernel, in_specs=[SMEM, HBM] + [VMEM] * 7, out_specs...  9.64 us
    ppermute x1, starting transfers between devices, per_device(): cross_0 = lax.ppermute(crosses[0], 'lon', across)  4.71 us
    pallas_call x1, Pallas kernels, radial_update(): pl.pallas_call(functools.partial(radial_kernel, fields), in_specs=[SMEM]...  4.7 us
    pallas_call x1, Pallas kernels, lon_edges(): pl.pallas_call(lon_edge_kernel, in_specs=[SMEM] * 3 + [HBM] * 4, out_spec...  3.77 us
    pallas_call x1, Pallas kernels, finish_most(): pl.pallas_call(most_kernel, in_specs=[SMEM] + [VMEM] * len(pins) + [HBM],...  3.58 us
    pallas_call x1, Pallas kernels, tile_sums(): pl.pallas_call(tile_sum_kernel, in_specs=[SMEM] + [VMEM] * 10, out_specs=...  2.38 us
    pallas_call x1, Pallas kernels, rad_edges(): pl.pallas_call(rad_edge_kernel, in_specs=[SMEM] * 2 + [VMEM] * (2 + len(t...  1.51 us
  transfers between devices with their start and end apart: 13, of which 3 were waited for; matrix products, arithmetic and copies ran while one was open for 0% of the time, Pallas kernels for 46%

profile of v6, /device:TPU:0, one launch (start us, length us, event | category | flops | bytes accessed | tf_op | source)
XLA Modules:
  0.0 49.3 jit_solution(17614222045839333850)
XLA Ops:
  0.6 0.0 copy-start.2
  0.6 0.0 copy-start.3
  0.7 0.0 copy-start.7
  0.7 0.0 copy-start.8
  0.7 0.0 copy-start.5
  0.7 0.0 copy-start.10
  0.7 0.0 copy-start.12
  0.7 0.0 copy-start.11
  0.7 0.0 copy-start.15
  0.7 0.0 copy-start.14
  0.7 0.0 copy-start.13
  0.8 0.0 copy-start.1
  0.8 0.0 copy-start
  0.8 0.0 copy-start.6
  0.8 0.0 copy-start.9
  0.8 3.8 %lon_edges.1 = (f32[8,6,16,256]{3,2,1,0:T(8,128)S(1)}, s32[3]{0:T(128)S(1)}, f32[64,24,256]{2,1,0:T(8,128)S(1)}, f32[64,8,256]{2,1,0:T(8,128)S(1)}, f32[64,16,256]{2,1,0:T(8,128)S(1)}) custom-call(s32[1]{0:T(128)} %bitcast.lon_ref, s32[1]{0:T(128)} %bitcast.1.rad_ref, s32[1]{0:T(128)} %bitcast.2.place_ref, f32[8,64,16,256]{3,2,1,0:T(8,128)} %state_hbm.3, ...), custom_call_target="tpu_custom_call" | custom-call | flops 1000 | bytes 1000 | tf_op jit(solution)/shard_map/lon_edges/pallas_call | solution.py:164
  4.6 0.5 %collective-permute-start.2 = (f32[64,24,256]{2,1,0:T(8,128)S(1)}, f32[64,24,256]{2,1,0:T(8,128)S(1)}, u32[]{:S(2)}, u32[]{:S(2)}) collective-permute-start(f32[64,24,256]{2,1,0:T(8,128)S(1)} %get-tuple-element.37), channel_id=1, source_target_pairs={{0,1},{1,0},{2,3},{3,2},{4,5},{5,4},{6,7},{7,6},{8,9},{9,8},{10,11... | collective-permute-start | bytes 4718600 | tf_op jit(solution)/shard_map/ppermute | solution.py:685
  5.1 4.7 %collective-permute-start.3 = (f32[64,8,256]{2,1,0:T(8,128)S(1)}, f32[64,8,256]{2,1,0:T(8,128)S(1)}, u32[]{:S(2)}, u32[]{:S(2)}) collective-permute-start(f32[64,8,256]{2,1,0:T(8,128)S(1)} %get-tuple-element.38), channel_id=1, source_target_pairs={{0,7},{1,2},{2,1},{3,4},{4,3},{5,6},{6,5},{7,0},{8,15},{9,10},{10,... | collective-permute-start | bytes 1572872 | tf_op jit(solution)/shard_map/ppermute | solution.py:708
  9.8 0.0 collective-permute-start.5
  9.9 0.0 copy-done.2
  9.9 0.0 copy-done.3
  9.9 0.0 copy-done.5
  9.9 0.0 copy-done.10
  9.9 1.5 %rad_edges.1 = (f32[2,3,16,256]{3,2,1,0:T(8,128)S(1)}, f32[6,3,16,256]{3,2,1,0:T(8,128)S(1)}, f32[8,3,16,256]{3,2,1,0:T(8,128)S(1)}) custom-call(s32[3]{0:T(128)S(1)} %get-tuple-element.31.ids_ref, f32[2]{0:T(128)S(1)} %copy-done.10, f32[8,6,16,256]{3,2,1,0:T(8,128)S(1)} %get-tuple-element.34.rim_ref, f32[2,8,8]{2,1,0:T(8,128)S(1)} %copy-done.5, ...), custom_call_target="tpu_custom_call" | custom-call | flops 1000 | bytes 1000 | tf_op jit(solution)/shard_map/rad_edges/pallas_call | solution.py:235
  11.4 0.7 %collective-permute-start.1 = (f32[8,3,16,256]{3,2,1,0:T(8,128)S(1)}, f32[8,3,16,256]{3,2,1,0:T(8,128)S(1)}, u32[]{:S(2)}, u32[]{:S(2)}) collective-permute-start(f32[8,3,16,256]{3,2,1,0:T(8,128)S(1)} %get-tuple-element.36), channel_id=1, source_target_pairs={{8,16},{16,8},{9,17},{17,9},{10,18},{18,10},{11,19},{19,11},{12,20... | collective-permute-start | bytes 1179656 | tf_op jit(solution)/shard_map/ppermute | solution.py:714
  12.1 4.3 %collective-permute-start = (f32[2,3,16,256]{3,2,1,0:T(8,128)S(1)}, f32[2,3,16,256]{3,2,1,0:T(8,128)S(1)}, u32[]{:S(2)}, u32[]{:S(2)}) collective-permute-start(f32[2,3,16,256]{3,2,1,0:T(8,128)S(1)} %get-tuple-element.35), channel_id=1, source_target_pairs={{0,8},{8,0},{16,24},{24,16},{1,9},{9,1},{17,25},{25,17},{2,10},{10... | collective-permute-start | bytes 294920 | tf_op jit(solution)/shard_map/ppermute | solution.py:685
  16.4 0.0 copy-done.12
  16.4 0.0 copy-done.11
  16.4 0.1 compare_convert_fusion.1.hit_ref
  16.4 0.0 copy-done.14
  16.5 0.0 copy-done.7
  16.5 0.0 copy-done.8
  16.5 0.0 copy-done.1
  16.5 9.6 %local_update.1 = (f32[8,64,16,256]{3,2,1,0:T(8,128)S(1)}, f32[70,128,256]{2,1,0:T(8,128)S(1)}, f32[8,70,16,256]{3,2,1,0:T(8,128)S(1)}, f32[16,128]{1,0:T(8,128)S(1)}, f32[3,200,128]{2,1,0:T(8,128)S(1)}) custom-call(f32[2]{0:T(128)S(1)} %copy-done.10, f32[8,64,16,256]{3,2,1,0:T(8,128)} %state_hbm.3, f32[2,8,8]{2,1,0:T(8,128)S(1)} %copy-done.5, ...), custom_call_target="tpu_custom_call" | custom-call | flops 1000 | bytes 1000 | tf_op jit(solution)/shard_map/local_update/pallas_call | solution.py:338
  26.1 0.0 collective-permute-done.near_ref.near_a.refs_0_
  26.2 0.0 collective-permute-done.1.far_ref.refs_2_
  26.2 0.0 collective-permute-done.3.cross_ref.refs_4_
  26.2 0.0 collective-permute-done.2.same_ref.refs_3_
  26.2 0.0 copy-done
  26.2 0.0 copy-done.6
  26.2 0.0 copy-done.9
  26.2 2.4 %tile_sums.1 = f32[32,384]{1,0:T(8,128)S(1)} custom-call(s32[3]{0:T(128)S(1)} %get-tuple-element.31.ids_ref, f32[8,64,16,256]{3,2,1,0:T(8,128)S(1)} %get-tuple-element.43.part_ref._, f32[64,16,256]{2,1,0:T(8,128)S(1)} %copy-done, f32[64,24,256]{2,1,0:T(8,128)S(1)} %collective-permute-done.2.same_ref.refs_3_, ...), custom_call_target="tpu_custom_call" | custom-call | flops 1000 | bytes 1000 | tf_op jit(solution)/shard_map/tile_sums/pallas_call | solution.py:462
  28.6 0.1 collective-permute-start.6
  28.7 1.9 %collective-permute-start.7 = (f32[32,384]{1,0:T(8,128)S(1)}, f32[32,384]{1,0:T(8,128)S(1)}, u32[]{:S(2)}, u32[]{:S(2)}) collective-permute-start(f32[32,384]{1,0:T(8,128)S(1)} %tile_sums.1), channel_id=1, source_target_pairs={{0,16},{8,24},{16,0},{24,8},{1,17},{9,25},{17,1},{25,9},{2,18},{10... | collective-permute-start | bytes 147464 | tf_op jit(solution)/shard_map/ppermute | solution.py:685
  30.6 1.5 %collective-permute-start.8 = (f32[32,384]{1,0:T(8,128)S(1)}, f32[32,384]{1,0:T(8,128)S(1)}, u32[]{:S(2)}, u32[]{:S(2)}) collective-permute-start(f32[32,384]{1,0:T(8,128)S(1)} %tile_sums.1), channel_id=1, source_target_pairs={{0,24},{8,16},{16,8},{24,0},{1,25},{9,17},{17,9},{25,1},{2,26},{10... | collective-permute-start | bytes 147464 | tf_op jit(solution)/shard_map/ppermute | solution.py:685
  32.1 4.7 %radial_update.1 = (f32[8,64,16,256]{3,2,1,0:T(8,128)S(1)}, f32[8,64,16,256]{3,2,1,0:T(8,128)}) custom-call(f32[2]{0:T(128)S(1)} %copy-done.10, s32[3]{0:T(128)S(1)} %get-tuple-element.31.ids_ref, f32[8,70,16,256]{3,2,1,0:T(8,128)S(1)} %get-tuple-element.32.cells, f32[70,128,256]{2,1,0:T(8,128)S(1)} %get-tuple-element.33.turned, ...), custom_call_target="tpu_custom_call", output_to_operand_aliasing={{0}: (8, {})} | custom-call | flops 100000000 | bytes 6000000 | tf_op jit(solution)/shard_map/radial_update/pallas_call | solution.py:374
  36.8 0.1 collective-permute-start.4
  36.9 0.0 collective-permute-done.6
  37.0 0.0 collective-permute-done.7
  37.0 0.0 collective-permute-done.8
  37.0 0.1 collective-permute-start.9
  37.1 1.2 %collective-permute-done.9.other_ref = f32[32,384]{1,0:T(8,128)S(1)} collective-permute-done((f32[32,384]{1,0:T(8,128)S(1)}, f32[32,384]{1,0:T(8,128)S(1)}, u32[]{:S(2)}, u32[]{:S(2)}) %collective-permute-start.9) | collective-permute-done | bytes 49184 | tf_op jit(solution)/shard_map/ppermute | solution.py:685
  38.3 0.6 %messages.1 = (f32[40,128]{1,0:T(8,128)S(1)}, f32[40,128]{1,0:T(8,128)S(1)}, f32[40,128]{1,0:T(8,128)S(1)}, f32[40,128]{1,0:T(8,128)S(1)}) custom-call(s32[3]{0:T(128)S(1)} %get-tuple-element.31.ids_ref, f32[32,384]{1,0:T(8,128)S(1)} %add_add_fusion.sums_ref, f32[32,384]{1,0:T(8,128)S(1)} %collective-permute-done.9.other_ref, ...), custom_call_target="tpu_custom_call" | custom-call | flops 1000 | bytes 1000 | tf_op jit(solution)/shard_map/messages/pallas_call | solution.py:625
  38.9 1.3 %collective-permute-start.10 = (f32[40,128]{1,0:T(8,128)S(1)}, f32[40,128]{1,0:T(8,128)S(1)}, u32[]{:S(2)}, u32[]{:S(2)}) collective-permute-start(f32[40,128]{1,0:T(8,128)S(1)} %get-tuple-element.56), channel_id=1, source_target_pairs={{0,2},{1,3},{2,0},{3,1},{4,6},{5,7},{6,4},{7,5},{8,10},{9,11},{10,... | collective-permute-start | bytes 61448 | tf_op jit(solution)/shard_map/ppermute | solution.py:685
  40.2 2.0 %collective-permute-start.11 = (f32[40,128]{1,0:T(8,128)S(1)}, f32[40,128]{1,0:T(8,128)S(1)}, u32[]{:S(2)}, u32[]{:S(2)}) collective-permute-start(f32[40,128]{1,0:T(8,128)S(1)} %get-tuple-element.57), channel_id=1, source_target_pairs={{0,4},{1,5},{2,6},{3,7},{4,0},{5,1},{6,2},{7,3},{8,12},{9,13},{10,... | collective-permute-start | bytes 61448 | tf_op jit(solution)/shard_map/ppermute | solution.py:685
  42.3 1.1 %collective-permute-start.12 = (f32[40,128]{1,0:T(8,128)S(1)}, f32[40,128]{1,0:T(8,128)S(1)}, u32[]{:S(2)}, u32[]{:S(2)}) collective-permute-start(f32[40,128]{1,0:T(8,128)S(1)} %get-tuple-element.58), channel_id=1, source_target_pairs={{0,6},{1,7},{2,4},{3,5},{4,2},{5,3},{6,0},{7,1},{8,14},{9,15},{10,... | collective-permute-start | bytes 61448 | tf_op jit(solution)/shard_map/ppermute | solution.py:685
  43.4 0.1 compare_convert_fusion.hit_ref
  43.4 0.6 %collective-permute-done.5.refs_5_ = f32[64,16,256]{2,1,0:T(8,128)S(1)} collective-permute-done((f32[64,16,256]{2,1,0:T(8,128)S(1)}, f32[64,16,256]{2,1,0:T(8,128)S(1)}, u32[]{:S(2)}, u32[]{:S(2)}) %collective-permute-start.5) | collective-permute-done | bytes 1048608 | tf_op jit(solution)/shard_map/ppermute | solution.py:710
  44.1 0.0 collective-permute-done.4.refs_1_
  44.1 3.6 %finish_most.1 = (f32[8,64,16,256]{3,2,1,0:T(8,128)}, f32[64,16,256]{2,1,0:T(8,128)S(1)}) custom-call(s32[3]{0:T(128)S(1)} %get-tuple-element.31.ids_ref, f32[8,64,16,256]{3,2,1,0:T(8,128)S(1)} %get-tuple-element.46.part_ref, f32[2,3,16,256]{3,2,1,0:T(8,128)S(1)} %collective-permute-done.near_ref.near_a.refs_0_, ...), custom_call_target="tpu_custom_call", output_to_operand_aliasing={{0}: (8, {})} | custom-call | flops 100000000 | bytes 16000000 | tf_op jit(solution)/shard_map/finish_most/pallas_call | solution.py:651
  47.7 0.0 collective-permute-done.10
  47.7 0.0 collective-permute-done.11
  47.7 0.2 collective-permute-done.12
  47.9 1.4 %finish_last.1 = (f32[8,64,16,256]{3,2,1,0:T(8,128)}, f32[1,200,128]{2,1,0:T(8,128)}) custom-call(f32[64,16,256]{2,1,0:T(8,128)S(1)} %get-tuple-element.50.cells_ref, f32[8,64,16,256]{3,2,1,0:T(8,128)} %get-tuple-element.54._, bf16[64,32]{1,0:T(8,128)(2,1)S(1)} %compare_convert_fusion.hit_ref, ...), custom_call_target="tpu_custom_call", output_to_operand_aliasing={{0}: (1, {})} | custom-call | flops 1000 | bytes 1000 | tf_op jit(solution)/shard_map/finish_last/pallas_call | solution.py:666
  (7 shorter events, 0.0 us)
Async XLA Ops:
  0.6 9.2 %copy-start.2 = (f32[128,8]{1,0:T(8,128)S(1)}, f32[128,8]{1,0:T(8,128)}, u32[]{:S(2)}) copy-start(f32[128,8]{1,0:T(8,128)} %constant.30.clone.pick_ref) | copy-start | bytes 12292
  0.6 9.2 %copy-start.3 = (f32[128,128]{1,0:T(8,128)S(1)}, f32[128,128]{1,0:T(8,128)}, u32[]{:S(2)}) copy-start(f32[128,128]{1,0:T(8,128)} %constant.31.clone.same_ref) | copy-start | bytes 196612
  0.7 15.8 %copy-start.7 = (f32[128,128]{1,0:T(8,128)S(1)}, f32[128,128]{1,0:T(8,128)}, u32[]{:S(2)}) copy-start(f32[128,128]{1,0:T(8,128)} %constant.32.clone.sum_ref) | copy-start | bytes 196612
  0.7 15.8 %copy-start.8 = (f32[128,128]{1,0:T(8,128)S(1)}, f32[128,128]{1,0:T(8,128)}, u32[]{:S(2)}) copy-start(f32[128,128]{1,0:T(8,128)} %constant.33.clone.gap_ref) | copy-start | bytes 196612
  0.7 9.2 %copy-start.5 = (f32[2,8,8]{2,1,0:T(8,128)S(1)}, f32[2,8,8]{2,1,0:T(8,128)}, u32[]{:S(2)}) copy-start(f32[2,8,8]{2,1,0:T(8,128)} %matrix_ref.3) | copy-start | bytes 1540
  0.7 9.2 %copy-start.10 = (f32[2]{0:T(128)S(1)}, f32[2]{0:T(128)}, u32[]{:S(2)}) copy-start(f32[2]{0:T(128)} %speed_ref.5) | copy-start | bytes 28
  0.7 15.6 %copy-start.12 = (s32[1,64,1]{1,2,0:T(1,128)S(1)}, s32[1,64,1]{1,2,0:T(1,128)}, u32[]{:S(2)}) copy-start(s32[1,64,1]{1,2,0:T(1,128)} %param.24) | copy-start | bytes 772
  0.7 15.6 %copy-start.11 = (s32[32]{0:T(128)S(1)}, s32[32]{0:T(128)}, u32[]{:S(2)}) copy-start(s32[32]{0:T(128)} %param.25) | copy-start | bytes 388
  0.7 15.7 %copy-start.15 = (f32[200]{0:T(256)S(1)}, f32[200]{0:T(256)}, u32[]{:S(2)}) copy-start(f32[200]{0:T(256)} %param.28) | copy-start | bytes 2404
  0.7 15.7 %copy-start.14 = (f32[200]{0:T(256)S(1)}, f32[200]{0:T(256)}, u32[]{:S(2)}) copy-start(f32[200]{0:T(256)} %param.29) | copy-start | bytes 2404
  0.7 15.7 %copy-start.13 = (f32[2,200]{1,0:T(2,128)S(1)}, f32[2,200]{1,0:T(2,128)}, u32[]{:S(2)}) copy-start(f32[2,200]{1,0:T(2,128)} %param.27) | copy-start | bytes 4804
  0.8 15.7 %copy-start.1 = (f32[1,200,128]{2,1,0:T(8,128)S(1)}, f32[1,200,128]{2,1,0:T(8,128)}, u32[]{:S(2)}) copy-start(f32[1,200,128]{2,1,0:T(8,128)} %density_ref.3) | copy-start | bytes 307204
  0.8 25.4 %copy-start = (f32[64,16,256]{2,1,0:T(8,128)S(1)}, f32[64,16,256]{2,1,0:T(8,128)}, u32[]{:S(2)}) copy-start(f32[64,16,256]{2,1,0:T(8,128)} %vol_ref.1) | copy-start | bytes 3145732
  0.8 25.4 %copy-start.6 = (bf16[256,128]{1,0:T(8,128)(2,1)S(1)}, bf16[256,128]{1,0:T(8,128)(2,1)}, u32[]{:S(2)}) copy-start(bf16[256,128]{1,0:T(8,128)(2,1)} %constant.34.clone.seg_ref) | copy-start | bytes 196612
  0.8 25.4 %copy-start.9 = (f32[16,128]{1,0:T(8,128)S(1)}, f32[16,128]{1,0:T(8,128)}, u32[]{:S(2)}) copy-start(f32[16,128]{1,0:T(8,128)} %constant.35.clone.spot_ref) | copy-start | bytes 24580
  4.6 21.6 %collective-permute-start.2 = (f32[64,24,256]{2,1,0:T(8,128)S(1)}, f32[64,24,256]{2,1,0:T(8,128)S(1)}, u32[]{:S(2)}, u32[]{:S(2)}) collective-permute-start(f32[64,24,256]{2,1,0:T(8,128)S(1)} %get-tuple-element.37), channel_id=1, source_target_pairs={{0,1},{1,0},{2,3},{3,2},{4,5},{5,4},{6,7},{7,6},{8,9},{9,8},{10,11... | collective-permute-start | bytes 4718600 | tf_op jit(solution)/shard_map/ppermute | solution.py:685
  5.1 21.1 %collective-permute-start.3 = (f32[64,8,256]{2,1,0:T(8,128)S(1)}, f32[64,8,256]{2,1,0:T(8,128)S(1)}, u32[]{:S(2)}, u32[]{:S(2)}) collective-permute-start(f32[64,8,256]{2,1,0:T(8,128)S(1)} %get-tuple-element.38), channel_id=1, source_target_pairs={{0,7},{1,2},{2,1},{3,4},{4,3},{5,6},{6,5},{7,0},{8,15},{9,10},{10,... | collective-permute-start | bytes 1572872 | tf_op jit(solution)/shard_map/ppermute | solution.py:708
  9.8 34.3 %collective-permute-start.5 = (f32[64,16,256]{2,1,0:T(8,128)S(1)}, f32[64,16,256]{2,1,0:T(8,128)S(1)}, u32[]{:S(2)}, u32[]{:S(2)}) collective-permute-start(f32[64,16,256]{2,1,0:T(8,128)S(1)} %get-tuple-element.48), channel_id=1, source_target_pairs={{0,7},{1,2},{2,1},{3,4},{4,3},{5,6},{6,5},{7,0},{8,15},{9,10},{10,... | collective-permute-start | bytes 3145736 | tf_op jit(solution)/shard_map/ppermute | solution.py:710
  11.4 14.8 %collective-permute-start.1 = (f32[8,3,16,256]{3,2,1,0:T(8,128)S(1)}, f32[8,3,16,256]{3,2,1,0:T(8,128)S(1)}, u32[]{:S(2)}, u32[]{:S(2)}) collective-permute-start(f32[8,3,16,256]{3,2,1,0:T(8,128)S(1)} %get-tuple-element.36), channel_id=1, source_target_pairs={{8,16},{16,8},{9,17},{17,9},{10,18},{18,10},{11,19},{19,11},{12,20... | collective-permute-start | bytes 1179656 | tf_op jit(solution)/shard_map/ppermute | solution.py:714
  12.1 14.1 %collective-permute-start = (f32[2,3,16,256]{3,2,1,0:T(8,128)S(1)}, f32[2,3,16,256]{3,2,1,0:T(8,128)S(1)}, u32[]{:S(2)}, u32[]{:S(2)}) collective-permute-start(f32[2,3,16,256]{3,2,1,0:T(8,128)S(1)} %get-tuple-element.35), channel_id=1, source_target_pairs={{0,8},{8,0},{16,24},{24,16},{1,9},{9,1},{17,25},{25,17},{2,10},{10... | collective-permute-start | bytes 294920 | tf_op jit(solution)/shard_map/ppermute | solution.py:685
  28.6 8.4 %collective-permute-start.6 = (f32[32,384]{1,0:T(8,128)S(1)}, f32[32,384]{1,0:T(8,128)S(1)}, u32[]{:S(2)}, u32[]{:S(2)}) collective-permute-start(f32[32,384]{1,0:T(8,128)S(1)} %tile_sums.1), channel_id=1, source_target_pairs={{0,8},{8,0},{16,24},{24,16},{1,9},{9,1},{17,25},{25,17},{2,10},{10... | collective-permute-start | bytes 147464 | tf_op jit(solution)/shard_map/ppermute | solution.py:685
  28.7 8.3 %collective-permute-start.7 = (f32[32,384]{1,0:T(8,128)S(1)}, f32[32,384]{1,0:T(8,128)S(1)}, u32[]{:S(2)}, u32[]{:S(2)}) collective-permute-start(f32[32,384]{1,0:T(8,128)S(1)} %tile_sums.1), channel_id=1, source_target_pairs={{0,16},{8,24},{16,0},{24,8},{1,17},{9,25},{17,1},{25,9},{2,18},{10... | collective-permute-start | bytes 147464 | tf_op jit(solution)/shard_map/ppermute | solution.py:685
  30.6 6.3 %collective-permute-start.8 = (f32[32,384]{1,0:T(8,128)S(1)}, f32[32,384]{1,0:T(8,128)S(1)}, u32[]{:S(2)}, u32[]{:S(2)}) collective-permute-start(f32[32,384]{1,0:T(8,128)S(1)} %tile_sums.1), channel_id=1, source_target_pairs={{0,24},{8,16},{16,8},{24,0},{1,25},{9,17},{17,9},{25,1},{2,26},{10... | collective-permute-start | bytes 147464 | tf_op jit(solution)/shard_map/ppermute | solution.py:685
  36.8 7.3 %collective-permute-start.4 = (f32[6,3,16,256]{3,2,1,0:T(8,128)S(1)}, f32[6,3,16,256]{3,2,1,0:T(8,128)S(1)}, u32[]{:S(2)}, u32[]{:S(2)}) collective-permute-start(f32[6,3,16,256]{3,2,1,0:T(8,128)S(1)} %get-tuple-element.47), channel_id=1, source_target_pairs={{0,8},{8,0},{16,24},{24,16},{1,9},{9,1},{17,25},{25,17},{2,10},{10... | collective-permute-start | bytes 884744 | tf_op jit(solution)/shard_map/ppermute | solution.py:685
  37.0 1.3 %collective-permute-start.9 = (f32[32,384]{1,0:T(8,128)S(1)}, f32[32,384]{1,0:T(8,128)S(1)}, u32[]{:S(2)}, u32[]{:S(2)}) collective-permute-start(f32[32,384]{1,0:T(8,128)S(1)} %add_add_fusion.sums_ref), channel_id=1, source_target_pairs={{0,1},{1,0},{2,3},{3,2},{4,5},{5,4},{6,7},{7,6},{8,9},{9,8},{10,11... | collective-permute-start | bytes 147464 | tf_op jit(solution)/shard_map/ppermute | solution.py:685
  38.9 8.8 %collective-permute-start.10 = (f32[40,128]{1,0:T(8,128)S(1)}, f32[40,128]{1,0:T(8,128)S(1)}, u32[]{:S(2)}, u32[]{:S(2)}) collective-permute-start(f32[40,128]{1,0:T(8,128)S(1)} %get-tuple-element.56), channel_id=1, source_target_pairs={{0,2},{1,3},{2,0},{3,1},{4,6},{5,7},{6,4},{7,5},{8,10},{9,11},{10,... | collective-permute-start | bytes 61448 | tf_op jit(solution)/shard_map/ppermute | solution.py:685
  40.2 7.4 %collective-permute-start.11 = (f32[40,128]{1,0:T(8,128)S(1)}, f32[40,128]{1,0:T(8,128)S(1)}, u32[]{:S(2)}, u32[]{:S(2)}) collective-permute-start(f32[40,128]{1,0:T(8,128)S(1)} %get-tuple-element.57), channel_id=1, source_target_pairs={{0,4},{1,5},{2,6},{3,7},{4,0},{5,1},{6,2},{7,3},{8,12},{9,13},{10,... | collective-permute-start | bytes 61448 | tf_op jit(solution)/shard_map/ppermute | solution.py:685
  42.3 5.6 %collective-permute-start.12 = (f32[40,128]{1,0:T(8,128)S(1)}, f32[40,128]{1,0:T(8,128)S(1)}, u32[]{:S(2)}, u32[]{:S(2)}) collective-permute-start(f32[40,128]{1,0:T(8,128)S(1)} %get-tuple-element.58), channel_id=1, source_target_pairs={{0,6},{1,7},{2,4},{3,5},{4,2},{5,3},{6,0},{7,1},{8,14},{9,15},{10,... | collective-permute-start | bytes 61448 | tf_op jit(solution)/shard_map/ppermute | solution.py:685
  44.1 3.8 %copy-start.4 = (bf16[384,256]{1,0:T(8,128)(2,1)S(1)}, bf16[384,256]{1,0:T(8,128)(2,1)}, u32[]{:S(2)}) copy-start(bf16[384,256]{1,0:T(8,128)(2,1)} %constant.36.clone.seg_ref) | copy-start | bytes 589828
